TPU v7x, 32 devices: a whole 2x2x4 slice. The times are simulated.
32 devices in a mesh: seq: 8 (over y, x, core), fsdp: 4 (over z).
Axes of the slice: x: 2, y: 2, z: 4, core: 2. Of those that a mesh axis runs over, the one named last changes fastest.
Arguments:
- first_tier_source: bfloat16 [4, 8192, 768], P('fsdp', 'seq'), may hold values from -6 to 6
- token_articles: int32 [4, 8192], P('fsdp', 'seq'), may hold values from 0 to 3, as said below
- extra_spikes: float32 [4, 8192, 24], P('fsdp', 'seq'), may hold values from -0.7 to 0, as said below
- upstream_gradient: bfloat16 [4, 8192, 768], P('fsdp', 'seq'), may hold values from -6 to 6
- entering_projection: bfloat16 [2, 768, 3352], P(None, 'fsdp'), may hold values from -0.21875 to 0.21875
- exit_projection: bfloat16 [2, 1536, 768], P(None, 'fsdp'), may hold values from -0.15625 to 0.15625
- filter_kernels: bfloat16 [2, 4, 1792], P(None, None, 'fsdp'), may hold values from -3 to 3
- filter_shifts: bfloat16 [2, 1792], P(None, 'fsdp'), may hold values from -1.75 to 1.75
- stride_shifts: bfloat16 [2, 24], P(None, 'fsdp'), may hold values from -6.875 to -2.25
- log_shrink_rates: bfloat16 [2, 24], P(None, 'fsdp'), may hold values from -3 to 2.765625
- bypass_coefficient: bfloat16 [2, 24], P(None, 'fsdp'), may hold values from 0.5 to 1.5
- entry_scaling_gains: bfloat16 [2, 768], P(None, 'fsdp'), may hold values from 0.5 to 1.5
- gated_scaling_gains: bfloat16 [2, 1536], P(None, 'fsdp'), may hold values from 0.5 to 1.5
Outputs:
- outputs: bfloat16 [4, 8192, 768], P('fsdp', 'seq')
- input_grad: float32 [4, 8192, 768], P('fsdp', 'seq')
- grad_in_weight: float32 [2, 768, 3352], P(None, 'fsdp')
- grad_out_weight: float32 [2, 1536, 768], P(None, 'fsdp')
- grad_conv_weight: float32 [2, 4, 1792], P(None, None, 'fsdp')
- grad_conv_bias: float32 [2, 1792], P(None, 'fsdp')
- grad_step_bias: float32 [2, 24], P(None, 'fsdp')
- grad_decay_log: float32 [2, 24], P(None, 'fsdp')
- grad_skip_gain: float32 [2, 24], P(None, 'fsdp')
- grad_norm_gain: float32 [2, 768], P(None, 'fsdp')
- grad_gate_gain: float32 [2, 1536], P(None, 'fsdp')
Inputs may be any that keep to these rules, and one draw needn't show every extreme that they name: `token_articles`: document numbers never fall along a sequence. In one sequence, drawn from the seed, one document begins on the first device of seq and ends on the last; in every other sequence documents begin exactly at the first tokens of the two middle devices of seq. `extra_spikes`: zero except at a few positions of each sequence, where every head gets its own negative value.
All inputs are finite; a program needn't handle non-finite values.
Results may differ from a plain program's by a relative error of at most 0.02.
Values may be sent and summed in bfloat16 or wider, within the bound.
No kernel may reach another device: no remote copies, remote signals or barrier semaphores. Data moves between devices by JAX's collectives and lax.ppermute only.
A program may use at most 384 MiB of HBM per device.

v0:
```python
from functools import partial

import jax
import jax.numpy as jnp
from jax import lax
from jax.sharding import PartitionSpec as P

H = 24
P_SIZE = 64
N = 128
K = 4
CH = 256
E = 1536
CV = 1792


eps = 1e-05
highest = lax.Precision.HIGHEST


def passed_along(value, axis, steps):
    count = lax.axis_size(axis)
    first, last = (max(0, -steps), min(count, count - steps))
    return lax.ppermute(value, axis, [(source, source + steps) for source in range(first, last)])


def carried_in_2(value, axis, join, neutral):
    count, mine = (lax.axis_size(axis), lax.axis_index(axis))
    pieces = jax.tree.map(lambda part: lax.all_gather(part, axis), value)
    so_far = jax.tree.map(
        lambda part, zero: jnp.full_like(part, 0) + jnp.asarray(zero, part.dtype), value, neutral
    )

    def carried_lap(position, so_far):
        longer = join(so_far, jax.tree.map(lambda part: part[position], pieces))
        return jax.tree.map(lambda new, old: jnp.where(position < mine, new, old), longer, so_far)

    return lax.fori_loop(0, count - 1, carried_lap, so_far)


def entering(array, axis, combine, identity):
    length, mine = (lax.axis_size(axis), lax.axis_index(axis))
    everything = jax.tree.map(
        lambda part, kind: lax.all_gather(part.astype(kind), axis),
        array,
        jax.tree.map(lambda a: jnp.bfloat16 if a.dtype == jnp.float32 else a.dtype, array),
    )
    start = jax.tree.map(
        lambda part, zero: jnp.broadcast_to(jnp.asarray(zero, part.dtype), part.shape),
        array,
        identity,
    )

    def entering_lap(k, before):
        at = length - 1 - k
        reached = at > mine
        new = combine(
            before, jax.tree.map(lambda part, own: part[at].astype(own.dtype), everything, array)
        )
        return jax.tree.map(lambda a, b: jnp.where(reached, a, b), new, before)

    return lax.fori_loop(0, length, entering_lap, start)


def norm_input(running_activation, gain_vec):
    return (
        running_activation
        * lax.rsqrt(jnp.mean(running_activation * running_activation, axis=-1, keepdims=True) + eps)
        * gain_vec
    )


def gated_norm(mixed_out, gate_proj, gain_vec):
    gated = mixed_out * jax.nn.silu(gate_proj)
    return gated * lax.rsqrt(jnp.mean(gated * gated, axis=-1, keepdims=True) + eps) * gain_vec


def conv_mix(extended, article_widened, filter_kernel_entry, filter_shift_term):
    taps_count = filter_kernel_entry.shape[0]
    row_count = extended.shape[0] - taps_count + 1
    own_doc = article_widened[taps_count - 1 :]
    mix_total = filter_shift_term
    for offset in range(taps_count):
        same_doc = (article_widened[offset : offset + row_count] == own_doc).astype(jnp.float32)[
            :, None
        ]
        mix_total = (
            mix_total
            + filter_kernel_entry[offset] * extended[offset : offset + row_count] * same_doc
        )
    return mix_total


def build_sources(
    filter_source,
    edge_series,
    unscaled_stride,
    filter_kernel_entry,
    filter_shift_term,
    stride_shift,
    shrink_multiplier,
    article_widened,
    spike_log_rate,
):
    extended = jnp.concatenate([edge_series, filter_source])
    activated = jax.nn.silu(
        conv_mix(extended, article_widened, filter_kernel_entry, filter_shift_term)
    )
    channel_group_source = activated[:, :E].reshape(activated.shape[0], H, P_SIZE)
    arriving_memory = activated[:, E : E + N]
    leaving_memory = activated[:, E + N :]
    stride_magnitude = jax.nn.softplus(unscaled_stride + stride_shift)
    shrink_log_rate = spike_log_rate - stride_magnitude * jnp.exp(shrink_multiplier)
    return (
        channel_group_source,
        arriving_memory,
        leaving_memory,
        stride_magnitude,
        shrink_log_rate,
    )


def group_math(
    prior_state,
    seg_prior,
    channel_group_source,
    arriving_memory,
    leaving_memory,
    stride_heads,
    log_heads,
    article_number,
):
    length = article_number.shape[0]
    cum_log = jnp.cumsum(log_heads, axis=1)
    order_mask = jnp.arange(length)[:, None] >= jnp.arange(length)[None, :]
    kept_mask = (order_mask & (article_number[:, None] == article_number[None, :]))[None, :, :]
    gap_log = jnp.where(kept_mask, cum_log[:, :, None] - cum_log[:, None, :], 0.0)
    decay_mat = jnp.where(kept_mask, jnp.exp(gap_log), 0.0)
    scores = jnp.dot(
        leaving_memory, arriving_memory.T, precision=highest, preferred_element_type=jnp.float32
    )
    mixing = decay_mat * scores[None, :, :] * stride_heads[:, None, :]
    result = jnp.einsum("hij,jhp->ihp", mixing, channel_group_source, precision=highest)
    start_gain = (article_number == seg_prior).astype(jnp.float32)[None, :] * jnp.exp(cum_log)
    result = result + start_gain.T[:, :, None] * jnp.einsum(
        "in,hpn->ihp", leaving_memory, prior_state, precision=highest
    )
    tail_gain = (
        (article_number == article_number[-1]).astype(jnp.float32)[None, :]
        * jnp.exp(cum_log[:, -1:] - cum_log)
        * stride_heads
    )
    carried = jnp.exp(cum_log[:, -1]) * (article_number[-1] == seg_prior).astype(jnp.float32)
    new_state = carried[:, None, None] * prior_state + jnp.einsum(
        "hj,jhp,jn->hpn", tail_gain, channel_group_source, arriving_memory, precision=highest
    )
    return (new_state, result)


def device_pass(
    channel_group_source,
    arriving_memory,
    leaving_memory,
    stride_magnitude,
    shrink_log_rate,
    article_number,
    seg_before,
):
    block_count = channel_group_source.shape[0] // CH

    def to_blocks(array_in):
        return array_in.reshape((block_count, CH) + array_in.shape[1:])

    def heads_blocks(array_in):
        return jnp.transpose(array_in.T.reshape(array_in.shape[1], block_count, CH), (1, 0, 2))

    prior_ids = jnp.concatenate([jnp.reshape(seg_before, (1,)), article_number[:-1]])
    starts = to_blocks(prior_ids)[:, 0]

    def one_block(prior_state, partition_parts):
        return group_math(prior_state, *partition_parts)

    zero_state = jnp.zeros(
        (channel_group_source.shape[1], channel_group_source.shape[2], arriving_memory.shape[1]),
        jnp.float32,
    )
    final_state, block_out = lax.scan(
        jax.checkpoint(one_block),
        zero_state,
        (
            starts,
            to_blocks(channel_group_source),
            to_blocks(arriving_memory),
            to_blocks(leaving_memory),
            heads_blocks(stride_magnitude),
            heads_blocks(shrink_log_rate),
            to_blocks(article_number),
        ),
    )
    carry_all = jnp.exp(jnp.sum(shrink_log_rate, axis=0)) * (
        article_number[-1] == seg_before
    ).astype(jnp.float32)
    return (block_out.reshape(channel_group_source.shape), carry_all, final_state)


def finish(
    local_out,
    channel_group_source,
    leaving_memory,
    shrink_log_rate,
    gate_proj,
    incoming,
    skip_vec,
    gain_out,
    article_number,
    seg_before,
):
    start_gain = (article_number == seg_before).astype(jnp.float32)[:, None] * jnp.exp(
        jnp.cumsum(shrink_log_rate, axis=0)
    )
    carried_in = jnp.einsum("in,hpn->ihp", leaving_memory, incoming, precision=highest)
    mixed_out = (
        local_out + start_gain[:, :, None] * carried_in + skip_vec[:, None] * channel_group_source
    )
    return gated_norm(mixed_out.reshape(mixed_out.shape[0], E), gate_proj, gain_out)


def chain_join(earlier, later):
    return (earlier[0] * later[0], later[1] + later[0][:, None, None] * earlier[1])


def contract_rows(left, right):
    return lax.dot_general(
        left, right, (((0,), (0,)), ((), ())), preferred_element_type=jnp.float32
    )


def contract_cols(left, right):
    return lax.dot_general(
        left, right, (((1,), (1,)), ((), ())), preferred_element_type=jnp.float32
    )


def fetch_layer(
    entering_projection,
    exit_projection,
    filter_kernels,
    filter_shifts,
    stride_shifts,
    log_shrink_rates,
    bypass_coefficient,
    entry_scaling_gains,
    gated_scaling_gains,
    tier_number,
):
    return (
        lax.all_gather(entering_projection[tier_number], "fsdp", axis=0, tiled=True),
        lax.all_gather(exit_projection[tier_number], "fsdp", axis=0, tiled=True),
        lax.all_gather(filter_kernels[tier_number], "fsdp", axis=1, tiled=True),
        lax.all_gather(filter_shifts[tier_number], "fsdp", axis=0, tiled=True),
        lax.all_gather(stride_shifts[tier_number], "fsdp", axis=0, tiled=True),
        lax.all_gather(log_shrink_rates[tier_number], "fsdp", axis=0, tiled=True),
        lax.all_gather(bypass_coefficient[tier_number], "fsdp", axis=0, tiled=True),
        lax.all_gather(entry_scaling_gains[tier_number], "fsdp", axis=0, tiled=True),
        lax.all_gather(gated_scaling_gains[tier_number], "fsdp", axis=0, tiled=True),
    )


def local(
    first_tier_source,
    token_articles,
    extra_spikes,
    upstream_gradient,
    entering_projection,
    exit_projection,
    filter_kernels,
    filter_shifts,
    stride_shifts,
    log_shrink_rates,
    bypass_coefficient,
    entry_scaling_gains,
    gated_scaling_gains,
):
    current = first_tier_source[0].astype(jnp.float32)
    article_number = token_articles[0]
    spike_log_rate = extra_spikes[0]
    row_count = article_number.shape[0]
    layers_count = entering_projection.shape[0]
    edge_ids = passed_along(article_number[row_count - (K - 1) :], "seq", 1)
    article_widened = jnp.concatenate([edge_ids, article_number])
    seg_before = edge_ids[K - 2]
    records = []
    for tier_number in range(layers_count):
        weights = fetch_layer(
            entering_projection,
            exit_projection,
            filter_kernels,
            filter_shifts,
            stride_shifts,
            log_shrink_rates,
            bypass_coefficient,
            entry_scaling_gains,
            gated_scaling_gains,
            tier_number,
        )
        mat_in, mat_out = (weights[0], weights[1])
        (
            filter_kernel_entry,
            filter_shift_term,
            stride_shift,
            shrink_multiplier,
            skip_vec,
            gain_in,
            gain_out,
        ) = tuple((partition_owner.astype(jnp.float32) for partition_owner in weights[2:]))
        normed, norm_pull = jax.vjp(norm_input, current, gain_in)
        normed_low = normed.astype(jnp.bfloat16)
        projected = jnp.dot(normed_low, mat_in, preferred_element_type=jnp.float32)
        gate_proj = projected[:, :E]
        filter_source = projected[:, E : E + CV]
        unscaled_stride = projected[:, E + CV :]
        edge_series = passed_along(filter_source[row_count - (K - 1) :], "seq", 1)
        prepared, prep_pull = jax.vjp(
            partial(build_sources, article_widened=article_widened, spike_log_rate=spike_log_rate),
            filter_source,
            edge_series,
            unscaled_stride,
            filter_kernel_entry,
            filter_shift_term,
            stride_shift,
            shrink_multiplier,
        )
        channel_group_source, arriving_memory, leaving_memory, stride_magnitude, shrink_log_rate = (
            prepared
        )
        passed, pass_pull = jax.vjp(
            partial(device_pass, article_number=article_number, seg_before=seg_before),
            channel_group_source,
            arriving_memory,
            leaving_memory,
            stride_magnitude,
            shrink_log_rate,
        )
        local_out, carry_all, final_state = passed
        incoming = carried_in_2(
            (carry_all, final_state),
            "seq",
            chain_join,
            (jnp.ones_like(carry_all), jnp.zeros_like(final_state)),
        )[1]
        normed_out, finish_pull = jax.vjp(
            partial(finish, article_number=article_number, seg_before=seg_before),
            local_out,
            channel_group_source,
            leaving_memory,
            shrink_log_rate,
            gate_proj,
            incoming,
            skip_vec,
            gain_out,
        )
        out_low = normed_out.astype(jnp.bfloat16)
        current = current + jnp.dot(out_low, mat_out, preferred_element_type=jnp.float32)
        stored = weights
        records.append(
            (
                stored,
                normed_low,
                out_low,
                norm_pull,
                prep_pull,
                pass_pull,
                finish_pull,
                carry_all,
                incoming,
            )
        )
    grad_x = upstream_gradient[0].astype(jnp.float32)
    gathered_grads = [None] * layers_count
    for tier_number in reversed(range(layers_count)):
        (
            stored,
            normed_low,
            out_low,
            norm_pull,
            prep_pull,
            pass_pull,
            finish_pull,
            carry_all,
            incoming,
        ) = records[tier_number]
        weights = stored
        mat_in, mat_out = (weights[0], weights[1])
        grad_branch = grad_x.astype(jnp.bfloat16)
        grad_mat_out = contract_rows(out_low, grad_branch)
        grad_normed_out = contract_cols(grad_branch, mat_out)
        (
            grad_local,
            grad_head_a,
            grad_sout_a,
            grad_decay_a,
            grad_gate,
            grad_incoming,
            grad_skip,
            grad_gain_out,
        ) = finish_pull(grad_normed_out)
        later_grads = entering(
            (carry_all, grad_incoming),
            "seq",
            chain_join,
            (jnp.ones_like(carry_all), jnp.zeros_like(grad_incoming)),
        )[1]
        grad_carry = jnp.sum(later_grads * incoming, axis=(1, 2))
        grad_head_b, grad_sin, grad_sout_b, grad_step, grad_decay_b = pass_pull(
            (grad_local, grad_carry, later_grads)
        )
        (
            grad_conv_in,
            grad_edge,
            grad_dt_raw,
            grad_conv_wt,
            grad_conv_shift,
            grad_step_shift,
            grad_decay_rate,
        ) = prep_pull(
            (
                grad_head_a + grad_head_b,
                grad_sin,
                grad_sout_a + grad_sout_b,
                grad_step,
                grad_decay_a + grad_decay_b,
            )
        )
        back_rows = passed_along(grad_edge, "seq", -1)
        grad_conv_in = grad_conv_in.at[row_count - (K - 1) :].add(back_rows)
        grad_projected = jnp.concatenate([grad_gate, grad_conv_in, grad_dt_raw], axis=1).astype(
            jnp.bfloat16
        )
        grad_mat_in = contract_rows(normed_low, grad_projected)
        grad_normed = contract_cols(grad_projected, mat_in)
        grad_resid, grad_gain_in = norm_pull(grad_normed)
        grad_x = grad_x + grad_resid
        shards = (
            lax.psum_scatter(
                grad_mat_in.astype(jnp.bfloat16), "fsdp", scatter_dimension=0, tiled=True
            ).astype(jnp.float32),
            lax.psum_scatter(
                grad_mat_out.astype(jnp.bfloat16), "fsdp", scatter_dimension=0, tiled=True
            ).astype(jnp.float32),
            lax.psum_scatter(
                grad_conv_wt.astype(jnp.bfloat16), "fsdp", scatter_dimension=1, tiled=True
            ).astype(jnp.float32),
            lax.psum_scatter(
                grad_conv_shift.astype(jnp.bfloat16), "fsdp", scatter_dimension=0, tiled=True
            ).astype(jnp.float32),
            lax.psum_scatter(
                grad_step_shift.astype(jnp.bfloat16), "fsdp", scatter_dimension=0, tiled=True
            ).astype(jnp.float32),
            lax.psum_scatter(
                grad_decay_rate.astype(jnp.bfloat16), "fsdp", scatter_dimension=0, tiled=True
            ).astype(jnp.float32),
            lax.psum_scatter(
                grad_skip.astype(jnp.bfloat16), "fsdp", scatter_dimension=0, tiled=True
            ).astype(jnp.float32),
            lax.psum_scatter(
                grad_gain_in.astype(jnp.bfloat16), "fsdp", scatter_dimension=0, tiled=True
            ).astype(jnp.float32),
            lax.psum_scatter(
                grad_gain_out.astype(jnp.bfloat16), "fsdp", scatter_dimension=0, tiled=True
            ).astype(jnp.float32),
        )
        gathered_grads[tier_number] = (
            lax.psum(shards[0].astype(jnp.bfloat16), "seq").astype(jnp.float32),
            lax.psum(shards[1].astype(jnp.bfloat16), "seq").astype(jnp.float32),
            lax.psum(shards[2].astype(jnp.bfloat16), "seq").astype(jnp.float32),
            lax.psum(shards[3].astype(jnp.bfloat16), "seq").astype(jnp.float32),
            lax.psum(shards[4].astype(jnp.bfloat16), "seq").astype(jnp.float32),
            lax.psum(shards[5].astype(jnp.bfloat16), "seq").astype(jnp.float32),
            lax.psum(shards[6].astype(jnp.bfloat16), "seq").astype(jnp.float32),
            lax.psum(shards[7].astype(jnp.bfloat16), "seq").astype(jnp.float32),
            lax.psum(shards[8].astype(jnp.bfloat16), "seq").astype(jnp.float32),
        )
    stacked = tuple(
        (
            jnp.stack(
                [
                    gathered_grads[tier_number][partition_owner]
                    for tier_number in range(layers_count)
                ]
            )
            for partition_owner in range(9)
        )
    )
    return (current.astype(jnp.bfloat16)[None], grad_x[None]) + stacked


def solution(mesh):
    placed = (
        P("fsdp", "seq", None),
        P("fsdp", "seq"),
        P("fsdp", "seq", None),
        P("fsdp", "seq", None),
        P(None, "fsdp", None),
        P(None, "fsdp", None),
        P(None, None, "fsdp"),
        P(None, "fsdp"),
        P(None, "fsdp"),
        P(None, "fsdp"),
        P(None, "fsdp"),
        P(None, "fsdp"),
        P(None, "fsdp"),
    )
    return jax.shard_map(
        local,
        mesh=mesh,
        in_specs=placed,
        out_specs=(
            P("fsdp", "seq", None),
            P("fsdp", "seq", None),
            P(None, "fsdp", None),
            P(None, "fsdp", None),
            P(None, None, "fsdp"),
            P(None, "fsdp"),
            P(None, "fsdp"),
            P(None, "fsdp"),
            P(None, "fsdp"),
            P(None, "fsdp"),
            P(None, "fsdp"),
        ),
        check_vma=False,
    )
```

profile of v0, /device:TPU:1, one launch (start us, length us, event | category | flops | bytes accessed | tf_op | source)
XLA Modules:
  0.0 2455.3 jit_solution(8878395210840862571)
XLA Ops:
  20.5 22.9 all-reduce.56
  46.0 33.0 %all-gather.5 = bf16[1,4,1792]{1,0,2:T(2,128)(2,1)S(1)} all-gather(bf16[1,4,448]{1,0,2:T(2,128)(2,1)S(1)} %copy.543), channel_id=7, replica_groups=mesh['seq'=8,'fsdp'=4] {'fsdp'}, dimensions={2}, use_global_device_ids=true | all-gather | bytes 17920 | tf_op jit(solution)/shard_map/all_gather | solution.py:259
  82.7 37.3 %slice_reduce_fusion.17 = (f32[1792]{0:T(1024)S(1)}, f32[1792]{0:T(1024)S(1)}, f32[1792]{0:T(1024)S(1)}, f32[1792]{0:T(1024)S(1)}) fusion(f32[1,4,1792]{1,0,2:T(1,128)S(1)} %convert_element_type.435), kind=kLoop, calls=%fused_computation.447 | loop fusion | bytes 57344 | tf_op jit(solution)/shard_map/jvp()/slice | solution.py:89
  155.3 19.4 fusion.203
  201.0 235.4 %while.146 = (s32[]{:T(128)}, f32[24,64,128]{2,1,0:T(8,128)S(1)}, f32[4,256,24,64]{1,0,3,2:T(4,128)}, f32[4,24,64,128]{3,2,1,0:T(8,128)}, f32[4,24,256]{2,1,0:T(...) while((s32[]{:T(128)}, f32[24,64,128]{2,1,0:T(8,128)S(1)}, ...), condition=%wide.region_4.6_spmd.clone, body=%wide.region_1.5_spmd.clone.sunk | while | flops 2527624192 | bytes 19774056 | solution.py:187
  220.0 34.6 %dynamic_update_slice.157 = f32[4,256,24,64]{1,0,3,2:T(4,128)} dynamic-update-slice(f32[4,256,24,64]{1,0,3,2:T(4,128)} %get-tuple-element.2930, f32[1,256,24,64]{1,0,3,2:T(1,128)S(1)} %copy.756, s32[]{:T(128)} %get-tuple-element.2928, s32[]{:T(128)} %constant.399.clone.1..sunk.2, s32[]{:T(128)} %constant.399.clone.1..sunk.2, s32[]{:T(128)} %constant.399.clone.1..sunk.2) | dynamic-update-slice | bytes 3145732 | tf_op jit(solution)/shard_map/jvp()/while/body/jit(dynamic_update_index_in_dim)/dynamic_update_slice | solution.py:187
  278.8 34.6 %dynamic_update_slice.157 = f32[4,256,24,64]{1,0,3,2:T(4,128)} dynamic-update-slice(f32[4,256,24,64]{1,0,3,2:T(4,128)} %get-tuple-element.2930, f32[1,256,24,64]{1,0,3,2:T(1,128)S(1)} %copy.756, s32[]{:T(128)} %get-tuple-element.2928, s32[]{:T(128)} %constant.399.clone.1..sunk.2, s32[]{:T(128)} %constant.399.clone.1..sunk.2, s32[]{:T(128)} %constant.399.clone.1..sunk.2) | dynamic-update-slice | bytes 3145732 | tf_op jit(solution)/shard_map/jvp()/while/body/jit(dynamic_update_index_in_dim)/dynamic_update_slice | solution.py:187
  337.6 34.6 %dynamic_update_slice.157 = f32[4,256,24,64]{1,0,3,2:T(4,128)} dynamic-update-slice(f32[4,256,24,64]{1,0,3,2:T(4,128)} %get-tuple-element.2930, f32[1,256,24,64]{1,0,3,2:T(1,128)S(1)} %copy.756, s32[]{:T(128)} %get-tuple-element.2928, s32[]{:T(128)} %constant.399.clone.1..sunk.2, s32[]{:T(128)} %constant.399.clone.1..sunk.2, s32[]{:T(128)} %constant.399.clone.1..sunk.2) | dynamic-update-slice | bytes 3145732 | tf_op jit(solution)/shard_map/jvp()/while/body/jit(dynamic_update_index_in_dim)/dynamic_update_slice | solution.py:187
  396.4 34.6 %dynamic_update_slice.157 = f32[4,256,24,64]{1,0,3,2:T(4,128)} dynamic-update-slice(f32[4,256,24,64]{1,0,3,2:T(4,128)} %get-tuple-element.2930, f32[1,256,24,64]{1,0,3,2:T(1,128)S(1)} %copy.756, s32[]{:T(128)} %get-tuple-element.2928, s32[]{:T(128)} %constant.399.clone.1..sunk.2, s32[]{:T(128)} %constant.399.clone.1..sunk.2, s32[]{:T(128)} %constant.399.clone.1..sunk.2) | dynamic-update-slice | bytes 3145732 | tf_op jit(solution)/shard_map/jvp()/while/body/jit(dynamic_update_index_in_dim)/dynamic_update_slice | solution.py:187
  459.1 17.4 all-gather.16
  479.2 37.1 %slice_reduce_fusion.13 = (f32[1792]{0:T(1024)S(1)}, f32[1792]{0:T(1024)S(1)}, f32[1792]{0:T(1024)S(1)}, f32[1792]{0:T(1024)S(1)}) fusion(f32[1,4,1792]{1,0,2:T(1,128)S(1)} %convert_element_type.442), kind=kLoop, calls=%fused_computation.443 | loop fusion | bytes 57344 | tf_op jit(solution)/shard_map/jvp()/slice | solution.py:89
  518.2 14.3 all-reduce.30
  566.8 12.3 multiply_add_fusion.5
  595.1 37.1 %all-gather.41.cloned.1.call-done = bf16[1,768,3352]{2,1,0:T(8,128)(2,1)} async-done(((bf16[1,192,3352]{2,1,0:T(8,128)(2,1)}), bf16[1,768,3352]{2,1,0:T(8,128)(2,1)}) %all-gather.41.cloned.1.call-update) | async-done | bytes 5148688 | tf_op jit(solution)/shard_map/all_gather | solution.py:257
  661.3 19.5 fusion.202
  707.0 235.0 %while.148 = (s32[]{:T(128)}, f32[24,64,128]{2,1,0:T(8,128)S(1)}, f32[4,256,24,64]{1,0,3,2:T(4,128)}, f32[4,24,64,128]{3,2,1,0:T(8,128)}, f32[4,24,256]{2,1,0:T(...) while((s32[]{:T(128)}, f32[24,64,128]{2,1,0:T(8,128)S(1)}, ...), condition=%wide.region_15.17_spmd.clone, body=%wide.region_12.16_spmd.clone.sunk | while | flops 2527624192 | bytes 19774056 | solution.py:187
  726.2 34.5 %dynamic_update_slice.159 = f32[4,256,24,64]{1,0,3,2:T(4,128)} dynamic-update-slice(f32[4,256,24,64]{1,0,3,2:T(4,128)} %get-tuple-element.2996, f32[1,256,24,64]{1,0,3,2:T(1,128)S(1)} %copy.760, s32[]{:T(128)} %get-tuple-element.2994, s32[]{:T(128)} %constant.399.clone.1..sunk.4, s32[]{:T(128)} %constant.399.clone.1..sunk.4, s32[]{:T(128)} %constant.399.clone.1..sunk.4) | dynamic-update-slice | bytes 3145732 | tf_op jit(solution)/shard_map/jvp()/while/body/jit(dynamic_update_index_in_dim)/dynamic_update_slice | solution.py:187
  784.8 34.5 %dynamic_update_slice.159 = f32[4,256,24,64]{1,0,3,2:T(4,128)} dynamic-update-slice(f32[4,256,24,64]{1,0,3,2:T(4,128)} %get-tuple-element.2996, f32[1,256,24,64]{1,0,3,2:T(1,128)S(1)} %copy.760, s32[]{:T(128)} %get-tuple-element.2994, s32[]{:T(128)} %constant.399.clone.1..sunk.4, s32[]{:T(128)} %constant.399.clone.1..sunk.4, s32[]{:T(128)} %constant.399.clone.1..sunk.4) | dynamic-update-slice | bytes 3145732 | tf_op jit(solution)/shard_map/jvp()/while/body/jit(dynamic_update_index_in_dim)/dynamic_update_slice | solution.py:187
  843.5 34.5 %dynamic_update_slice.159 = f32[4,256,24,64]{1,0,3,2:T(4,128)} dynamic-update-slice(f32[4,256,24,64]{1,0,3,2:T(4,128)} %get-tuple-element.2996, f32[1,256,24,64]{1,0,3,2:T(1,128)S(1)} %copy.760, s32[]{:T(128)} %get-tuple-element.2994, s32[]{:T(128)} %constant.399.clone.1..sunk.4, s32[]{:T(128)} %constant.399.clone.1..sunk.4, s32[]{:T(128)} %constant.399.clone.1..sunk.4) | dynamic-update-slice | bytes 3145732 | tf_op jit(solution)/shard_map/jvp()/while/body/jit(dynamic_update_index_in_dim)/dynamic_update_slice | solution.py:187
  902.1 34.5 %dynamic_update_slice.159 = f32[4,256,24,64]{1,0,3,2:T(4,128)} dynamic-update-slice(f32[4,256,24,64]{1,0,3,2:T(4,128)} %get-tuple-element.2996, f32[1,256,24,64]{1,0,3,2:T(1,128)S(1)} %copy.760, s32[]{:T(128)} %get-tuple-element.2994, s32[]{:T(128)} %constant.399.clone.1..sunk.4, s32[]{:T(128)} %constant.399.clone.1..sunk.4, s32[]{:T(128)} %constant.399.clone.1..sunk.4) | dynamic-update-slice | bytes 3145732 | tf_op jit(solution)/shard_map/jvp()/while/body/jit(dynamic_update_index_in_dim)/dynamic_update_slice | solution.py:187
  963.9 13.1 all-reduce.36
  1004.0 12.3 multiply_add_fusion.4
  1023.9 13.7 all-gather.45.cloned.1.call-done
  1070.5 13.0 all-reduce.53
  1098.3 29.7 %reduce-window.160 = f32[24,8,128]{2,1,0:T(8,128)S(1)} reduce-window(f32[24,8,128]{2,1,0:T(8,128)S(1)} %bitcast.1029, f32[]{:T(128)} %constant.400.clone.1), window={size=1x1x128 pad=0_0x0_0x0_127}, to_apply=%region_39.41 | reduce-window | flops 3121152 | bytes 196612 | tf_op jit(solution)/shard_map/reduce-window.12
  1146.8 389.4 %while.144 = (s32[]{:T(128)}, f32[24,64,128]{2,1,0:T(8,128)}, f32[4,256,24,64]{1,0,3,2:T(4,128)}, f32[4,256,128]{2,1,0:T(8,128)}, f32[4,256,128]{2,1,0:T(8,128)}...) while((s32[]{:T(128)}, f32[24,64,128]{2,1,0:T(8,128)}, ...), condition=%wide.region_37.39_spmd, body=%wide.region_25.38_spmd.sunk | while | flops 5775502336 | bytes 68711848 | solution.py:187
  1203.5 34.7 %dynamic_update_slice.150 = f32[4,256,24,64]{1,0,3,2:T(4,128)} dynamic-update-slice(f32[4,256,24,64]{1,0,3,2:T(4,128)} %get-tuple-element.3094, f32[1,256,24,64]{1,0,3,2:T(1,128)} %copy.739, s32[]{:T(128)S(6)} %sub.522, s32[]{:T(128)} %constant.399.clone.1..sunk, s32[]{:T(128)} %constant.399.clone.1..sunk, s32[]{:T(128)} %constant.399.clone.1..sunk) | dynamic-update-slice | bytes 3145732 | tf_op jit(solution)/shard_map/transpose(jvp())/while/body/jit(dynamic_update_index_in_dim)/dynamic_update_slice | solution.py:187
  1300.7 34.7 %dynamic_update_slice.150 = f32[4,256,24,64]{1,0,3,2:T(4,128)} dynamic-update-slice(f32[4,256,24,64]{1,0,3,2:T(4,128)} %get-tuple-element.3094, f32[1,256,24,64]{1,0,3,2:T(1,128)} %copy.739, s32[]{:T(128)S(6)} %sub.522, s32[]{:T(128)} %constant.399.clone.1..sunk, s32[]{:T(128)} %constant.399.clone.1..sunk, s32[]{:T(128)} %constant.399.clone.1..sunk) | dynamic-update-slice | bytes 3145732 | tf_op jit(solution)/shard_map/transpose(jvp())/while/body/jit(dynamic_update_index_in_dim)/dynamic_update_slice | solution.py:187
  1397.9 34.7 %dynamic_update_slice.150 = f32[4,256,24,64]{1,0,3,2:T(4,128)} dynamic-update-slice(f32[4,256,24,64]{1,0,3,2:T(4,128)} %get-tuple-element.3094, f32[1,256,24,64]{1,0,3,2:T(1,128)} %copy.739, s32[]{:T(128)S(6)} %sub.522, s32[]{:T(128)} %constant.399.clone.1..sunk, s32[]{:T(128)} %constant.399.clone.1..sunk, s32[]{:T(128)} %constant.399.clone.1..sunk) | dynamic-update-slice | bytes 3145732 | tf_op jit(solution)/shard_map/transpose(jvp())/while/body/jit(dynamic_update_index_in_dim)/dynamic_update_slice | solution.py:187
  1495.1 34.7 %dynamic_update_slice.150 = f32[4,256,24,64]{1,0,3,2:T(4,128)} dynamic-update-slice(f32[4,256,24,64]{1,0,3,2:T(4,128)} %get-tuple-element.3094, f32[1,256,24,64]{1,0,3,2:T(1,128)} %copy.739, s32[]{:T(128)S(6)} %sub.522, s32[]{:T(128)} %constant.399.clone.1..sunk, s32[]{:T(128)} %constant.399.clone.1..sunk, s32[]{:T(128)} %constant.399.clone.1..sunk) | dynamic-update-slice | bytes 3145732 | tf_op jit(solution)/shard_map/transpose(jvp())/while/body/jit(dynamic_update_index_in_dim)/dynamic_update_slice | solution.py:187
  1558.1 15.3 multiply_reduce_fusion.12
  1587.5 11.5 pad_add_fusion.1
  1622.8 12.2 multiply_reduce_fusion.28
  1696.5 29.7 %reduce-window.162 = f32[24,8,128]{2,1,0:T(8,128)S(1)} reduce-window(f32[24,8,128]{2,1,0:T(8,128)S(1)} %bitcast.1030, f32[]{:T(128)} %constant.400.clone.1), window={size=1x1x128 pad=0_0x0_0x0_127}, to_apply=%region_60.62 | reduce-window | flops 3121152 | bytes 196612 | tf_op jit(solution)/shard_map/reduce-window.14
  1727.2 12.2 convolution_convert_fusion
  1757.4 389.5 %while.145 = (s32[]{:T(128)}, f32[24,64,128]{2,1,0:T(8,128)}, f32[4,256,24,64]{1,0,3,2:T(4,128)}, f32[4,256,128]{2,1,0:T(8,128)}, f32[4,256,128]{2,1,0:T(8,128)}...) while((s32[]{:T(128)}, f32[24,64,128]{2,1,0:T(8,128)}, ...), condition=%wide.region_58.60_spmd, body=%wide.region_46.59_spmd.sunk | while | flops 5775502336 | bytes 68711848 | solution.py:187
  1814.2 34.8 %dynamic_update_slice.155 = f32[4,256,24,64]{1,0,3,2:T(4,128)} dynamic-update-slice(f32[4,256,24,64]{1,0,3,2:T(4,128)} %get-tuple-element.3181, f32[1,256,24,64]{1,0,3,2:T(1,128)} %copy.750, s32[]{:T(128)S(6)} %sub.535, s32[]{:T(128)} %constant.399.clone.1..sunk.1, s32[]{:T(128)} %constant.399.clone.1..sunk.1, s32[]{:T(128)} %constant.399.clone.1..sunk.1) | dynamic-update-slice | bytes 3145732 | tf_op jit(solution)/shard_map/transpose(jvp())/while/body/jit(dynamic_update_index_in_dim)/dynamic_update_slice | solution.py:187
  1911.4 34.7 %dynamic_update_slice.155 = f32[4,256,24,64]{1,0,3,2:T(4,128)} dynamic-update-slice(f32[4,256,24,64]{1,0,3,2:T(4,128)} %get-tuple-element.3181, f32[1,256,24,64]{1,0,3,2:T(1,128)} %copy.750, s32[]{:T(128)S(6)} %sub.535, s32[]{:T(128)} %constant.399.clone.1..sunk.1, s32[]{:T(128)} %constant.399.clone.1..sunk.1, s32[]{:T(128)} %constant.399.clone.1..sunk.1) | dynamic-update-slice | bytes 3145732 | tf_op jit(solution)/shard_map/transpose(jvp())/while/body/jit(dynamic_update_index_in_dim)/dynamic_update_slice | solution.py:187
  2008.6 34.7 %dynamic_update_slice.155 = f32[4,256,24,64]{1,0,3,2:T(4,128)} dynamic-update-slice(f32[4,256,24,64]{1,0,3,2:T(4,128)} %get-tuple-element.3181, f32[1,256,24,64]{1,0,3,2:T(1,128)} %copy.750, s32[]{:T(128)S(6)} %sub.535, s32[]{:T(128)} %constant.399.clone.1..sunk.1, s32[]{:T(128)} %constant.399.clone.1..sunk.1, s32[]{:T(128)} %constant.399.clone.1..sunk.1) | dynamic-update-slice | bytes 3145732 | tf_op jit(solution)/shard_map/transpose(jvp())/while/body/jit(dynamic_update_index_in_dim)/dynamic_update_slice | solution.py:187
  2105.8 34.7 %dynamic_update_slice.155 = f32[4,256,24,64]{1,0,3,2:T(4,128)} dynamic-update-slice(f32[4,256,24,64]{1,0,3,2:T(4,128)} %get-tuple-element.3181, f32[1,256,24,64]{1,0,3,2:T(1,128)} %copy.750, s32[]{:T(128)S(6)} %sub.535, s32[]{:T(128)} %constant.399.clone.1..sunk.1, s32[]{:T(128)} %constant.399.clone.1..sunk.1, s32[]{:T(128)} %constant.399.clone.1..sunk.1) | dynamic-update-slice | bytes 3145732 | tf_op jit(solution)/shard_map/transpose(jvp())/while/body/jit(dynamic_update_index_in_dim)/dynamic_update_slice | solution.py:187
  2172.5 14.6 multiply_reduce_fusion.16
  2205.3 12.9 pad_add_fusion
  2232.0 11.3 convolution_convert_fusion.1
  2270.0 16.8 all-reduce.55
  2287.4 49.7 %reduce-scatter.11.cloned.1.call-done = bf16[192,3352]{1,0:T(8,128)(2,1)} async-done(((bf16[768,3352]{1,0:T(8,128)(2,1)}), bf16[192,3352]{1,0:T(8,128)(2,1)}) %reduce-scatter.11.cloned.1.call-update) | async-done | bytes 1287184 | tf_op jit(solution)/shard_map/reduce_scatter | solution.py:444
  2346.4 13.1 reduce-scatter.19.cloned.1.call-done
  2360.5 22.2 all-reduce.52
  2386.8 54.5 %all-reduce.59.cloned.1.call-done = (bf16[1,192,3352]{2,1,0:T(8,128)(2,1)}, bf16[1,192,3352]{2,1,0:T(8,128)(2,1)}, bf16[1,384,768]{2,1,0:T(8,128)(2,1)}, bf16[1,384,768]{2,1,0:T(8,128)(2,1)}) async-done(((bf16[1,192,3352]{2,1,0:T(8,128)(2,1)}, bf16[1,192,3352]{2,1,0:T(8,128)(2,1)}, bf16[1,384,768]{2,1,0:T(8,128)(2,1)}, bf16[1,384,768]{2,1,0:T(8,128)(2,1)}), (bf16[1,192,3352]{2,1,0:T(8,128)(2,1)}, ...) | async-done | bytes 3754000 | tf_op jit(solution)/shard_map/psum | solution.py:473
  (1522 shorter events, 1282.0 us)
Async XLA Ops:
  7.3 120.0 %all-gather.35.cloned.1.call-start = ((), (), s32[]{:S(2)}) async-start(), calls=%async_computation.10 | async-start | bytes 6635520 | tf_op jit(solution)/shard_map/all_gather | solution.py:257
  10.8 538.2 %all-gather.37.cloned.1.call-start = ((), (), s32[]{:S(2)}) async-start(), calls=%async_computation.11 | async-start | bytes 7077888 | tf_op jit(solution)/shard_map/all_gather | solution.py:29
  10.9 109.2 %collective-permute-start = (s32[3]{0:T(128)S(1)}, s32[3]{0:T(128)S(1)}, u32[]{:S(2)}, u32[]{:S(2)}) collective-permute-start(s32[3]{0:T(128)S(1)} %slice_bitcast_fusion.4), channel_id=1, source_target_pairs={{0,4},{4,8},{8,12},{12,16},{16,20},{20,24},{24,28},{1,5},{5,9},{9,... | collective-permute-start | bytes 44 | tf_op jit(solution)/shard_map/ppermute | solution.py:24
  43.4 92.5 %copy-start.139 = (f32[768]{0:T(1024)}, f32[768]{0:T(1024)S(1)}, u32[]{:S(2)}) copy-start(f32[768]{0:T(1024)S(1)} %convert_element_type.447) | copy-start | bytes 9220
  45.1 90.8 %copy-start.34 = (bf16[1,1024,768]{1,2,0:T(8,128)(2,1)}, bf16[1,1024,768]{1,2,0:T(8,128)(2,1)S(1)}, u32[]{:S(2)}) copy-start(bf16[1,1024,768]{1,2,0:T(8,128)(2,1)S(1)} %copy.425) | copy-start | bytes 4718596
  80.0 65.0 %copy-start.163 = (f32[24]{0:T(128)}, f32[24]{0:T(128)S(1)}, u32[]{:S(2)}) copy-start(f32[24]{0:T(128)S(1)} %convert_element_type.448) | copy-start | bytes 292
  82.7 62.3 %copy-start.165 = (f32[24]{0:T(128)}, f32[24]{0:T(128)S(1)}, u32[]{:S(2)}) copy-start(f32[24]{0:T(128)S(1)} %convert_exponential_fusion.1) | copy-start | bytes 292
  82.7 53.2 %copy-start.141 = (f32[1024]{0:T(1024)}, f32[1024]{0:T(1024)S(1)}, u32[]{:S(2)}) copy-start(f32[1024]{0:T(1024)S(1)} %fusion.308) | copy-start | bytes 12292
  141.4 13.5 collective-permute-start.1
  436.4 103.0 %copy-start.39 = (f32[4,256,128]{2,1,0:T(8,128)}, f32[4,256,128]{2,1,0:T(8,128)S(1)}, u32[]{:S(2)}) copy-start(f32[4,256,128]{2,1,0:T(8,128)S(1)} %get-tuple-element.3247) | copy-start | bytes 1572868
  436.4 103.0 %copy-start.40 = (f32[4,256,128]{2,1,0:T(8,128)}, f32[4,256,128]{2,1,0:T(8,128)S(1)}, u32[]{:S(2)}) copy-start(f32[4,256,128]{2,1,0:T(8,128)S(1)} %get-tuple-element.3248) | copy-start | bytes 1572868
  436.4 103.0 %copy-start.63 = (f32[4,24,256]{2,1,0:T(8,128)}, f32[4,24,256]{2,1,0:T(8,128)S(1)}, u32[]{:S(2)}) copy-start(f32[4,24,256]{2,1,0:T(8,128)S(1)} %get-tuple-element.3287) | copy-start | bytes 294916
  436.5 81.2 %copy-start.157 = (f32[24]{0:T(128)S(1)}, f32[24]{0:T(128)}, u32[]{:S(2)}) copy-start(f32[24]{0:T(128)} %get-tuple-element.2234) | copy-start | bytes 292
  436.5 96.1 %copy-start.72 = (f32[1024,24]{0,1:T(8,128)S(1)}, f32[1024,24]{0,1:T(8,128)}, u32[]{:S(2)}) copy-start(f32[1024,24]{0,1:T(8,128)} %copy-done.71) | copy-start | bytes 294916
  437.3 103.1 %copy-start.102 = (f32[1024]{0:T(1024)S(1)}, f32[1024]{0:T(1024)}, u32[]{:S(2)}) copy-start(f32[1024]{0:T(1024)} %get-tuple-element.2296) | copy-start | bytes 12292
  437.3 149.6 %all-gather.39.cloned.1.call-start = ((), (), s32[]{:S(2)}) async-start(), calls=%async_computation.12 | async-start | bytes 2949120 | tf_op jit(solution)/shard_map/all_gather | solution.py:258
  439.7 192.4 %all-gather.41.cloned.1.call-start = ((), (), s32[]{:S(2)}) async-start(), calls=%async_computation.13 | async-start | bytes 6635520 | tf_op jit(solution)/shard_map/all_gather | solution.py:257
  440.3 545.9 %all-gather.43.cloned.1.call-start = ((), (), s32[]{:S(2)}) async-start(), calls=%async_computation.14 | async-start | bytes 7077888 | tf_op jit(solution)/shard_map/all_gather | solution.py:29
  455.3 176.9 %copy-start.143 = (f32[768]{0:T(1024)}, f32[768]{0:T(1024)S(1)}, u32[]{:S(2)}) copy-start(f32[768]{0:T(1024)S(1)} %convert_element_type.452) | copy-start | bytes 9220
  516.3 145.0 %copy-start.113 = (f32[1792]{0:T(1024)}, f32[1792]{0:T(1024)S(1)}, u32[]{:S(2)}) copy-start(f32[1792]{0:T(1024)S(1)} %get-tuple-element.2005) | copy-start | bytes 21508
  516.3 145.0 %copy-start.115 = (f32[1792]{0:T(1024)}, f32[1792]{0:T(1024)S(1)}, u32[]{:S(2)}) copy-start(f32[1792]{0:T(1024)S(1)} %get-tuple-element.2006) | copy-start | bytes 21508
  516.3 145.0 %copy-start.117 = (f32[1792]{0:T(1024)}, f32[1792]{0:T(1024)S(1)}, u32[]{:S(2)}) copy-start(f32[1792]{0:T(1024)S(1)} %get-tuple-element.2007) | copy-start | bytes 21508
  516.3 145.0 %copy-start.119 = (f32[1792]{0:T(1024)}, f32[1792]{0:T(1024)S(1)}, u32[]{:S(2)}) copy-start(f32[1792]{0:T(1024)S(1)} %get-tuple-element.2008) | copy-start | bytes 21508
  595.1 46.8 %copy-start.148 = (f32[1024]{0:T(1024)}, f32[1024]{0:T(1024)S(1)}, u32[]{:S(2)}) copy-start(f32[1024]{0:T(1024)S(1)} %get-tuple-element.2311) | copy-start | bytes 12292
  647.4 13.5 collective-permute-start.2
  942.0 43.3 %copy-start.41 = (f32[4,256,128]{2,1,0:T(8,128)}, f32[4,256,128]{2,1,0:T(8,128)S(1)}, u32[]{:S(2)}) copy-start(f32[4,256,128]{2,1,0:T(8,128)S(1)} %get-tuple-element.3249) | copy-start | bytes 1572868
  942.1 43.3 %copy-start.42 = (f32[4,256,128]{2,1,0:T(8,128)}, f32[4,256,128]{2,1,0:T(8,128)S(1)}, u32[]{:S(2)}) copy-start(f32[4,256,128]{2,1,0:T(8,128)S(1)} %get-tuple-element.3250) | copy-start | bytes 1572868
  942.9 94.7 %all-gather.45.cloned.1.call-start = ((), (), s32[]{:S(2)}) async-start(), calls=%async_computation.15 | async-start | bytes 2949120 | tf_op jit(solution)/shard_map/all_gather | solution.py:258
  943.5 185.5 %all-gather.47.cloned.1.call-start = ((), (), s32[]{:S(2)}) async-start(), calls=%async_computation.16 | async-start | bytes 3538944 | tf_op jit(solution)/shard_map/all_gather | solution.py:44
  963.1 95.2 %copy-start.62 = (f32[1024,24]{0,1:T(8,128)}, f32[1024,24]{0,1:T(8,128)S(1)}, u32[]{:S(2)}) copy-start(f32[1024,24]{0,1:T(8,128)S(1)} %fusion.296) | copy-start | bytes 294916
  1066.7 672.8 %all-gather.49.cloned.1.call-start = ((), (), s32[]{:S(2)}) async-start(), calls=%async_computation.17 | async-start | bytes 3538944 | tf_op jit(solution)/shard_map/all_gather | solution.py:44
  1200.6 41.0 %copy-start.87 = (f32[24]{0:T(128)S(1)}, f32[24]{0:T(128)}, u32[]{:S(2)}) copy-start(f32[24]{0:T(128)} %copy-done.86) | copy-start | bytes 292 | tf_op jit(solution)/shard_map/transpose(jvp())/while
  1200.6 41.0 %copy-start.2 = (f32[24,64,128]{2,1,0:T(8,128)S(1)}, f32[24,64,128]{2,1,0:T(8,128)}, u32[]{:S(2)}) copy-start(f32[24,64,128]{2,1,0:T(8,128)} %get-tuple-element.2803) | copy-start | bytes 2359300 | tf_op jit(solution)/shard_map/transpose(jvp())/while
  1297.8 41.0 %copy-start.87 = (f32[24]{0:T(128)S(1)}, f32[24]{0:T(128)}, u32[]{:S(2)}) copy-start(f32[24]{0:T(128)} %copy-done.86) | copy-start | bytes 292 | tf_op jit(solution)/shard_map/transpose(jvp())/while
  1297.8 41.0 %copy-start.2 = (f32[24,64,128]{2,1,0:T(8,128)S(1)}, f32[24,64,128]{2,1,0:T(8,128)}, u32[]{:S(2)}) copy-start(f32[24,64,128]{2,1,0:T(8,128)} %get-tuple-element.2803) | copy-start | bytes 2359300 | tf_op jit(solution)/shard_map/transpose(jvp())/while
  1492.2 41.0 %copy-start.87 = (f32[24]{0:T(128)S(1)}, f32[24]{0:T(128)}, u32[]{:S(2)}) copy-start(f32[24]{0:T(128)} %copy-done.86) | copy-start | bytes 292 | tf_op jit(solution)/shard_map/transpose(jvp())/while
  1492.2 41.0 %copy-start.2 = (f32[24,64,128]{2,1,0:T(8,128)S(1)}, f32[24,64,128]{2,1,0:T(8,128)}, u32[]{:S(2)}) copy-start(f32[24,64,128]{2,1,0:T(8,128)} %get-tuple-element.2803) | copy-start | bytes 2359300 | tf_op jit(solution)/shard_map/transpose(jvp())/while
  1601.9 12.3 collective-permute-start.3
  1664.5 592.0 %reduce-scatter.21.cloned.1.call-start = ((), (), s32[]{:S(2)}) async-start(), calls=%async_computation.19 | async-start | bytes 573440
  1665.7 621.6 %reduce-scatter.17.cloned.1.call-start = ((), (), s32[]{:S(2)}) async-start(), calls=%async_computation.9 | async-start | bytes 2949120 | tf_op jit(solution)/shard_map/reduce_scatter | solution.py:447
  1673.6 613.8 %reduce-scatter.15.cloned.1.call-start = ((), (), s32[]{:S(2)}) async-start(), calls=%async_computation.8 | async-start | bytes 2949120 | tf_op jit(solution)/shard_map/reduce_scatter | solution.py:447
  1680.5 606.9 %reduce-scatter.13.cloned.1.call-start = ((), (), s32[]{:S(2)}) async-start(), calls=%async_computation.7 | async-start | bytes 6635520 | tf_op jit(solution)/shard_map/reduce_scatter | solution.py:444
  1739.4 597.7 %reduce-scatter.11.cloned.1.call-start = ((), (), s32[]{:S(2)}) async-start(), calls=%async_computation.6 | async-start | bytes 6635520 | tf_op jit(solution)/shard_map/reduce_scatter | solution.py:444
  1811.3 41.1 %copy-start.89 = (f32[24]{0:T(128)S(1)}, f32[24]{0:T(128)}, u32[]{:S(2)}) copy-start(f32[24]{0:T(128)} %copy-done.88) | copy-start | bytes 292 | tf_op jit(solution)/shard_map/transpose(jvp())/while
  1811.3 41.1 %copy-start.6 = (f32[24,64,128]{2,1,0:T(8,128)S(1)}, f32[24,64,128]{2,1,0:T(8,128)}, u32[]{:S(2)}) copy-start(f32[24,64,128]{2,1,0:T(8,128)} %get-tuple-element.2848) | copy-start | bytes 2359300 | tf_op jit(solution)/shard_map/transpose(jvp())/while
  2203.1 20.1 collective-permute-start.4
  2243.2 116.3 %reduce-scatter.19.cloned.1.call-start = ((), (), s32[]{:S(2)}) async-start(), calls=%async_computation.18 | async-start | bytes 573440
  2258.8 182.6 %all-reduce.59.cloned.1.call-start = ((), (), s32[]{:S(2)}) async-start(), calls=%async_computation.20 | async-start | bytes 7667712 | tf_op jit(solution)/shard_map/psum | solution.py:473
  (268 other events, 3598.3 us)
Sparse Core Ops, SparseCore 0:
  10.9 116.3 all-gather.34
  437.4 42.8 all-gather.36
  481.9 50.0 all-gather.38
  534.0 98.1 all-gather.40
  943.1 43.1 all-gather.42
  987.6 49.9 all-gather.44
  1066.8 31.6 all-gather.46
  1664.7 29.0 all-gather.48
  1696.1 19.2 reduce-scatter.20
  1718.2 47.5 reduce-scatter.16
  1768.3 47.5 reduce-scatter.14
  1818.8 94.4 reduce-scatter.12
  2243.4 93.7 reduce-scatter.10
  2339.4 20.1 reduce-scatter.18
  2363.2 78.1 all-reduce.58
where the time goes:
time: 2480 us; the launch traced here: 2460 us
  local copies, waits for them, and re-layouts  1030 us (42%)
  matrix products  533 us (21%)
  other arithmetic  476 us (19%)
  waiting for transfers between devices  174 us (7%)
  blocking collectives  172 us (7%)
  loops' own time  26.3 us (1%)
    dynamic_update_slice x40, local copies, waits for them, and re-layouts, device_pass(): lax.scan(jax.checkpoint(one_block), zero_state, (starts, to_blocks(channe...  595 us
    dot_general x24, matrix products, group_math(): jnp.einsum('hij,jhp->ihp', mixing, channel_group_source, precision=highest)  202 us
    another operation x82, other arithmetic  107 us
    unnamed x5, blocking collectives  80.1 us
    unnamed x398, local copies, waits for them, and re-layouts  76.9 us
    dot_general x32, matrix products, group_math(): jnp.einsum('in,hpn->ihp', leaving_memory, prior_state, precision=highest)  76.7 us
    slice x2, local copies, waits for them, and re-layouts, conv_mix(): filter_kernel_entry[offset] * extended[offset:offset + row_count] * same_doc  74.4 us
    dot_general x24, matrix products, group_math(): jnp.einsum('hj,jhp,jn->hpn', tail_gain, channel_group_source, arriving_me...  66.3 us
  transfers between devices with their start and end apart: 20, of which 7 were waited for; matrix products, arithmetic and copies ran while one was open for 36% of the time, Pallas kernels for 0%

commit v1 on v0

v1 whole, which is shorter than its diff:
```python
import jax
import jax.numpy as jnp
import numpy as np
from jax import lax
from jax.experimental import pallas as pl
from jax.experimental.pallas import tpu as pltpu
from jax.sharding import PartitionSpec as P

D = 768
H = 24
P_SIZE = 64
N = 128
K = 4
E = 1536
CV = 1792
CX = CV + 128
Q = 128
TT = 256
SUB = TT // Q
W = 256
HP = 32
PAIRS = H // 2
eps = 1e-05
LOG2E = 1.4426950408889634
BIG = -1e30
CUT = 30000.0
f32 = jnp.float32
bf16 = jnp.bfloat16
highest = lax.Precision.HIGHEST
VMEM_LIMIT = 56 * 1024 * 1024


def nn(a, b):
    return lax.dot_general(a, b, (((1,), (0,)), ((), ())), preferred_element_type=f32)


def nt(a, b):
    return lax.dot_general(a, b, (((1,), (1,)), ((), ())), preferred_element_type=f32)


def tn(a, b):
    return lax.dot_general(a, b, (((0,), (0,)), ((), ())), preferred_element_type=f32)


def nn_exact(a, b):
    return lax.dot_general(
        a, b, (((1,), (0,)), ((), ())), precision=highest, preferred_element_type=f32
    )


def halves(v):
    hi = v.astype(bf16)
    lo = (v - hi.astype(f32)).astype(bf16)
    return jnp.concatenate([hi, lo], axis=1)


def sigmoid(v):
    return 0.5 + 0.5 * jnp.tanh(0.5 * v)


def softplus(v):
    return jnp.maximum(v, 0.0) + jnp.log1p(jnp.exp(-jnp.abs(v)))


def iota2(shape, dim):
    return lax.broadcasted_iota(jnp.int32, shape, dim)


def lane_halves():
    lane = iota2((1, 2 * P_SIZE), 1)
    left = (lane < P_SIZE).astype(f32).astype(bf16)
    right = (lane >= P_SIZE).astype(f32).astype(bf16)
    return left, right


def full(shape):
    return pl.BlockSpec(shape, lambda i: (0,) * len(shape))


def rows(width, size=TT):
    return pl.BlockSpec((size, width), lambda i: (i, 0))


def cols(height):
    return pl.BlockSpec((height, TT), lambda i: (0, i))


def params():
    return pltpu.CompilerParams(vmem_limit_bytes=VMEM_LIMIT, dimension_semantics=("arbitrary",))


def shape(dims, dtype):
    return jax.ShapeDtypeStruct(dims, dtype)


def project_kernel(x_ref, gain_ref, w_ref, normed_ref, xc_ref, dtr_ref):
    x = x_ref[...].astype(f32)
    scale = lax.rsqrt(jnp.mean(x * x, axis=-1, keepdims=True) + eps)
    normed = (x * scale * gain_ref[...]).astype(bf16)
    normed_ref[...] = normed
    xc_ref[...] = nn(normed, w_ref[:, :CV]).astype(bf16)
    dtr_ref[...] = nn(normed, w_ref[:, CV:])


def project(x, gain, w):
    t = x.shape[0]
    return pl.pallas_call(
        project_kernel,
        grid=(t // TT,),
        in_specs=[rows(D), full((1, D)), full((D, CX))],
        out_specs=[rows(D), rows(CV), rows(128)],
        out_shape=[shape((t, D), bf16), shape((t, CV), bf16), shape((t, 128), f32)],
        compiler_params=params(),
        name="project",
    )(x, gain, w)


def gate_kernel(normed_ref, w_ref, z_ref):
    z_ref[...] = nn(normed_ref[...], w_ref[...]).astype(bf16)


def project_gate(normed, w):
    t = normed.shape[0]
    return pl.pallas_call(
        gate_kernel,
        grid=(t // TT,),
        in_specs=[rows(D), full((D, E))],
        out_specs=rows(E),
        out_shape=shape((t, E), bf16),
        compiler_params=params(),
        name="project_gate",
    )(normed, w)


def prepare_kernel(
    xc_ref, edge_ref, cw_ref, dtr_ref, spike_ref, tok_ref, pv_ref, e2_ref,
    pre_ref, x_ref, bc_ref, dt_ref, cum_ref, cumt_ref, dtt_ref, packed_ref,
    ext, state_ref, carry_ref,
):
    step = pl.program_id(0)

    @pl.when(step == 0)
    def _():
        ext[0:8, :] = edge_ref[...]
        state_ref[...] = jnp.zeros_like(state_ref)
        carry_ref[...] = jnp.zeros_like(carry_ref)

    @pl.when(step > 0)
    def _():
        ext[0:8, :] = ext[TT : TT + 8, :]

    ext[8 : TT + 8, :] = xc_ref[...].astype(f32)
    masks = [tok_ref[:, k : k + 1] for k in range(K - 1)]
    for b in range(CV // 128):
        at = slice(b * 128, (b + 1) * 128)
        total = cw_ref[K : K + 1, at] + cw_ref[K - 1 : K, at] * ext[8 : TT + 8, at]
        for k in range(K - 1):
            total = total + cw_ref[k : k + 1, at] * (ext[5 + k : 5 + k + TT, at] * masks[k])
        pre_ref[:, at] = total.astype(bf16)
        act = (total * sigmoid(total)).astype(bf16)
        if b < E // 128:
            x_ref[:, at] = act
        else:
            bc_ref[:, (b - E // 128) * 128 : (b - E // 128 + 1) * 128] = act

    dt = softplus(dtr_ref[...] + pv_ref[0:1, :])
    log_decay = (spike_ref[...] - dt * pv_ref[1:2, :]) * LOG2E
    dt_ref[...] = dt
    dtt_ref[...] = jnp.transpose(dt)[:HP, :]
    lower = (iota2((Q, Q), 0) >= iota2((Q, Q), 1)).astype(f32)
    for s in range(SUB):
        r = slice(s * Q, (s + 1) * Q)
        cum = nn_exact(lower, log_decay[r])
        cum_ref[r, :] = cum
        cumt_ref[:, r] = jnp.transpose(cum)[:HP, :]
        last = cum[Q - 1 : Q, :]
        tail = jnp.exp2(last - cum) * tok_ref[r, 7:8] * dt[r]
        kept = tok_ref[s * Q + Q - 1 : s * Q + Q, 6:7]
        carried = jnp.exp2(last) * kept
        carry_ref[...] = carry_ref[...] + (last + (kept - 1.0) * CUT)
        wide = jnp.concatenate([tail, jnp.broadcast_to(carried, (16, 128))], axis=0)
        wide = halves(wide)
        b_in = bc_ref[r, :N]
        for b in range(E // W):
            at = slice(b * W, (b + 1) * W)
            grown = nn(wide, e2_ref[:, at])
            weighted = (x_ref[r, at].astype(f32) * grown[:Q]).astype(bf16)
            state_ref[:, at] = state_ref[:, at] * grown[Q : Q + 1] + tn(b_in, weighted)

    @pl.when(step == pl.num_programs(0) - 1)
    def _():
        packed_ref[:N, :] = state_ref[...].astype(bf16)
        packed_ref[N:, :] = jnp.zeros((16, E), bf16)
        rest = jnp.concatenate([carry_ref[...], carry_ref[...]], axis=0)
        for k in range(3):
            part = rest.astype(bf16)
            packed_ref[N:, k * 128 : (k + 1) * 128] = part
            rest = rest - part.astype(f32)


def prepare(xc, edge, cw, dtr, spike, tok, pv, e2):
    t = xc.shape[0]
    return pl.pallas_call(
        prepare_kernel,
        grid=(t // TT,),
        in_specs=[
            rows(CV), full((8, CV)), full((8, CV)), rows(128), rows(128), rows(128),
            full((8, 128)), full((256, E)),
        ],
        out_specs=[
            rows(CV), rows(E), rows(2 * N), rows(128), rows(128), cols(HP), cols(HP),
            full((N + 16, E)),
        ],
        out_shape=[
            shape((t, CV), bf16),
            shape((t, E), bf16),
            shape((t, 2 * N), bf16),
            shape((t, 128), f32),
            shape((t, 128), f32),
            shape((HP, t), f32),
            shape((HP, t), f32),
            shape((N + 16, E), bf16),
        ],
        scratch_shapes=[
            pltpu.VMEM((TT + 8, CV), f32),
            pltpu.VMEM((N, E), f32),
            pltpu.VMEM((8, 128), f32),
        ],
        compiler_params=params(),
        name="prepare",
    )(xc, edge, cw, dtr, spike, tok, pv, e2)


def within_kernel(x_ref, bc_ref, cum_ref, cumt_ref, dtt_ref, tok_ref, doct_ref, y_ref):
    left, right = lane_halves()
    order = iota2((Q, Q), 0) >= iota2((Q, Q), 1)
    for s in range(SUB):
        r = slice(s * Q, (s + 1) * Q)
        same = tok_ref[r, 8:9] == doct_ref[0:1, r]
        bias = jnp.where(order & same, 0.0, BIG)
        scores = nt(bc_ref[r, N:], bc_ref[r, :N])
        cum = cum_ref[r, :]
        for p in range(PAIRS):
            at = slice(p * 128, (p + 1) * 128)
            xp = x_ref[r, at]
            mixes = []
            for h in (2 * p, 2 * p + 1):
                gap = (cum[:, h : h + 1] - cumt_ref[h : h + 1, r]) + bias
                mixes.append((jnp.exp2(gap) * (scores * dtt_ref[h : h + 1, r])).astype(bf16))
            both = jnp.concatenate([xp * left, xp * right], axis=0)
            y_ref[r, at] = nn(jnp.concatenate(mixes, axis=1), both).astype(bf16)


def within(x, bc, cum, cumt, dtt, tok, doct):
    t = x.shape[0]
    return pl.pallas_call(
        within_kernel,
        grid=(t // TT,),
        in_specs=[rows(E), rows(2 * N), rows(128), cols(HP), cols(HP), rows(128), cols(8)],
        out_specs=rows(E),
        out_shape=shape((t, E), bf16),
        compiler_params=params(),
        name="within",
    )(x, bc, cum, cumt, dtt, tok, doct)


def across_kernel(
    yi_ref, x_ref, bc_ref, dt_ref, cum_ref, tok_ref, z_ref, first_ref, skip_ref, gain_ref,
    w_ref, res_ref, e2_ref,
    y_ref, low_ref, new_ref, prior_ref,
    state, gated,
):
    step = pl.program_id(0)

    @pl.when(step == 0)
    def _():
        state[...] = first_ref[...]

    for s in range(SUB):
        r = slice(s * Q, (s + 1) * Q)
        cum = cum_ref[r, :]
        last = cum[Q - 1 : Q, :]
        tail = jnp.exp2(last - cum) * tok_ref[r, 7:8] * dt_ref[r, :]
        head = jnp.exp2(cum) * tok_ref[r, 6:7]
        carried = head[Q - 1 : Q, :]
        wide = halves(
            jnp.concatenate([tail, head, jnp.broadcast_to(carried, (16, 128))], axis=0)
        )
        b_in = bc_ref[r, :N]
        c_out = bc_ref[r, N:]
        square = jnp.zeros((Q, W), f32)
        for b in range(E // W):
            at = slice(b * W, (b + 1) * W)
            grown = nn(wide, e2_ref[:, at])
            xs = x_ref[r, at].astype(f32)
            held = state[:, at]
            prior_ref[s, :, at] = held.astype(bf16)
            y = (
                yi_ref[r, at].astype(f32)
                + nn(c_out, held.astype(bf16)) * grown[Q : 2 * Q]
                + skip_ref[0:1, at] * xs
            )
            y_ref[r, at] = y.astype(bf16)
            z = z_ref[r, at].astype(f32)
            made = y * (z * sigmoid(z))
            gated[r, at] = made
            square = square + made * made
            weighted = (xs * grown[:Q]).astype(bf16)
            state[:, at] = held * grown[2 * Q : 2 * Q + 1] + tn(b_in, weighted)
        scale = lax.rsqrt(jnp.sum(square, axis=-1, keepdims=True) * (1.0 / E) + eps)
        for b in range(E // W):
            at = slice(b * W, (b + 1) * W)
            low_ref[r, at] = (gated[r, at] * scale * gain_ref[0:1, at]).astype(bf16)
    new = res_ref[...].astype(f32) + nn(low_ref[...], w_ref[...])
    new_ref[...] = new.astype(new_ref.dtype)


def across(yi, x, bc, dt, cum, tok, z, first, skip, gain, w, res, e2, out_type):
    t = x.shape[0]
    return pl.pallas_call(
        across_kernel,
        grid=(t // TT,),
        in_specs=[
            rows(E), rows(E), rows(2 * N), rows(128), rows(128), rows(128), rows(E),
            full((N, E)), full((1, E)), full((1, E)), full((E, D)), rows(D), full((256, E)),
        ],
        out_specs=[rows(E), rows(E), rows(D), pl.BlockSpec((SUB, N, E), lambda i: (i, 0, 0))],
        out_shape=[
            shape((t, E), bf16),
            shape((t, E), bf16),
            shape((t, D), out_type),
            shape((t // Q, N, E), bf16),
        ],
        scratch_shapes=[pltpu.VMEM((N, E), f32), pltpu.VMEM((TT, E), f32)],
        compiler_params=params(),
        name="across",
    )(yi, x, bc, dt, cum, tok, z, first, skip, gain, w, res, e2)


def open_back_kernel(
    g_ref, w_ref, y_ref, z_ref, x_ref, bc_ref, cum_ref, tok_ref, gain_ref, e2_ref,
    dy_ref, dz_ref, gb_ref, acc_ref, low_ref,
    held, state_ref,
):
    step = pl.program_id(0)

    @pl.when(step == 0)
    def _():
        acc_ref[...] = jnp.zeros_like(acc_ref)
        state_ref[...] = jnp.zeros_like(state_ref)

    gb = g_ref[...].astype(bf16)
    gb_ref[...] = gb
    held[...] = nt(gb, w_ref[...])
    for s in reversed(range(SUB)):
        r = slice(s * Q, (s + 1) * Q)
        square = jnp.zeros((Q, W), f32)
        cross = jnp.zeros((Q, W), f32)
        for b in range(E // W):
            at = slice(b * W, (b + 1) * W)
            z = z_ref[r, at].astype(f32)
            gated = y_ref[r, at].astype(f32) * (z * sigmoid(z))
            square = square + gated * gated
            cross = cross + gated * (held[r, at] * gain_ref[0:1, at])
        scale = lax.rsqrt(jnp.sum(square, axis=-1, keepdims=True) * (1.0 / E) + eps)
        pull = (scale * scale * scale) * (jnp.sum(cross, axis=-1, keepdims=True) * (1.0 / E))
        cum = cum_ref[r, :]
        head = jnp.exp2(cum) * tok_ref[r, 6:7]
        wide = halves(
            jnp.concatenate([head, jnp.broadcast_to(head[Q - 1 : Q, :], (16, 128))], axis=0)
        )
        c_out = bc_ref[r, N:]
        for b in range(E // W):
            at = slice(b * W, (b + 1) * W)
            z = z_ref[r, at].astype(f32)
            gate = sigmoid(z)
            y = y_ref[r, at].astype(f32)
            gated = y * (z * gate)
            dn = held[r, at]
            acc_ref[0:1, at] += jnp.sum(dn * (gated * scale), axis=0, keepdims=True)
            dgated = scale * (dn * gain_ref[0:1, at]) - gated * pull
            dy = dgated * (z * gate)
            dz_ref[r, at] = (dgated * y * (gate * (1.0 + z * (1.0 - gate)))).astype(bf16)
            acc_ref[1:2, at] += jnp.sum(dy * x_ref[r, at].astype(f32), axis=0, keepdims=True)
            dy_ref[r, at] = dy.astype(bf16)
            grown = nn(wide, e2_ref[:, at])
            state_ref[:, at] = state_ref[:, at] * grown[Q : Q + 1] + tn(
                c_out, (dy * grown[:Q]).astype(bf16)
            )

    @pl.when(step == pl.num_programs(0) - 1)
    def _():
        low_ref[...] = state_ref[...].astype(bf16)


def open_back(g, w, y, z, x, bc, cum, tok, gain, e2):
    t = x.shape[0]
    n = t // TT

    def turned(width):
        return pl.BlockSpec((TT, width), lambda i: (n - 1 - i, 0))

    return pl.pallas_call(
        open_back_kernel,
        grid=(n,),
        in_specs=[
            turned(D), full((E, D)), turned(E), turned(E), turned(E), turned(2 * N),
            turned(128), turned(128), full((1, E)), full((256, E)),
        ],
        out_specs=[turned(E), turned(E), turned(D), full((8, E)), full((N, E))],
        out_shape=[
            shape((t, E), bf16),
            shape((t, E), bf16),
            shape((t, D), bf16),
            shape((8, E), f32),
            shape((N, E), bf16),
        ],
        scratch_shapes=[pltpu.VMEM((TT, E), f32), pltpu.VMEM((N, E), f32)],
        compiler_params=params(),
        name="open_back",
    )(g, w, y, z, x, bc, cum, tok, gain, e2)


def within_back_kernel(
    x_ref, dy_ref, bc_ref, dt_ref, cum_ref, cumt_ref, tok_ref, doct_ref, hot_ref, sel_ref,
    dxdt_ref, dbc_ref, cross_ref,
):
    left, right = lane_halves()
    order = iota2((Q, Q), 1) >= iota2((Q, Q), 0)
    suffix = order.astype(f32)
    for s in range(SUB):
        r = slice(s * Q, (s + 1) * Q)
        same = tok_ref[r, 8:9] == doct_ref[0:1, r]
        bias = jnp.where(order & same, 0.0, BIG)
        b_in = bc_ref[r, :N]
        c_out = bc_ref[r, N:]
        scores = nt(b_in, c_out)
        cum = cum_ref[r, :]
        dt = dt_ref[r, :]
        grad_scores = jnp.zeros((Q, Q), f32)
        by_source = jnp.zeros((Q, 128), f32)
        by_target = jnp.zeros((HP, Q), f32)
        for p in range(PAIRS):
            at = slice(p * 128, (p + 1) * 128)
            xp = x_ref[r, at]
            dyp = dy_ref[r, at]
            dmix = nt(jnp.concatenate([xp * left, xp * right], axis=0), dyp)
            mixes = []
            flows = []
            for i in range(2):
                h = 2 * p + i
                decay = jnp.exp2((cumt_ref[h : h + 1, r] - cum[:, h : h + 1]) + bias)
                mixes.append((decay * scores).astype(bf16))
                part = dmix[i * Q : (i + 1) * Q] * (decay * dt[:, h : h + 1])
                grad_scores = grad_scores + part
                flows.append((part * scores).astype(bf16))
            both = jnp.concatenate([dyp * left, dyp * right], axis=0)
            dxdt_ref[r, at] = nn(jnp.concatenate(mixes, axis=1), both).astype(bf16)
            by_source = by_source + nn(jnp.concatenate(flows, axis=1), hot_ref[p])
            by_target = by_target + nn(sel_ref[p], jnp.concatenate(flows, axis=0))
        low = grad_scores.astype(bf16)
        dbc_ref[r, :N] = nn(low, c_out)
        dbc_ref[r, N:] = tn(low, b_in)
        target = jnp.transpose(
            jnp.concatenate([by_target, jnp.zeros((128 - HP, Q), f32)], axis=0)
        )
        cross_ref[r, :] = nn_exact(suffix, target - by_source)


def within_back(x, dy, bc, dt, cum, cumt, tok, doct, hot, sel):
    t = x.shape[0]
    return pl.pallas_call(
        within_back_kernel,
        grid=(t // TT,),
        in_specs=[
            rows(E), rows(E), rows(2 * N), rows(128), rows(128), cols(HP), rows(128), cols(8),
            full(hot.shape), full(sel.shape),
        ],
        out_specs=[rows(E), rows(2 * N), rows(128)],
        out_shape=[shape((t, E), bf16), shape((t, 2 * N), f32), shape((t, 128), f32)],
        compiler_params=params(),
        name="within_back",
    )(x, dy, bc, dt, cum, cumt, tok, doct, hot, sel)


def across_back_kernel(
    x_ref, pre_ref, xc_ref, halo_ref, edge_ref, bc_ref, dy_ref, dxdt_ref, dbc_ref, cross_ref,
    dt_ref, cum_ref, dtr_ref, tok_ref, prior_ref, last_ref, skip_ref, cw_ref, pv_ref, e2_ref,
    et_ref,
    dxc_ref, cacc_ref, hacc_ref, first_ref,
    state, dp, ext,
):
    step = pl.program_id(0)
    count = pl.num_programs(0)

    @pl.when(step == 0)
    def _():
        state[...] = last_ref[...]
        cacc_ref[...] = jnp.zeros_like(cacc_ref)
        hacc_ref[...] = jnp.zeros_like(hacc_ref)
        dp[TT : TT + 8, :] = jnp.zeros((8, CV), f32)

    @pl.when(step > 0)
    def _():
        dp[TT : TT + 8, :] = dp[0:8, :]

    @pl.when(step == count - 1)
    def _():
        ext[0:8, :] = edge_ref[...]

    @pl.when(step < count - 1)
    def _():
        ext[0:8, :] = halo_ref[...].astype(f32)[8:16, :]

    def through_silu(grad, r, at):
        v = pre_ref[r, at].astype(f32)
        gate = sigmoid(v)
        dp[r, at] = grad * (gate * (1.0 + v * (1.0 - gate)))

    strict = (iota2((Q, Q), 0) > iota2((Q, Q), 1)).astype(f32)
    suffix = (iota2((Q, Q), 0) <= iota2((Q, Q), 1)).astype(f32)
    rate = pv_ref[1:2, :]
    for s in reversed(range(SUB)):
        r = slice(s * Q, (s + 1) * Q)
        cum = cum_ref[r, :]
        dt = dt_ref[r, :]
        last = cum[Q - 1 : Q, :]
        tail = jnp.exp2(last - cum) * tok_ref[r, 7:8]
        head = jnp.exp2(cum) * tok_ref[r, 6:7]
        carried = head[Q - 1 : Q, :]
        wide = halves(
            jnp.concatenate([tail, head, dt, jnp.broadcast_to(carried, (16, 128))], axis=0)
        )
        b_in = bc_ref[r, :N]
        c_out = bc_ref[r, N:]
        grad_b = dbc_ref[r, :N]
        grad_c = dbc_ref[r, N:]
        sums = jnp.zeros((3 * Q + 16, 128), f32)
        for b in range(E // W):
            at = slice(b * W, (b + 1) * W)
            grown = nn(wide, e2_ref[:, at])
            dt_wide = grown[2 * Q : 3 * Q]
            after = state[:, at]
            after_low = after.astype(bf16)
            before = prior_ref[s, :, at]
            xs = x_ref[r, at].astype(f32)
            dy = dy_ref[r, at].astype(f32)
            reach = nn(b_in, after_low) * grown[:Q]
            read = nn(c_out, before)
            dxdt = dxdt_ref[r, at].astype(f32) + reach
            dyg = dy * grown[Q : 2 * Q]
            dyg_low = dyg.astype(bf16)
            joint = jnp.sum(after * before.astype(f32), axis=0, keepdims=True)
            stacked = jnp.concatenate(
                [
                    (xs * dxdt).astype(bf16),
                    (xs * reach).astype(bf16),
                    (dyg * read).astype(bf16),
                    jnp.broadcast_to(joint, (16, W)).astype(bf16),
                ],
                axis=0,
            )
            sums = sums + nn(stacked, et_ref[at, :])
            through_silu(dxdt * dt_wide + skip_ref[0:1, at] * dy, r, at)
            grad_c = grad_c + nt(dyg_low, before)
            grad_b = grad_b + nt((xs * (grown[:Q] * dt_wide)).astype(bf16), after_low)
            state[:, at] = after * grown[3 * Q : 3 * Q + 1] + tn(c_out, dyg_low)
        through_silu(grad_b, r, slice(E, E + N))
        through_silu(grad_c, r, slice(E + N, CV))
        dlog = (
            cross_ref[r, :]
            + nn_exact(strict, sums[Q : 2 * Q] * dt)
            + nn_exact(suffix, sums[2 * Q : 3 * Q])
            + carried * sums[3 * Q : 3 * Q + 1]
        )
        draw = (sums[:Q] - rate * dlog) * sigmoid(dtr_ref[r, :] + pv_ref[0:1, :])
        dxc_ref[r, CV:] = draw.astype(bf16)
        hacc_ref[0:1, :] += jnp.sum(draw, axis=0, keepdims=True)
        hacc_ref[1:2, :] -= rate * jnp.sum(dt * dlog, axis=0, keepdims=True)

    ext[8 : TT + 8, :] = xc_ref[...].astype(f32)
    masks = [tok_ref[:, k : k + 1] for k in range(K - 1)]
    ahead = [tok_ref[:, 3 + k : 4 + k] for k in range(K - 1)]
    for b in range(CV // 128):
        at = slice(b * 128, (b + 1) * 128)
        own = dp[0:TT, at]
        total = cw_ref[K - 1 : K, at] * own
        cacc_ref[K : K + 1, at] += jnp.sum(own, axis=0, keepdims=True)
        cacc_ref[K - 1 : K, at] += jnp.sum(own * ext[8 : TT + 8, at], axis=0, keepdims=True)
        for k in range(K - 1):
            total = total + cw_ref[k : k + 1, at] * (dp[3 - k : 3 - k + TT, at] * ahead[k])
            cacc_ref[k : k + 1, at] += jnp.sum(
                own * (ext[5 + k : 5 + k + TT, at] * masks[k]), axis=0, keepdims=True
            )
        dxc_ref[:, at] = total.astype(bf16)

    @pl.when(step == count - 1)
    def _():
        first_ref[...] = dp[0:8, :]


def across_back(
    x, pre, xc, edge, bc, dy, dxdt, dbc, cross, dt, cum, dtr, tok, prior, last, skip, cw, pv, e2,
    et,
):
    t = x.shape[0]
    n = t // TT

    def turned(width):
        return pl.BlockSpec((TT, width), lambda i: (n - 1 - i, 0))

    halo = pl.BlockSpec((16, CV), lambda i: (jnp.maximum((n - 1 - i) * (TT // 16) - 1, 0), 0))
    return pl.pallas_call(
        across_back_kernel,
        grid=(n,),
        in_specs=[
            turned(E), turned(CV), turned(CV), halo, full((8, CV)), turned(2 * N), turned(E),
            turned(E), turned(2 * N), turned(128), turned(128), turned(128), turned(128),
            turned(128), pl.BlockSpec((SUB, N, E), lambda i: (n - 1 - i, 0, 0)), full((N, E)),
            full((1, E)), full((8, CV)), full((8, 128)), full((256, E)), full((E, 128)),
        ],
        out_specs=[turned(CX), full((8, CV)), full((8, 128)), full((8, CV))],
        out_shape=[
            shape((t, CX), bf16),
            shape((8, CV), f32),
            shape((8, 128), f32),
            shape((8, CV), f32),
        ],
        scratch_shapes=[
            pltpu.VMEM((N, E), f32),
            pltpu.VMEM((TT + 8, CV), f32),
            pltpu.VMEM((TT + 8, CV), f32),
        ],
        compiler_params=params(),
        name="across_back",
    )(
        x, pre, xc, xc, edge, bc, dy, dxdt, dbc, cross, dt, cum, dtr, tok, prior, last, skip, cw,
        pv, e2, et,
    )


def close_back_kernel(
    dz_ref, dxc_ref, wz_ref, wx_ref, x_ref, gain_ref, g_ref, new_ref, acc_ref
):
    @pl.when(pl.program_id(0) == 0)
    def _():
        acc_ref[...] = jnp.zeros_like(acc_ref)

    dn = nt(dz_ref[...], wz_ref[...]) + nt(dxc_ref[...], wx_ref[...])
    x = x_ref[...].astype(f32)
    scale = lax.rsqrt(jnp.mean(x * x, axis=-1, keepdims=True) + eps)
    acc_ref[0:1, :] += jnp.sum(dn * (x * scale), axis=0, keepdims=True)
    pulled = dn * gain_ref[...]
    mean = jnp.mean(pulled * x, axis=-1, keepdims=True)
    new_ref[...] = g_ref[...].astype(f32) + scale * pulled - x * (scale * scale * scale * mean)


def close_back(dz, dxc, wz, wx, x, gain, g):
    t = x.shape[0]
    return pl.pallas_call(
        close_back_kernel,
        grid=(t // TT,),
        in_specs=[
            rows(E), rows(CX), full((D, E)), full((D, CX)), rows(D), full((1, D)), rows(D),
        ],
        out_specs=[rows(D), full((8, D))],
        out_shape=[shape((t, D), f32), shape((8, D), f32)],
        compiler_params=params(),
        name="close_back",
    )(dz, dxc, wz, wx, x, gain, g)


def passed_along(value, axis, steps):
    count = lax.axis_size(axis)
    first, last = (max(0, -steps), min(count, count - steps))
    return lax.ppermute(value, axis, [(source, source + steps) for source in range(first, last)])


def swapped(value, axis, bit):
    count = lax.axis_size(axis)
    return lax.ppermute(value, axis, [(source, source ^ bit) for source in range(count)])


def bits_of(axis):
    return [1 << k for k in range((lax.axis_size(axis) - 1).bit_length())]


def all_states(packed):
    bits = bits_of("seq")
    half = E // 2
    sides = [(packed[:, :half], bits[1:] + bits[:1]), (packed[:, half:], bits[:0:-1] + bits[:1])]
    held = [value[None] for value, _ in sides]
    orders = [[0], [0]]
    for k in range(len(bits)):
        for side, (_, path) in enumerate(sides):
            came = swapped(held[side], "seq", path[k])
            held[side] = jnp.concatenate([held[side], came])
            orders[side] = orders[side] + [o ^ path[k] for o in orders[side]]
    return held, orders


def decay_table(held, order):
    logs = held[:, N, :384].astype(f32).reshape(-1, 3, 128).sum(axis=1)
    count = logs.shape[0]
    place = [order.index(k) for k in range(count)]
    return jnp.stack([logs[i] for i in place])


def joined_states(held, orders, logs, forward):
    count, mine = logs.shape[0], lax.axis_index("seq")
    who = jnp.arange(count) ^ mine
    if forward:
        counts = who < mine
        between = (who[None] > who[:, None]) & (who[None] < mine)
    else:
        counts = who > mine
        between = (who[None] < who[:, None]) & (who[None] > mine)
    power = jnp.sum(jnp.where(between[:, :, None], logs[None], 0.0), axis=1)
    factor = jnp.where(counts[:, None], jnp.exp2(power), 0.0)
    factor = jnp.repeat(factor[:, :H], P_SIZE, axis=1)
    half = E // 2
    sides = []
    for side in range(2):
        total = 0.0
        for i, k in enumerate(orders[side]):
            weight = factor[k, side * half : (side + 1) * half]
            total = total + weight[None] * held[side][i, :N].astype(f32)
        sides.append(total)
    return jnp.concatenate(sides, axis=1)


def gathered(piece):
    seqs, parts = lax.axis_size("seq"), lax.axis_size("fsdp")
    height, width = piece.shape
    mine = height // seqs
    own = lax.dynamic_slice_in_dim(piece, lax.axis_index("seq") * mine, mine, 0)
    pieces = lax.all_gather(own, ("seq", "fsdp"))
    pieces = pieces.reshape(seqs, parts, mine, width).transpose(1, 0, 2, 3)
    return pieces.reshape(parts * height, width)


def reduced(value):
    seqs, parts = lax.axis_size("seq"), lax.axis_size("fsdp")
    height, width = value.shape
    value = value.astype(bf16).reshape(parts, height // parts, width)
    value = lax.psum_scatter(value, "seq", scatter_dimension=1, tiled=True)
    value = lax.psum_scatter(value, "fsdp", scatter_dimension=0, tiled=True)
    value = lax.all_gather(value, "seq", axis=1, tiled=True)
    return value[0].astype(f32)


def reduced_small(value):
    parts, mine = lax.axis_size("fsdp"), lax.axis_index("fsdp")
    bit = parts // 2
    while bit:
        value = value.reshape((2, value.shape[0] // 2) + value.shape[1:])
        upper = (mine & bit) != 0
        kept = jnp.where(upper, value[1], value[0])
        value = kept + swapped(jnp.where(upper, value[0], value[1]), "fsdp", bit)
        bit //= 2
    for bit in bits_of("seq"):
        value = value + swapped(value, "seq", bit)
    return value[0]


def pad_lanes(value):
    return jnp.pad(value, ((0, 0), (0, 128 - value.shape[1])))


def token_table(doc, edge_ids):
    t = doc.shape[0]
    widened = jnp.concatenate([edge_ids, doc, jnp.full((K - 1,), -1, doc.dtype)])
    ids = [widened[k : k + t] == doc for k in range(K - 1)]
    ids += [widened[K - 1 + (K - 1 - k) :][:t] == doc for k in range(K - 1)]
    before = widened[K - 2 : K - 2 + t].reshape(t // Q, Q)[:, :1]
    blocks = doc.reshape(t // Q, Q)
    ids.append((blocks == before).reshape(t))
    ids.append((blocks == blocks[:, Q - 1 :]).reshape(t))
    cols_in = [v.astype(f32) for v in ids] + [doc.astype(f32)]
    table = pad_lanes(jnp.stack(cols_in, axis=1))
    return table, jnp.broadcast_to(doc.astype(f32)[None], (8, t))


def constants():
    spread = np.zeros((128, E), np.float32)
    for h in range(H):
        spread[h, h * P_SIZE : (h + 1) * P_SIZE] = 1
    hot = np.zeros((PAIRS, 2 * Q, 128), np.float32)
    sel = np.zeros((PAIRS, HP, 2 * Q), np.float32)
    for p in range(PAIRS):
        for i in range(2):
            hot[p, i * Q : (i + 1) * Q, 2 * p + i] = 1
            sel[p, 2 * p + i, i * Q : (i + 1) * Q] = 1
    return tuple(
        jnp.asarray(v, bf16) for v in (np.concatenate([spread, spread]), spread.T, hot, sel)
    )


SMALL = (K * CV, CV, H, H, H, D, E)


def local(
    first_tier_source,
    token_articles,
    extra_spikes,
    upstream_gradient,
    entering_projection,
    exit_projection,
    filter_kernels,
    filter_shifts,
    stride_shifts,
    log_shrink_rates,
    bypass_coefficient,
    entry_scaling_gains,
    gated_scaling_gains,
):
    current = first_tier_source[0]
    doc = token_articles[0]
    spike = pad_lanes(extra_spikes[0])
    t = doc.shape[0]
    layers = entering_projection.shape[0]
    parts = lax.axis_size("fsdp")
    e2, et, hot, sel = constants()
    edge_ids = passed_along(doc[t - (K - 1) :], "seq", 1)
    tok, doct = token_table(doc, edge_ids)

    small = (
        filter_kernels, filter_shifts, stride_shifts, log_shrink_rates, bypass_coefficient,
        entry_scaling_gains, gated_scaling_gains,
    )
    flat = jnp.concatenate([v.reshape(layers, -1) for v in small], axis=1)
    flat = lax.all_gather(flat, "fsdp").astype(f32)

    def small_of(layer):
        found, at = [], 0
        for size in SMALL:
            width = size // parts
            found.append(flat[:, layer, at : at + width])
            at += width
        taps = found[0].reshape(parts, K, CV // parts).transpose(1, 0, 2).reshape(K, CV)
        return [taps] + [v.reshape(-1) for v in found[1:]]

    weights = [
        (
            gathered(jnp.pad(entering_projection[i][:, E:], ((0, 0), (0, 128 - H)))),
            gathered(entering_projection[i][:, :E]),
            gathered(exit_projection[i]),
        )
        for i in range(layers)
    ]
    kept = []
    for i in range(layers):
        wx, wz, w_out = weights[i]
        taps, shifts, strides, rates, bypass, gain_in, gain_out = small_of(i)
        cw = jnp.concatenate([taps, shifts[None], jnp.zeros((3, CV), f32)])
        pv = jnp.concatenate(
            [pad_lanes(jnp.stack([strides, jnp.exp(rates)])), jnp.zeros((6, 128), f32)]
        )
        skip = jnp.repeat(bypass, P_SIZE)[None]
        gain_in, gain_out = gain_in[None], gain_out[None]
        normed, xc, dtr = project(current, gain_in, wx)
        edge = passed_along(xc[t - (K - 1) :], "seq", 1).astype(f32)
        edge = jnp.concatenate([jnp.zeros((8 - (K - 1), CV), f32), edge])
        pre, x, bc, dt, cum, cumt, dtt, packed = prepare(xc, edge, cw, dtr, spike, tok, pv, e2)
        held, orders = all_states(packed)
        yi = within(x, bc, cum, cumt, dtt, tok, doct)
        z = project_gate(normed, wz)
        logs = decay_table(held[0], orders[0])
        incoming = joined_states(held, orders, logs, True)
        out_type = bf16 if i == layers - 1 else f32
        y, low, new, prior = across(
            yi, x, bc, dt, cum, tok, z, incoming, skip, gain_out, w_out, current, e2, out_type
        )
        kept.append(
            (current, normed, z, xc, dtr, edge, pre, x, bc, dt, cum, cumt, logs, y, low, prior,
             cw, pv, skip, gain_in, gain_out)
        )
        current = new
    grad = upstream_gradient[0]
    results = [None] * layers
    for i in reversed(range(layers)):
        wx, wz, w_out = weights[i]
        (source, normed, z, xc, dtr, edge, pre, x, bc, dt, cum, cumt, logs, y, low, prior,
         cw, pv, skip, gain_in, gain_out) = kept[i]
        dy, dz, gb, acc, state = open_back(
            grad, w_out, y, z, x, bc, cum, tok, gain_out, e2
        )
        held, orders = all_states(state)
        grad_out = reduced(tn(low, gb))
        grad_gate = reduced(tn(normed, dz))
        dxdt, dbc, cross = within_back(x, dy, bc, dt, cum, cumt, tok, doct, hot, sel)
        later = joined_states(held, orders, logs, False)
        dxc, cacc, hacc, first = across_back(
            x, pre, xc, edge, bc, dy, dxdt, dbc, cross, dt, cum, dtr, tok, prior, later, skip, cw,
            pv, e2, et,
        )
        masked = [first[: K - 1] * tok[: K - 1, k : k + 1] for k in range(K - 1)]
        borrowed = jnp.stack(
            [sum(cw[k] * masked[k][e - k] for k in range(e + 1)) for e in range(K - 1)]
        )
        back = passed_along(borrowed, "seq", -1)
        mended = (dxc[t - (K - 1) :, :CV].astype(f32) + back).astype(bf16)
        dxc = dxc.at[t - (K - 1) :, :CV].set(mended)
        grad_conv = reduced(tn(normed, dxc))
        grad, nacc = close_back(dz, dxc, wz, wx, source, gain_in, grad)
        big = (jnp.concatenate([grad_gate, grad_conv[:, : CV + H]], axis=1), grad_out)
        tiny = [
            cacc[:K], cacc[K], hacc[0, :H], hacc[1, :H],
            jnp.sum(acc[1].reshape(H, P_SIZE), axis=1), nacc[0], acc[0],
        ]
        results[i] = (big, tiny)
    packed = []
    for i in range(layers):
        tiny = results[i][1]
        taps = tiny[0].reshape(K, parts, CV // parts).transpose(1, 0, 2).reshape(parts, -1)
        packed.append(jnp.concatenate([taps] + [v.reshape(parts, -1) for v in tiny[1:]], axis=1))
    mine = reduced_small(jnp.stack(packed, axis=1))
    smalls, at = [], 0
    for size in SMALL:
        width = size // parts
        smalls.append(mine[:, at : at + width])
        at += width
    smalls[0] = smalls[0].reshape(layers, K, CV // parts)
    bigs = [jnp.stack([results[i][0][j] for i in range(layers)]) for j in range(2)]
    return (current[None], grad[None], *bigs, *smalls)


def solution(mesh):
    placed = (
        P("fsdp", "seq", None),
        P("fsdp", "seq"),
        P("fsdp", "seq", None),
        P("fsdp", "seq", None),
        P(None, "fsdp", None),
        P(None, "fsdp", None),
        P(None, None, "fsdp"),
        P(None, "fsdp"),
        P(None, "fsdp"),
        P(None, "fsdp"),
        P(None, "fsdp"),
        P(None, "fsdp"),
        P(None, "fsdp"),
    )
    return jax.shard_map(
        local,
        mesh=mesh,
        in_specs=placed,
        out_specs=(
            P("fsdp", "seq", None),
            P("fsdp", "seq", None),
            P(None, "fsdp", None),
            P(None, "fsdp", None),
            P(None, None, "fsdp"),
            P(None, "fsdp"),
            P(None, "fsdp"),
            P(None, "fsdp"),
            P(None, "fsdp"),
            P(None, "fsdp"),
            P(None, "fsdp"),
        ),
        check_vma=False,
    )
```

time: 2480 us -> 935 us (0.38)
  local copies, waits for them, and re-layouts: 1030 us -> 88.9 us
  matrix products: 533 us -> 30.1 us
  other arithmetic: 476 us -> 34.7 us
  Pallas kernels: 0 us -> 280 us
  waiting for transfers between devices: 174 us -> 337 us
  blocking collectives: 172 us -> 86.3 us
  starting transfers between devices: 18.9 us -> 53.1 us
  loops' own time: 26.3 us -> 0 us
    dynamic_update_slice x40 -> x0, local copies, waits for them, and re-layouts: 595 us -> none  [device_pass(): lax.scan(jax.checkpoint(one_block), zero_state, (starts, to_blocks(channe...]
    dot_general x130 -> x6, matrix products: 533 us -> 30.1 us  [tn(): lax.dot_general(a, b, (((0,), (0,)), ((), ())), preferred_element_type=f32)]
    pallas_call x0 -> x18, Pallas kernels: none -> 280 us  [the longest x2 63.1 us: across_back(): pl.pallas_call(across_back_kernel, grid=(n,), in_specs=[turned(E), turned...]
    all_gather x8 -> x6, waiting for transfers between devices: 55.7 us -> 171 us  [gathered(): pieces = lax.all_gather(own, ('seq', 'fsdp'))]
    another operation x91 -> x9, other arithmetic: 118 us -> 4.62 us  [the longest x4 4.47 us: local(): jnp.stack([results[i][0][j] for i in range(layers)])]
    slice x46 -> x41, local copies, waits for them, and re-layouts: 125 us -> 14.8 us  [the longest x5 2.54 us: local(): smalls.append(mine[:, at:at + width])]
    reduce_sum x33 -> x6, other arithmetic: 101 us -> 2.3 us  [the longest x2 2.06 us: joined_states(): power = jnp.sum(jnp.where(between[:, :, None], logs[None], 0.0), axis=1)]
    mul x64 -> x2, other arithmetic: 85.7 us -> 1.8 us  [local(): masked = [first[:K - 1] * tok[:K - 1, k:k + 1] for k in range(K - 1)]]
  transfers between devices with their start and end apart: 20 -> 52, of which waited for: 7 -> 29; matrix products, arithmetic and copies ran while one was open for 36% -> 15% of each run, Pallas kernels for 0% -> 26%
where the time goes in v1:
time: 935 us; the launch traced here: 926 us
  waiting for transfers between devices  337 us (36%)
  Pallas kernels  280 us (30%)
  local copies, waits for them, and re-layouts  88.9 us (10%)
  blocking collectives  86.3 us (9%)
  starting transfers between devices  53.1 us (6%)
  other arithmetic  34.7 us (4%)
  matrix products  30.1 us (3%)
  between operations  15.7 us (2%)
    all_gather x6, waiting for transfers between devices, gathered(): pieces = lax.all_gather(own, ('seq', 'fsdp'))  171 us
    ppermute x29, waiting for transfers between devices, swapped(): lax.ppermute(value, axis, [(source, source ^ bit) for source in range(cou...  75.5 us
    all_gather x6, blocking collectives, reduced(): value = lax.all_gather(value, 'seq', axis=1, tiled=True)  75.5 us
    pallas_call x2, Pallas kernels, across_back(): pl.pallas_call(across_back_kernel, grid=(n,), in_specs=[turned(E), turned...  63.1 us
    unnamed x24, waiting for transfers between devices  51.6 us
    pallas_call x2, Pallas kernels, within_back(): pl.pallas_call(within_back_kernel, grid=(t // TT,), in_specs=[rows(E), ro...  46.6 us
    pallas_call x2, Pallas kernels, open_back(): pl.pallas_call(open_back_kernel, grid=(n,), in_specs=[turned(D), full((E,...  39.9 us
    ppermute x29, starting transfers between devices, swapped(): lax.ppermute(value, axis, [(source, source ^ bit) for source in range(cou...  37.2 us
  transfers between devices with their start and end apart: 52, of which 29 were waited for; matrix products, arithmetic and copies ran while one was open for 15% of the time, Pallas kernels for 26%

profile of v1, /device:TPU:1, one launch (start us, length us, event | category | flops | bytes accessed | tf_op | source)
XLA Modules:
  0.0 926.2 jit_solution(2983095606623356411)
XLA Ops:
  19.4 10.8 %all-gather.5 = bf16[4,2,2834]{2,1,0:T(2,128)(2,1)S(1)} all-gather(bf16[1,2,2834]{2,1,0:T(2,128)(2,1)S(1)} %bitcast.486), channel_id=2, replica_groups=mesh['seq'=8,'fsdp'=4] {'fsdp'}, dimensions={0}, use_global_device_ids=true | all-gather | bytes 56680 | tf_op jit(solution)/shard_map/all_gather | solution.py:832
  35.8 37.0 %all-gather.17.cloned.1.call-done = bf16[768,1920]{1,0:T(8,128)(2,1)} async-done(((bf16[24,1920]{1,0:T(8,128)(2,1)}), bf16[768,1920]{1,0:T(8,128)(2,1)}) %all-gather.17.cloned.1.call-update) | async-done | bytes 2949136 | tf_op jit(solution)/shard_map/all_gather | solution.py:737
  76.6 7.6 project.2
  90.0 15.0 %prepare.2 = (bf16[1024,1792]{1,0:T(8,128)(2,1)}, bf16[1024,1536]{1,0:T(8,128)(2,1)}, bf16[1024,256]{1,0:T(8,128)(2,1)}, f32[1024,128]{1,0:T(8,128)}, f32[1024,1...) custom-call(bf16[1024,1792]{1,0:T(8,128)(2,1)} %get-tuple-element.93.xc_ref.halo_ref, ...), custom_call_target="tpu_custom_call" | custom-call | tf_op jit(solution)/shard_map/prepare/pallas_call | solution.py:203
  107.4 5.6 collective-permute-done.2
  117.3 10.9 %collective-permute-done.3 = bf16[2,144,768]{2,1,0:T(8,128)(2,1)S(1)} collective-permute-done((bf16[2,144,768]{2,1,0:T(8,128)(2,1)S(1)}, bf16[2,144,768]{2,1,0:T(8,128)(2,1)S(1)}, u32[]{:S(2)}, u32[]{:S(2)}) %collective-permute-start.3) | collective-permute-done | bytes 442400 | tf_op jit(solution)/shard_map/ppermute | solution.py:681
  138.4 56.0 %all-gather.19.cloned.1.call-done = bf16[768,1536]{1,0:T(8,128)(2,1)} async-done(((bf16[24,1536]{1,0:T(8,128)(2,1)}), bf16[768,1536]{1,0:T(8,128)(2,1)}) %all-gather.19.cloned.1.call-update) | async-done | bytes 2359312 | tf_op jit(solution)/shard_map/all_gather | solution.py:737
  197.7 57.8 %all-gather.21.cloned.1.call-done = bf16[768,1920]{1,0:T(8,128)(2,1)} async-done(((bf16[24,1920]{1,0:T(8,128)(2,1)}), bf16[768,1920]{1,0:T(8,128)(2,1)}) %all-gather.21.cloned.1.call-update) | async-done | bytes 2949136 | tf_op jit(solution)/shard_map/all_gather | solution.py:737
  259.1 6.4 project_gate.2.z_ref
  266.1 7.7 within.2.yi_ref
  280.1 16.5 %across.2 = (bf16[1024,1536]{1,0:T(8,128)(2,1)}, bf16[1024,1536]{1,0:T(8,128)(2,1)}, f32[1024,768]{1,0:T(8,128)}, bf16[8,128,1536]{2,1,0:T(8,128)(2,1)}) custom-call(bf16[1024,1536]{1,0:T(8,128)(2,1)} %within.2.yi_ref, bf16[1024,1536]{1,0:T(8,128)(2,1)} %get-tuple-element.95.x_ref, bf16[1024,256]{1,0:T(8,128)(2,1)} %get-tuple-element.96.bc_ref, ...), custom_call_target="tpu_custom_call" | custom-call | tf_op jit(solution)/shard_map/across/pallas_call | solution.py:320
  296.6 8.0 project.3
  310.0 15.0 %prepare.3 = (bf16[1024,1792]{1,0:T(8,128)(2,1)}, bf16[1024,1536]{1,0:T(8,128)(2,1)}, bf16[1024,256]{1,0:T(8,128)(2,1)}, f32[1024,128]{1,0:T(8,128)}, f32[1024,1...) custom-call(bf16[1024,1792]{1,0:T(8,128)(2,1)} %get-tuple-element.104.xc_ref.halo_ref, ...), custom_call_target="tpu_custom_call" | custom-call | tf_op jit(solution)/shard_map/prepare/pallas_call | solution.py:203
  327.4 5.2 collective-permute-done.9
  334.1 8.7 collective-permute-done.10
  343.9 5.4 collective-permute-start.11
  354.5 19.3 %all-gather.23.cloned.1.call-done = bf16[768,1536]{1,0:T(8,128)(2,1)} async-done(((bf16[24,1536]{1,0:T(8,128)(2,1)}), bf16[768,1536]{1,0:T(8,128)(2,1)}) %all-gather.23.cloned.1.call-update) | async-done | bytes 2359312 | tf_op jit(solution)/shard_map/all_gather | solution.py:737
  377.1 6.3 project_gate.3.z_ref
  383.4 7.7 within.3.yi_ref
  401.6 16.3 %across.3 = (bf16[1024,1536]{1,0:T(8,128)(2,1)}, bf16[1024,1536]{1,0:T(8,128)(2,1)}, bf16[1024,768]{1,0:T(8,128)(2,1)}, bf16[8,128,1536]{2,1,0:T(8,128)(2,1)}) custom-call(bf16[1024,1536]{1,0:T(8,128)(2,1)} %within.3.yi_ref, bf16[1024,1536]{1,0:T(8,128)(2,1)} %get-tuple-element.106.x_ref, bf16[1024,256]{1,0:T(8,128)(2,1)} %get-tuple-element.107.bc_ref, ...), custom_call_target="tpu_custom_call" | custom-call | tf_op jit(solution)/shard_map/across/pallas_call | solution.py:320
  417.9 20.1 %open_back.2 = (bf16[1024,1536]{1,0:T(8,128)(2,1)}, bf16[1024,1536]{1,0:T(8,128)(2,1)}, bf16[1024,768]{1,0:T(8,128)(2,1)}, f32[8,1536]{1,0:T(8,128)}, bf16[128,1536]{1,0:T(8,128)(2,1)}) custom-call(bf16[1024,768]{1,0:T(8,128)(2,1)} %bitcast.450, bf16[1536,768]{1,0:T(8,128)(2,1)} %bitcast.434, bf16[1024,1536]{1,0:T(8,128)(2,1)} %get-tuple-element.115.y_ref, ...), custom_call_target="tpu_custom_call" | custom-call | tf_op jit(solution)/shard_map/open_back/pallas_call | solution.py:403
  438.0 5.4 convolution_convert_fusion
  445.6 5.5 collective-permute-done.15
  452.6 12.3 %collective-permute-done.18 = bf16[1,128,768]{2,1,0:T(8,128)(2,1)S(1)} collective-permute-done((bf16[1,128,768]{2,1,0:T(8,128)(2,1)S(1)}, bf16[1,128,768]{2,1,0:T(8,128)(2,1)S(1)}, u32[]{:S(2)}, u32[]{:S(2)}) %collective-permute-start.18) | collective-permute-done | bytes 196640 | tf_op jit(solution)/shard_map/ppermute | solution.py:681
  482.8 23.3 %within_back.2 = (bf16[1024,1536]{1,0:T(8,128)(2,1)}, f32[1024,256]{1,0:T(8,128)}, f32[1024,128]{1,0:T(8,128)}) custom-call(bf16[1024,1536]{1,0:T(8,128)(2,1)} %get-tuple-element.106.x_ref, bf16[1024,1536]{1,0:T(8,128)(2,1)} %get-tuple-element.118.dy_ref, bf16[1024,256]{1,0:T(8,128)(2,1)} %get-tuple-element.107.bc_ref, ...), custom_call_target="tpu_custom_call" | custom-call | tf_op jit(solution)/shard_map/within_back/pallas_call | solution.py:472
  510.1 31.3 %across_back.2 = (bf16[1024,1920]{1,0:T(8,128)(2,1)}, f32[8,1792]{1,0:T(8,128)}, f32[8,128]{1,0:T(8,128)}, f32[8,1792]{1,0:T(8,128)}) custom-call(bf16[1024,1536]{1,0:T(8,128)(2,1)} %get-tuple-element.106.x_ref, bf16[1024,1792]{1,0:T(8,128)(2,1)} %get-tuple-element.117.pre_ref, bf16[1024,1792]{1,0:T(8,128)(2,1)} %get-tuple-element.104.xc_ref.halo_ref, ...), custom_call_target="tpu_custom_call" | custom-call | tf_op jit(solution)/shard_map/across_back/pallas_call | solution.py:613
  551.0 11.9 %close_back.2 = (f32[1024,768]{1,0:T(8,128)}, f32[8,768]{1,0:T(8,128)}) custom-call(bf16[1024,1536]{1,0:T(8,128)(2,1)} %get-tuple-element.116.dz_ref, bf16[1024,1920]{1,0:T(8,128)(2,1)} %scatter.6.dxc_ref, bf16[768,1536]{1,0:T(8,128)(2,1)} %bitcast.438, bf16[768,1920]{1,0:T(8,128)(2,1)} %bitcast.430, f32[1024,768]{1,0:T(8,128)} %get-tuple-element.103.x_ref.res_ref, ...), custom_call_target="tpu_custom_call" | custom-call | tf_op jit(solution)/shard_map/close_back/pallas_call | solution.py:660
  562.9 19.8 %open_back.3 = (bf16[1024,1536]{1,0:T(8,128)(2,1)}, bf16[1024,1536]{1,0:T(8,128)(2,1)}, bf16[1024,768]{1,0:T(8,128)(2,1)}, f32[8,1536]{1,0:T(8,128)}, bf16[128,1536]{1,0:T(8,128)(2,1)}) custom-call(f32[1024,768]{1,0:T(8,128)} %get-tuple-element.126.g_ref, bf16[1536,768]{1,0:T(8,128)(2,1)} %bitcast.432, bf16[1024,1536]{1,0:T(8,128)(2,1)} %get-tuple-element.127.y_ref, ...), custom_call_target="tpu_custom_call" | custom-call | tf_op jit(solution)/shard_map/open_back/pallas_call | solution.py:403
  582.7 5.5 convolution_convert_fusion.1
  596.6 6.0 convolution_convert_fusion.4
  609.3 8.2 collective-permute-done.22
  620.2 10.3 %collective-permute-done.23 = bf16[2,128,768]{2,1,0:T(8,128)(2,1)S(1)} collective-permute-done((bf16[2,128,768]{2,1,0:T(8,128)(2,1)S(1)}, bf16[2,128,768]{2,1,0:T(8,128)(2,1)S(1)}, u32[]{:S(2)}, u32[]{:S(2)}) %collective-permute-start.23) | collective-permute-done | bytes 393248 | tf_op jit(solution)/shard_map/ppermute | solution.py:681
  632.5 23.2 %within_back.3 = (bf16[1024,1536]{1,0:T(8,128)(2,1)}, f32[1024,256]{1,0:T(8,128)}, f32[1024,128]{1,0:T(8,128)}) custom-call(bf16[1024,1536]{1,0:T(8,128)(2,1)} %get-tuple-element.95.x_ref, bf16[1024,1536]{1,0:T(8,128)(2,1)} %get-tuple-element.130.dy_ref, bf16[1024,256]{1,0:T(8,128)(2,1)} %get-tuple-element.96.bc_ref, f32[1024,128]{1,0:T(8,128)} %get-tuple-element.100.dt_ref, ...), custom_call_target="tpu_custom_call" | custom-call | tf_op jit(solution)/shard_map/within_back/pallas_call | solution.py:472
  659.8 31.8 %across_back.3 = (bf16[1024,1920]{1,0:T(8,128)(2,1)}, f32[8,1792]{1,0:T(8,128)}, f32[8,128]{1,0:T(8,128)}, f32[8,1792]{1,0:T(8,128)}) custom-call(bf16[1024,1536]{1,0:T(8,128)(2,1)} %get-tuple-element.95.x_ref, bf16[1024,1792]{1,0:T(8,128)(2,1)} %get-tuple-element.129.pre_ref, bf16[1024,1792]{1,0:T(8,128)(2,1)} %get-tuple-element.93.xc_ref.halo_ref, ...), custom_call_target="tpu_custom_call" | custom-call | tf_op jit(solution)/shard_map/across_back/pallas_call | solution.py:613
  703.2 5.8 convolution_convert_fusion.5
  719.3 12.1 %close_back.3 = (f32[1024,768]{1,0:T(8,128)}, f32[8,768]{1,0:T(8,128)}) custom-call(bf16[1024,1536]{1,0:T(8,128)(2,1)} %get-tuple-element.128.dz_ref, bf16[1024,1920]{1,0:T(8,128)(2,1)} %scatter.9.dxc_ref, bf16[768,1536]{1,0:T(8,128)(2,1)} %bitcast.436, bf16[768,1920]{1,0:T(8,128)(2,1)} %bitcast.428, bf16[1024,768]{1,0:T(8,128)(2,1)} %bitcast.441, ...), custom_call_target="tpu_custom_call" | custom-call | tf_op jit(solution)/shard_map/close_back/pallas_call | solution.py:660
  753.0 11.8 %all_gather.73 = bf16[1,384,768]{2,1,0:T(8,128)(2,1)S(1)} all-gather(bf16[1,48,768]{2,1,0:T(8,128)(2,1)} %reduce-scatter.35.cloned.1.call-done), channel_id=1, replica_groups=mesh['seq'=8,'fsdp'=4] {'seq'}, dimensions={1}, use_global_device_ids=true | all-gather | bytes 663552 | tf_op jit(solution)/shard_map/all_gather | solution.py:748
  764.8 6.7 reduce-scatter.27.cloned.1.call-done
  771.5 12.4 %all_gather.70 = bf16[1,192,1536]{2,1,0:T(8,128)(2,1)S(1)} all-gather(bf16[1,24,1536]{2,1,0:T(8,128)(2,1)} %reduce-scatter.27.cloned.1.call-done), channel_id=1, replica_groups=mesh['seq'=8,'fsdp'=4] {'seq'}, dimensions={1}, use_global_device_ids=true | all-gather | bytes 663552 | tf_op jit(solution)/shard_map/all_gather | solution.py:748
  783.9 7.8 reduce-scatter.31.cloned.1.call-done
  791.8 12.4 %all_gather.72 = bf16[1,384,768]{2,1,0:T(8,128)(2,1)S(1)} all-gather(bf16[1,48,768]{2,1,0:T(8,128)(2,1)} %reduce-scatter.31.cloned.1.call-done), channel_id=1, replica_groups=mesh['seq'=8,'fsdp'=4] {'seq'}, dimensions={1}, use_global_device_ids=true | all-gather | bytes 663552 | tf_op jit(solution)/shard_map/all_gather | solution.py:748
  805.8 34.4 %reduce-scatter.39.cloned.1.call-done = bf16[24,7680]{1,0:T(8,128)(2,1)} async-done(((bf16[192,7680]{1,0:T(8,128)(2,1)}), bf16[24,7680]{1,0:T(8,128)(2,1)}) %reduce-scatter.39.cloned.1.call-update) | async-done | bytes 368656
  842.1 18.5 %reduce-scatter.25.cloned.1.call-done = bf16[1,24,1536]{2,1,0:T(8,128)(2,1)} async-done(((bf16[4,24,1536]{2,1,0:T(8,128)(2,1)}), bf16[1,24,1536]{2,1,0:T(8,128)(2,1)}) %reduce-scatter.25.cloned.1.call-update) | async-done | bytes 73744 | tf_op jit(solution)/shard_map/reduce_scatter | solution.py:747
  860.6 12.5 %all_gather.68 = bf16[1,192,1536]{2,1,0:T(8,128)(2,1)S(1)} all-gather(bf16[1,24,1536]{2,1,0:T(8,128)(2,1)} %reduce-scatter.25.cloned.1.call-done), channel_id=1, replica_groups=mesh['seq'=8,'fsdp'=4] {'seq'}, dimensions={1}, use_global_device_ids=true | all-gather | bytes 663552 | tf_op jit(solution)/shard_map/all_gather | solution.py:748
  873.0 8.8 reduce-scatter.47.cloned.1.call-done
  881.9 13.1 %all_gather.71 = bf16[1,192,1920]{2,1,0:T(8,128)(2,1)S(1)} all-gather(bf16[1,24,1920]{2,1,0:T(8,128)(2,1)} %reduce-scatter.47.cloned.1.call-done), channel_id=1, replica_groups=mesh['seq'=8,'fsdp'=4] {'seq'}, dimensions={1}, use_global_device_ids=true | all-gather | bytes 829440 | tf_op jit(solution)/shard_map/all_gather | solution.py:748
  895.1 8.0 reduce-scatter.45.cloned.1.call-done
  903.1 13.2 %all_gather.69 = bf16[1,192,1920]{2,1,0:T(8,128)(2,1)S(1)} all-gather(bf16[1,24,1920]{2,1,0:T(8,128)(2,1)} %reduce-scatter.45.cloned.1.call-done), channel_id=1, replica_groups=mesh['seq'=8,'fsdp'=4] {'seq'}, dimensions={1}, use_global_device_ids=true | all-gather | bytes 829440 | tf_op jit(solution)/shard_map/all_gather | solution.py:748
  (398 shorter events, 194.6 us)
Async XLA Ops:
  7.2 65.7 %all-gather.17.cloned.1.call-start = ((), (), s32[]{:S(2)}) async-start(), calls=%async_computation.20 | async-start | bytes 3041280 | tf_op jit(solution)/shard_map/all_gather | solution.py:737
  9.9 125.2 %all-gather.13.cloned.1.call-start = ((), (), s32[]{:S(2)}) async-start(), calls=%async_computation.12 | async-start | bytes 2433024 | tf_op jit(solution)/shard_map/all_gather | solution.py:737
  12.0 182.4 %all-gather.19.cloned.1.call-start = ((), (), s32[]{:S(2)}) async-start(), calls=%async_computation.21 | async-start | bytes 2433024 | tf_op jit(solution)/shard_map/all_gather | solution.py:737
  12.8 242.7 %all-gather.21.cloned.1.call-start = ((), (), s32[]{:S(2)}) async-start(), calls=%async_computation.22 | async-start | bytes 3041280 | tf_op jit(solution)/shard_map/all_gather | solution.py:737
  13.6 337.7 %all-gather.15.cloned.1.call-start = ((), (), s32[]{:S(2)}) async-start(), calls=%async_computation.13 | async-start | bytes 2433024 | tf_op jit(solution)/shard_map/all_gather | solution.py:737
  14.3 359.5 %all-gather.23.cloned.1.call-start = ((), (), s32[]{:S(2)}) async-start(), calls=%async_computation.23 | async-start | bytes 2433024 | tf_op jit(solution)/shard_map/all_gather | solution.py:737
  14.4 21.1 %collective-permute-start.1 = (s32[3]{0:T(128)S(1)}, s32[3]{0:T(128)S(1)}, u32[]{:S(2)}, u32[]{:S(2)}) collective-permute-start(s32[3]{0:T(128)S(1)} %slice_bitcast_fusion.66), channel_id=1, source_target_pairs={{0,4},{4,8},{8,12},{12,16},{16,20},{20,24},{24,28},{1,5},{5,9},{9,... | collective-permute-start | bytes 44 | tf_op jit(solution)/shard_map/ppermute | solution.py:676
  84.9 4.5 collective-permute-start
  106.1 6.9 collective-permute-start.2
  113.1 15.1 %collective-permute-start.3 = (bf16[2,144,768]{2,1,0:T(8,128)(2,1)S(1)}, bf16[2,144,768]{2,1,0:T(8,128)(2,1)S(1)}, u32[]{:S(2)}, u32[]{:S(2)}) collective-permute-start(bf16[2,144,768]{2,1,0:T(8,128)(2,1)S(1)} %pad_maximum_fusion.12), channel_id=1, source_target_pairs={{0,16},{4,20},{8,24},{12,28},{16,0},{20,4},{24,8},{28,12},{1,17},{... | collective-permute-start | bytes 1327112 | tf_op jit(solution)/shard_map/ppermute | solution.py:681
  113.9 577.7 %reduce-scatter.33.cloned.1.call-start = ((), (), s32[]{:S(2)}) async-start(), calls=%async_computation.18 | async-start | bytes 2654208 | tf_op jit(solution)/shard_map/reduce_scatter | solution.py:746
  115.8 17.1 %collective-permute-start.5 = (bf16[1,144,768]{2,1,0:T(8,128)(2,1)S(1)}, bf16[1,144,768]{2,1,0:T(8,128)(2,1)S(1)}, u32[]{:S(2)}, u32[]{:S(2)}) collective-permute-start(bf16[1,144,768]{2,1,0:T(8,128)(2,1)S(1)} %get-tuple-element.246), channel_id=1, source_target_pairs={{0,16},{4,20},{8,24},{12,28},{16,0},{20,4},{24,8},{28,12},{1,17},{... | collective-permute-start | bytes 663560 | tf_op jit(solution)/shard_map/ppermute | solution.py:681
  129.2 145.9 %collective-permute-start.4 = (bf16[4,144,768]{2,1,0:T(8,128)(2,1)}, bf16[4,144,768]{2,1,0:T(8,128)(2,1)S(1)}, u32[]{:S(2)}, u32[]{:S(2)}) collective-permute-start(bf16[4,144,768]{2,1,0:T(8,128)(2,1)} %pad_maximum_fusion), channel_id=1, source_target_pairs={{0,4},{4,0},{8,12},{12,8},{16,20},{20,16},{24,28},{28,24},{1,5},{5... | collective-permute-start | bytes 2654216 | tf_op jit(solution)/shard_map/ppermute | solution.py:681
  133.0 140.9 %collective-permute-start.6 = (bf16[2,144,768]{2,1,0:T(8,128)(2,1)S(1)}, bf16[2,144,768]{2,1,0:T(8,128)(2,1)S(1)}, u32[]{:S(2)}, u32[]{:S(2)}) collective-permute-start(bf16[2,144,768]{2,1,0:T(8,128)(2,1)S(1)} %pad_maximum_fusion.13), channel_id=1, source_target_pairs={{0,8},{4,12},{8,0},{12,4},{16,24},{20,28},{24,16},{28,20},{1,9},{5... | collective-permute-start | bytes 1327112 | tf_op jit(solution)/shard_map/ppermute | solution.py:681
  305.3 4.0 collective-permute-start.8
  326.1 6.5 collective-permute-start.9
  332.6 10.3 %collective-permute-start.10 = (bf16[2,144,768]{2,1,0:T(8,128)(2,1)S(1)}, bf16[2,144,768]{2,1,0:T(8,128)(2,1)S(1)}, u32[]{:S(2)}, u32[]{:S(2)}) collective-permute-start(bf16[2,144,768]{2,1,0:T(8,128)(2,1)S(1)} %pad_maximum_fusion.14), channel_id=1, source_target_pairs={{0,16},{4,20},{8,24},{12,28},{16,0},{20,4},{24,8},{28,12},{1,17},{... | collective-permute-start | bytes 1327112 | tf_op jit(solution)/shard_map/ppermute | solution.py:681
  332.7 16.6 %collective-permute-start.12 = (bf16[1,144,768]{2,1,0:T(8,128)(2,1)S(1)}, bf16[1,144,768]{2,1,0:T(8,128)(2,1)S(1)}, u32[]{:S(2)}, u32[]{:S(2)}) collective-permute-start(bf16[1,144,768]{2,1,0:T(8,128)(2,1)S(1)} %get-tuple-element.244), channel_id=1, source_target_pairs={{0,16},{4,20},{8,24},{12,28},{16,0},{20,4},{24,8},{28,12},{1,17},{... | collective-permute-start | bytes 663560 | tf_op jit(solution)/shard_map/ppermute | solution.py:681
  343.9 47.7 %collective-permute-start.11 = (bf16[4,144,768]{2,1,0:T(8,128)(2,1)}, bf16[4,144,768]{2,1,0:T(8,128)(2,1)S(1)}, u32[]{:S(2)}, u32[]{:S(2)}) collective-permute-start(bf16[4,144,768]{2,1,0:T(8,128)(2,1)} %pad_maximum_fusion.2), channel_id=1, source_target_pairs={{0,4},{4,0},{8,12},{12,8},{16,20},{20,16},{24,28},{28,24},{1,5},{5... | collective-permute-start | bytes 2654216 | tf_op jit(solution)/shard_map/ppermute | solution.py:681
  349.3 41.8 %collective-permute-start.13 = (bf16[2,144,768]{2,1,0:T(8,128)(2,1)S(1)}, bf16[2,144,768]{2,1,0:T(8,128)(2,1)S(1)}, u32[]{:S(2)}, u32[]{:S(2)}) collective-permute-start(bf16[2,144,768]{2,1,0:T(8,128)(2,1)S(1)} %pad_maximum_fusion.15), channel_id=1, source_target_pairs={{0,8},{4,12},{8,0},{12,4},{16,24},{20,28},{24,16},{28,20},{1,9},{5... | collective-permute-start | bytes 1327112 | tf_op jit(solution)/shard_map/ppermute | solution.py:681
  391.3 7.8 collective-permute-start.14
  443.5 249.8 %reduce-scatter.41.cloned.1.call-start = ((), (), s32[]{:S(2)}) async-start(), calls=%async_computation.26 | async-start | bytes 2654208
  444.7 6.3 collective-permute-start.15
  451.1 15.5 %collective-permute-start.16 = (bf16[2,128,768]{2,1,0:T(8,128)(2,1)S(1)}, bf16[2,128,768]{2,1,0:T(8,128)(2,1)S(1)}, u32[]{:S(2)}, u32[]{:S(2)}) collective-permute-start(bf16[2,128,768]{2,1,0:T(8,128)(2,1)S(1)} %pad_maximum_fusion.16), channel_id=1, source_target_pairs={{0,16},{4,20},{8,24},{12,28},{16,0},{20,4},{24,8},{28,12},{1,17},{... | collective-permute-start | bytes 1179656 | tf_op jit(solution)/shard_map/ppermute | solution.py:681
  452.0 12.9 %collective-permute-start.18 = (bf16[1,128,768]{2,1,0:T(8,128)(2,1)S(1)}, bf16[1,128,768]{2,1,0:T(8,128)(2,1)S(1)}, u32[]{:S(2)}, u32[]{:S(2)}) collective-permute-start(bf16[1,128,768]{2,1,0:T(8,128)(2,1)S(1)} %get-tuple-element.250), channel_id=1, source_target_pairs={{0,16},{4,20},{8,24},{12,28},{16,0},{20,4},{24,8},{28,12},{1,17},{... | collective-permute-start | bytes 589832 | tf_op jit(solution)/shard_map/ppermute | solution.py:681
  465.7 12.6 %collective-permute-start.19 = (bf16[2,128,768]{2,1,0:T(8,128)(2,1)}, bf16[2,128,768]{2,1,0:T(8,128)(2,1)}, u32[]{:S(2)}, u32[]{:S(2)}) collective-permute-start(bf16[2,128,768]{2,1,0:T(8,128)(2,1)} %pad_maximum_fusion.17), channel_id=1, source_target_pairs={{0,8},{4,12},{8,0},{12,4},{16,24},{20,28},{24,16},{28,20},{1,9},{5... | collective-permute-start | bytes 1179656 | tf_op jit(solution)/shard_map/ppermute | solution.py:681
  467.6 38.7 %collective-permute-start.17 = (bf16[4,128,768]{2,1,0:T(8,128)(2,1)}, bf16[4,128,768]{2,1,0:T(8,128)(2,1)}, u32[]{:S(2)}, u32[]{:S(2)}) collective-permute-start(bf16[4,128,768]{2,1,0:T(8,128)(2,1)} %pad_maximum_fusion.6), channel_id=1, source_target_pairs={{0,4},{4,0},{8,12},{12,8},{16,20},{20,16},{24,28},{28,24},{1,5},{5... | collective-permute-start | bytes 2359304 | tf_op jit(solution)/shard_map/ppermute | solution.py:681
  478.0 225.1 %reduce-scatter.29.cloned.1.call-start = ((), (), s32[]{:S(2)}) async-start(), calls=%async_computation.16 | async-start | bytes 2654208 | tf_op jit(solution)/shard_map/reduce_scatter | solution.py:746
  479.4 28.4 %collective-permute-start.20 = (bf16[4,128,768]{2,1,0:T(8,128)(2,1)S(1)}, bf16[4,128,768]{2,1,0:T(8,128)(2,1)S(1)}, u32[]{:S(2)}, u32[]{:S(2)}) collective-permute-start(bf16[4,128,768]{2,1,0:T(8,128)(2,1)S(1)} %pad_maximum_fusion.7), channel_id=1, source_target_pairs={{0,4},{4,0},{8,12},{12,8},{16,20},{20,16},{24,28},{28,24},{1,5},{5... | collective-permute-start | bytes 2359304 | tf_op jit(solution)/shard_map/ppermute | solution.py:681
  543.0 5.2 collective-permute-start.21
  588.3 157.4 %reduce-scatter.37.cloned.1.call-start = ((), (), s32[]{:S(2)}) async-start(), calls=%async_computation.24 | async-start | bytes 2654208
  596.6 153.8 %reduce-scatter.43.cloned.1.call-start = ((), (), s32[]{:S(2)}) async-start(), calls=%async_computation.27 | async-start | bytes 3317760
  606.9 146.0 %reduce-scatter.35.cloned.1.call-start = ((), (), s32[]{:S(2)}) async-start(), calls=%async_computation.19 | async-start | bytes 368640 | tf_op jit(solution)/shard_map/reduce_scatter | solution.py:747
  607.9 9.6 %collective-permute-start.22 = (bf16[1,128,768]{2,1,0:T(8,128)(2,1)S(1)}, bf16[1,128,768]{2,1,0:T(8,128)(2,1)S(1)}, u32[]{:S(2)}, u32[]{:S(2)}) collective-permute-start(bf16[1,128,768]{2,1,0:T(8,128)(2,1)S(1)} %get-tuple-element.247), channel_id=1, source_target_pairs={{0,8},{4,12},{8,0},{12,4},{16,24},{20,28},{24,16},{28,20},{1,9},{5... | collective-permute-start | bytes 589832 | tf_op jit(solution)/shard_map/ppermute | solution.py:681
  609.2 10.9 %collective-permute-start.25 = (bf16[1,128,768]{2,1,0:T(8,128)(2,1)S(1)}, bf16[1,128,768]{2,1,0:T(8,128)(2,1)S(1)}, u32[]{:S(2)}, u32[]{:S(2)}) collective-permute-start(bf16[1,128,768]{2,1,0:T(8,128)(2,1)S(1)} %get-tuple-element.248), channel_id=1, source_target_pairs={{0,16},{4,20},{8,24},{12,28},{16,0},{20,4},{24,8},{28,12},{1,17},{... | collective-permute-start | bytes 589832 | tf_op jit(solution)/shard_map/ppermute | solution.py:681
  617.6 13.0 %collective-permute-start.23 = (bf16[2,128,768]{2,1,0:T(8,128)(2,1)S(1)}, bf16[2,128,768]{2,1,0:T(8,128)(2,1)S(1)}, u32[]{:S(2)}, u32[]{:S(2)}) collective-permute-start(bf16[2,128,768]{2,1,0:T(8,128)(2,1)S(1)} %pad_maximum_fusion.18), channel_id=1, source_target_pairs={{0,16},{4,20},{8,24},{12,28},{16,0},{20,4},{24,8},{28,12},{1,17},{... | collective-permute-start | bytes 1179656 | tf_op jit(solution)/shard_map/ppermute | solution.py:681
  620.2 10.9 %collective-permute-start.26 = (bf16[2,128,768]{2,1,0:T(8,128)(2,1)S(1)}, bf16[2,128,768]{2,1,0:T(8,128)(2,1)S(1)}, u32[]{:S(2)}, u32[]{:S(2)}) collective-permute-start(bf16[2,128,768]{2,1,0:T(8,128)(2,1)S(1)} %pad_maximum_fusion.19), channel_id=1, source_target_pairs={{0,8},{4,12},{8,0},{12,4},{16,24},{20,28},{24,16},{28,20},{1,9},{5... | collective-permute-start | bytes 1179656 | tf_op jit(solution)/shard_map/ppermute | solution.py:681
  630.6 25.1 %collective-permute-start.24 = (bf16[4,128,768]{2,1,0:T(8,128)(2,1)S(1)}, bf16[4,128,768]{2,1,0:T(8,128)(2,1)}, u32[]{:S(2)}, u32[]{:S(2)}) collective-permute-start(bf16[4,128,768]{2,1,0:T(8,128)(2,1)S(1)} %pad_maximum_fusion.9), channel_id=1, source_target_pairs={{0,4},{4,0},{8,12},{12,8},{16,20},{20,16},{24,28},{28,24},{1,5},{5... | collective-permute-start | bytes 2359304 | tf_op jit(solution)/shard_map/ppermute | solution.py:681
  631.2 26.1 %collective-permute-start.27 = (bf16[4,128,768]{2,1,0:T(8,128)(2,1)S(1)}, bf16[4,128,768]{2,1,0:T(8,128)(2,1)}, u32[]{:S(2)}, u32[]{:S(2)}) collective-permute-start(bf16[4,128,768]{2,1,0:T(8,128)(2,1)S(1)} %pad_maximum_fusion.10), channel_id=1, source_target_pairs={{0,4},{4,0},{8,12},{12,8},{16,20},{20,16},{24,28},{28,24},{1,5},{5... | collective-permute-start | bytes 2359304 | tf_op jit(solution)/shard_map/ppermute | solution.py:681
  691.6 79.8 %reduce-scatter.27.cloned.1.call-start = ((), (), s32[]{:S(2)}) async-start(), calls=%async_computation.15 | async-start | bytes 368640 | tf_op jit(solution)/shard_map/reduce_scatter | solution.py:747
  695.3 96.5 %reduce-scatter.31.cloned.1.call-start = ((), (), s32[]{:S(2)}) async-start(), calls=%async_computation.17 | async-start | bytes 368640 | tf_op jit(solution)/shard_map/reduce_scatter | solution.py:747
  695.4 5.2 collective-permute-start.28
  703.2 137.1 %reduce-scatter.39.cloned.1.call-start = ((), (), s32[]{:S(2)}) async-start(), calls=%async_computation.25 | async-start | bytes 3317760
  713.3 147.3 %reduce-scatter.25.cloned.1.call-start = ((), (), s32[]{:S(2)}) async-start(), calls=%async_computation.14 | async-start | bytes 368640 | tf_op jit(solution)/shard_map/reduce_scatter | solution.py:747
  732.5 4.1 collective-permute-start.29
  740.7 3.8 collective-permute-start.32
  747.7 134.2 %reduce-scatter.47.cloned.1.call-start = ((), (), s32[]{:S(2)}) async-start(), calls=%async_computation.29 | async-start | bytes 460800
  752.3 150.8 %reduce-scatter.45.cloned.1.call-start = ((), (), s32[]{:S(2)}) async-start(), calls=%async_computation.28 | async-start | bytes 460800
  (39 other events, 815.3 us)
Sparse Core Ops, SparseCore 0:
  11.4 61.3 all-gather.16
  75.7 59.4 all-gather.12
  138.5 55.9 all-gather.18
  197.7 57.7 all-gather.20
  258.2 56.1 all-gather.14
  317.0 56.8 all-gather.22
  443.6 44.5 reduce-scatter.32
  491.9 42.5 reduce-scatter.40
  588.4 47.4 reduce-scatter.28
  639.5 42.4 reduce-scatter.36
  685.4 45.2 reduce-scatter.42
  732.8 18.1 reduce-scatter.34
  753.3 18.1 reduce-scatter.26
  773.6 18.1 reduce-scatter.30
  795.0 45.1 reduce-scatter.38
  842.3 18.1 reduce-scatter.24
  863.3 18.5 reduce-scatter.46
  884.1 18.9 reduce-scatter.44

commit v2 on v1

--- a/solution.py
+++ b/solution.py
@@ -1,3 +1,5 @@
+from functools import partial
+
 import jax
 import jax.numpy as jnp
 import numpy as np
@@ -13,7 +15,10 @@
 K = 4
 E = 1536
 CV = 1792
-CX = CV + 128
+HX = CV // 2
+HZ = E // 2
+HD = D // 2
+CX = HX + 128
 Q = 128
 TT = 256
 SUB = TT // Q
@@ -89,47 +94,69 @@
     return pltpu.CompilerParams(vmem_limit_bytes=VMEM_LIMIT, dimension_semantics=("arbitrary",))
 
 
+def cost(micros):
+    return pl.CostEstimate(
+        flops=int(micros * 1e9), bytes_accessed=int(micros * 3e6), transcendentals=0
+    )
+
+
+SMEM = pl.BlockSpec(memory_space=pltpu.SMEM)
+
+
+def sides(core_ref, width):
+    mine = core_ref[0] * width
+    return pl.ds(pl.multiple_of(mine, 128), width), pl.ds(
+        pl.multiple_of(width - mine, 128), width
+    )
+
+
 def shape(dims, dtype):
     return jax.ShapeDtypeStruct(dims, dtype)
 
 
-def project_kernel(x_ref, gain_ref, w_ref, normed_ref, xc_ref, dtr_ref):
+def project_kernel(core_ref, x_ref, gain_ref, mine_ref, other_ref, normed_ref, xc_ref, dtr_ref):
     x = x_ref[...].astype(f32)
     scale = lax.rsqrt(jnp.mean(x * x, axis=-1, keepdims=True) + eps)
     normed = (x * scale * gain_ref[...]).astype(bf16)
     normed_ref[...] = normed
-    xc_ref[...] = nn(normed, w_ref[:, :CV]).astype(bf16)
-    dtr_ref[...] = nn(normed, w_ref[:, CV:])
-
-
-def project(x, gain, w):
+    own, far = sides(core_ref, HX)
+    xc_ref[:, own] = nn(normed, mine_ref[:, :HX]).astype(bf16)
+    dtr_ref[...] = nn(normed, mine_ref[:, HX:])
+    xc_ref[:, far] = nn(normed, other_ref[:, :HX]).astype(bf16)
+
+
+def project(core, x, gain, mine, other):
     t = x.shape[0]
     return pl.pallas_call(
         project_kernel,
         grid=(t // TT,),
-        in_specs=[rows(D), full((1, D)), full((D, CX))],
+        in_specs=[SMEM, rows(D), full((1, D)), full((D, CX)), full((D, CX))],
         out_specs=[rows(D), rows(CV), rows(128)],
         out_shape=[shape((t, D), bf16), shape((t, CV), bf16), shape((t, 128), f32)],
         compiler_params=params(),
+        cost_estimate=cost(8),
         name="project",
-    )(x, gain, w)
-
-
-def gate_kernel(normed_ref, w_ref, z_ref):
-    z_ref[...] = nn(normed_ref[...], w_ref[...]).astype(bf16)
-
-
-def project_gate(normed, w):
+    )(core, x, gain, mine, other)
+
+
+def gate_kernel(core_ref, normed_ref, mine_ref, other_ref, z_ref):
+    own, far = sides(core_ref, HZ)
+    z_ref[:, own] = nn(normed_ref[...], mine_ref[...]).astype(bf16)
+    z_ref[:, far] = nn(normed_ref[...], other_ref[...]).astype(bf16)
+
+
+def project_gate(core, normed, mine, other):
     t = normed.shape[0]
     return pl.pallas_call(
         gate_kernel,
         grid=(t // TT,),
-        in_specs=[rows(D), full((D, E))],
+        in_specs=[SMEM, rows(D), full((D, HZ)), full((D, HZ))],
         out_specs=rows(E),
         out_shape=shape((t, E), bf16),
         compiler_params=params(),
+        cost_estimate=cost(6),
         name="project_gate",
-    )(normed, w)
+    )(core, normed, mine, other)
 
 
 def prepare_kernel(
@@ -227,6 +254,7 @@
             pltpu.VMEM((8, 128), f32),
         ],
         compiler_params=params(),
+        cost_estimate=cost(15),
         name="prepare",
     )(xc, edge, cw, dtr, spike, tok, pv, e2)
 
@@ -260,13 +288,14 @@
         out_specs=rows(E),
         out_shape=shape((t, E), bf16),
         compiler_params=params(),
+        cost_estimate=cost(8),
         name="within",
     )(x, bc, cum, cumt, dtt, tok, doct)
 
 
 def across_kernel(
-    yi_ref, x_ref, bc_ref, dt_ref, cum_ref, tok_ref, z_ref, first_ref, skip_ref, gain_ref,
-    w_ref, res_ref, e2_ref,
+    core_ref, yi_ref, x_ref, bc_ref, dt_ref, cum_ref, tok_ref, z_ref, first_ref, skip_ref,
+    gain_ref, mine_ref, other_ref, res_ref, e2_ref,
     y_ref, low_ref, new_ref, prior_ref,
     state, gated,
 ):
@@ -311,18 +340,20 @@
         for b in range(E // W):
             at = slice(b * W, (b + 1) * W)
             low_ref[r, at] = (gated[r, at] * scale * gain_ref[0:1, at]).astype(bf16)
-    new = res_ref[...].astype(f32) + nn(low_ref[...], w_ref[...])
-    new_ref[...] = new.astype(new_ref.dtype)
-
-
-def across(yi, x, bc, dt, cum, tok, z, first, skip, gain, w, res, e2, out_type):
+    for at, w_ref in zip(sides(core_ref, HD), (mine_ref, other_ref)):
+        new = res_ref[:, at].astype(f32) + nn(low_ref[...], w_ref[...])
+        new_ref[:, at] = new.astype(new_ref.dtype)
+
+
+def across(core, yi, x, bc, dt, cum, tok, z, first, skip, gain, mine, other, res, e2, out_type):
     t = x.shape[0]
     return pl.pallas_call(
         across_kernel,
         grid=(t // TT,),
         in_specs=[
-            rows(E), rows(E), rows(2 * N), rows(128), rows(128), rows(128), rows(E),
-            full((N, E)), full((1, E)), full((1, E)), full((E, D)), rows(D), full((256, E)),
+            SMEM, rows(E), rows(E), rows(2 * N), rows(128), rows(128), rows(128), rows(E),
+            full((N, E)), full((1, E)), full((1, E)), full((E, HD)), full((E, HD)), rows(D),
+            full((256, E)),
         ],
         out_specs=[rows(E), rows(E), rows(D), pl.BlockSpec((SUB, N, E), lambda i: (i, 0, 0))],
         out_shape=[
@@ -333,12 +364,14 @@
         ],
         scratch_shapes=[pltpu.VMEM((N, E), f32), pltpu.VMEM((TT, E), f32)],
         compiler_params=params(),
+        cost_estimate=cost(16),
         name="across",
-    )(yi, x, bc, dt, cum, tok, z, first, skip, gain, w, res, e2)
+    )(core, yi, x, bc, dt, cum, tok, z, first, skip, gain, mine, other, res, e2)
 
 
 def open_back_kernel(
-    g_ref, w_ref, y_ref, z_ref, x_ref, bc_ref, cum_ref, tok_ref, gain_ref, e2_ref,
+    core_ref, g_ref, mine_ref, other_ref, y_ref, z_ref, x_ref, bc_ref, cum_ref, tok_ref,
+    gain_ref, e2_ref,
     dy_ref, dz_ref, gb_ref, acc_ref, low_ref,
     held, state_ref,
 ):
@@ -349,9 +382,9 @@
         acc_ref[...] = jnp.zeros_like(acc_ref)
         state_ref[...] = jnp.zeros_like(state_ref)
 
-    gb = g_ref[...].astype(bf16)
-    gb_ref[...] = gb
-    held[...] = nt(gb, w_ref[...])
+    gb_ref[...] = g_ref[...].astype(bf16)
+    own, far = sides(core_ref, HD)
+    held[...] = nt(gb_ref[:, own], mine_ref[...]) + nt(gb_ref[:, far], other_ref[...])
     for s in reversed(range(SUB)):
         r = slice(s * Q, (s + 1) * Q)
         square = jnp.zeros((Q, W), f32)
@@ -393,7 +426,7 @@
         low_ref[...] = state_ref[...].astype(bf16)
 
 
-def open_back(g, w, y, z, x, bc, cum, tok, gain, e2):
+def open_back(core, g, mine, other, y, z, x, bc, cum, tok, gain, e2):
     t = x.shape[0]
     n = t // TT
 
@@ -404,8 +437,8 @@
         open_back_kernel,
         grid=(n,),
         in_specs=[
-            turned(D), full((E, D)), turned(E), turned(E), turned(E), turned(2 * N),
-            turned(128), turned(128), full((1, E)), full((256, E)),
+            SMEM, turned(D), full((E, HD)), full((E, HD)), turned(E), turned(E), turned(E),
+            turned(2 * N), turned(128), turned(128), full((1, E)), full((256, E)),
         ],
         out_specs=[turned(E), turned(E), turned(D), full((8, E)), full((N, E))],
         out_shape=[
@@ -417,11 +450,13 @@
         ],
         scratch_shapes=[pltpu.VMEM((TT, E), f32), pltpu.VMEM((N, E), f32)],
         compiler_params=params(),
+        cost_estimate=cost(20),
         name="open_back",
-    )(g, w, y, z, x, bc, cum, tok, gain, e2)
+    )(core, g, mine, other, y, z, x, bc, cum, tok, gain, e2)
 
 
 def within_back_kernel(
+    pairs,
     x_ref, dy_ref, bc_ref, dt_ref, cum_ref, cumt_ref, tok_ref, doct_ref, hot_ref, sel_ref,
     dxdt_ref, dbc_ref, cross_ref,
 ):
@@ -440,8 +475,8 @@
         grad_scores = jnp.zeros((Q, Q), f32)
         by_source = jnp.zeros((Q, 128), f32)
         by_target = jnp.zeros((HP, Q), f32)
-        for p in range(PAIRS):
-            at = slice(p * 128, (p + 1) * 128)
+        for p in pairs:
+            at = slice((p - pairs[0]) * 128, (p - pairs[0] + 1) * 128)
             xp = x_ref[r, at]
             dyp = dy_ref[r, at]
             dmix = nt(jnp.concatenate([xp * left, xp * right], axis=0), dyp)
@@ -456,8 +491,12 @@
                 flows.append((part * scores).astype(bf16))
             both = jnp.concatenate([dyp * left, dyp * right], axis=0)
             dxdt_ref[r, at] = nn(jnp.concatenate(mixes, axis=1), both).astype(bf16)
-            by_source = by_source + nn(jnp.concatenate(flows, axis=1), hot_ref[p])
-            by_target = by_target + nn(sel_ref[p], jnp.concatenate(flows, axis=0))
+            by_source = by_source + nn(
+                jnp.concatenate(flows, axis=1), hot_ref[p - pairs[0]]
+            )
+            by_target = by_target + nn(
+                sel_ref[p - pairs[0]], jnp.concatenate(flows, axis=0)
+            )
         low = grad_scores.astype(bf16)
         dbc_ref[r, :N] = nn(low, c_out)
         dbc_ref[r, N:] = tn(low, b_in)
@@ -467,24 +506,29 @@
         cross_ref[r, :] = nn_exact(suffix, target - by_source)
 
 
-def within_back(x, dy, bc, dt, cum, cumt, tok, doct, hot, sel):
+def within_back(x, dy, bc, dt, cum, cumt, tok, doct, hot, sel, part):
     t = x.shape[0]
+    size = PAIRS // 2
+    half = pl.BlockSpec((TT, HZ), lambda i: (i, part))
     return pl.pallas_call(
-        within_back_kernel,
+        partial(within_back_kernel, range(part * size, (part + 1) * size)),
         grid=(t // TT,),
         in_specs=[
-            rows(E), rows(E), rows(2 * N), rows(128), rows(128), cols(HP), rows(128), cols(8),
-            full(hot.shape), full(sel.shape),
-        ],
-        out_specs=[rows(E), rows(2 * N), rows(128)],
-        out_shape=[shape((t, E), bf16), shape((t, 2 * N), f32), shape((t, 128), f32)],
+            half, half, rows(2 * N), rows(128), rows(128), cols(HP), rows(128), cols(8),
+            pl.BlockSpec((size,) + hot.shape[1:], lambda i: (part, 0, 0)),
+            pl.BlockSpec((size,) + sel.shape[1:], lambda i: (part, 0, 0)),
+        ],
+        out_specs=[rows(HZ), rows(2 * N), rows(128)],
+        out_shape=[shape((t, HZ), bf16), shape((t, 2 * N), f32), shape((t, 128), f32)],
         compiler_params=params(),
+        cost_estimate=cost(12),
         name="within_back",
     )(x, dy, bc, dt, cum, cumt, tok, doct, hot, sel)
 
 
 def across_back_kernel(
-    x_ref, pre_ref, xc_ref, halo_ref, edge_ref, bc_ref, dy_ref, dxdt_ref, dbc_ref, cross_ref,
+    x_ref, pre_ref, xc_ref, halo_ref, edge_ref, bc_ref, dy_ref, dxdt0_ref, dxdt1_ref,
+    dbc0_ref, dbc1_ref, cross0_ref, cross1_ref,
     dt_ref, cum_ref, dtr_ref, tok_ref, prior_ref, last_ref, skip_ref, cw_ref, pv_ref, e2_ref,
     et_ref,
     dxc_ref, cacc_ref, hacc_ref, first_ref,
@@ -533,8 +577,8 @@
         )
         b_in = bc_ref[r, :N]
         c_out = bc_ref[r, N:]
-        grad_b = dbc_ref[r, :N]
-        grad_c = dbc_ref[r, N:]
+        grad_b = dbc0_ref[r, :N] + dbc1_ref[r, :N]
+        grad_c = dbc0_ref[r, N:] + dbc1_ref[r, N:]
         sums = jnp.zeros((3 * Q + 16, 128), f32)
         for b in range(E // W):
             at = slice(b * W, (b + 1) * W)
@@ -547,7 +591,8 @@
             dy = dy_ref[r, at].astype(f32)
             reach = nn(b_in, after_low) * grown[:Q]
             read = nn(c_out, before)
-            dxdt = dxdt_ref[r, at].astype(f32) + reach
+            near = (dxdt0_ref, dxdt1_ref)[b * W // HZ]
+            dxdt = near[r, b * W % HZ : b * W % HZ + W].astype(f32) + reach
             dyg = dy * grown[Q : 2 * Q]
             dyg_low = dyg.astype(bf16)
             joint = jnp.sum(after * before.astype(f32), axis=0, keepdims=True)
@@ -568,13 +613,15 @@
         through_silu(grad_b, r, slice(E, E + N))
         through_silu(grad_c, r, slice(E + N, CV))
         dlog = (
-            cross_ref[r, :]
+            cross0_ref[r, :]
+            + cross1_ref[r, :]
             + nn_exact(strict, sums[Q : 2 * Q] * dt)
             + nn_exact(suffix, sums[2 * Q : 3 * Q])
             + carried * sums[3 * Q : 3 * Q + 1]
         )
         draw = (sums[:Q] - rate * dlog) * sigmoid(dtr_ref[r, :] + pv_ref[0:1, :])
-        dxc_ref[r, CV:] = draw.astype(bf16)
+        dxc_ref[r, HX:CX] = draw.astype(bf16)
+        dxc_ref[r, CX + HX :] = draw.astype(bf16)
         hacc_ref[0:1, :] += jnp.sum(draw, axis=0, keepdims=True)
         hacc_ref[1:2, :] -= rate * jnp.sum(dt * dlog, axis=0, keepdims=True)
 
@@ -592,7 +639,8 @@
             cacc_ref[k : k + 1, at] += jnp.sum(
                 own * (ext[5 + k : 5 + k + TT, at] * masks[k]), axis=0, keepdims=True
             )
-        dxc_ref[:, at] = total.astype(bf16)
+        to = b * 128 + (128 if b * 128 >= HX else 0)
+        dxc_ref[:, to : to + 128] = total.astype(bf16)
 
     @pl.when(step == count - 1)
     def _():
@@ -600,8 +648,7 @@
 
 
 def across_back(
-    x, pre, xc, edge, bc, dy, dxdt, dbc, cross, dt, cum, dtr, tok, prior, last, skip, cw, pv, e2,
-    et,
+    x, pre, xc, edge, bc, dy, near0, near1, dt, cum, dtr, tok, prior, last, skip, cw, pv, e2, et
 ):
     t = x.shape[0]
     n = t // TT
@@ -615,13 +662,13 @@
         grid=(n,),
         in_specs=[
             turned(E), turned(CV), turned(CV), halo, full((8, CV)), turned(2 * N), turned(E),
-            turned(E), turned(2 * N), turned(128), turned(128), turned(128), turned(128),
-            turned(128), pl.BlockSpec((SUB, N, E), lambda i: (n - 1 - i, 0, 0)), full((N, E)),
+            turned(HZ), turned(HZ), turned(2 * N), turned(2 * N), turned(128), turned(128),
+            turned(128), turned(128), turned(128), turned(128), pl.BlockSpec((SUB, N, E), lambda i: (n - 1 - i, 0, 0)), full((N, E)),
             full((1, E)), full((8, CV)), full((8, 128)), full((256, E)), full((E, 128)),
         ],
-        out_specs=[turned(CX), full((8, CV)), full((8, 128)), full((8, CV))],
+        out_specs=[turned(2 * CX), full((8, CV)), full((8, 128)), full((8, CV))],
         out_shape=[
-            shape((t, CX), bf16),
+            shape((t, 2 * CX), bf16),
             shape((8, CV), f32),
             shape((8, 128), f32),
             shape((8, CV), f32),
@@ -632,21 +679,30 @@
             pltpu.VMEM((TT + 8, CV), f32),
         ],
         compiler_params=params(),
+        cost_estimate=cost(31),
         name="across_back",
     )(
-        x, pre, xc, xc, edge, bc, dy, dxdt, dbc, cross, dt, cum, dtr, tok, prior, last, skip, cw,
-        pv, e2, et,
+        x, pre, xc, xc, edge, bc, dy, near0[0], near1[0], near0[1], near1[1], near0[2], near1[2],
+        dt, cum, dtr, tok, prior, last, skip, cw, pv, e2, et,
     )
 
 
 def close_back_kernel(
-    dz_ref, dxc_ref, wz_ref, wx_ref, x_ref, gain_ref, g_ref, new_ref, acc_ref
+    core_ref, dz_ref, dxc_ref, zm_ref, zo_ref, xm_ref, xo_ref, x_ref, gain_ref, g_ref,
+    new_ref, acc_ref,
 ):
     @pl.when(pl.program_id(0) == 0)
     def _():
         acc_ref[...] = jnp.zeros_like(acc_ref)
 
-    dn = nt(dz_ref[...], wz_ref[...]) + nt(dxc_ref[...], wx_ref[...])
+    own_z, far_z = sides(core_ref, HZ)
+    own_x, far_x = sides(core_ref, CX)
+    dn = (
+        nt(dz_ref[:, own_z], zm_ref[...])
+        + nt(dz_ref[:, far_z], zo_ref[...])
+        + nt(dxc_ref[:, own_x], xm_ref[...])
+        + nt(dxc_ref[:, far_x][:, :HX], xo_ref[:, :HX])
+    )
     x = x_ref[...].astype(f32)
     scale = lax.rsqrt(jnp.mean(x * x, axis=-1, keepdims=True) + eps)
     acc_ref[0:1, :] += jnp.sum(dn * (x * scale), axis=0, keepdims=True)
@@ -655,19 +711,21 @@
     new_ref[...] = g_ref[...].astype(f32) + scale * pulled - x * (scale * scale * scale * mean)
 
 
-def close_back(dz, dxc, wz, wx, x, gain, g):
+def close_back(core, dz, dxc, zs, xs, x, gain, g):
     t = x.shape[0]
     return pl.pallas_call(
         close_back_kernel,
         grid=(t // TT,),
         in_specs=[
-            rows(E), rows(CX), full((D, E)), full((D, CX)), rows(D), full((1, D)), rows(D),
+            SMEM, rows(E), rows(2 * CX), full((D, HZ)), full((D, HZ)), full((D, CX)),
+            full((D, CX)), rows(D), full((1, D)), rows(D),
         ],
         out_specs=[rows(D), full((8, D))],
         out_shape=[shape((t, D), f32), shape((8, D), f32)],
         compiler_params=params(),
+        cost_estimate=cost(12),
         name="close_back",
-    )(dz, dxc, wz, wx, x, gain, g)
+    )(core, dz, dxc, *zs, *xs, x, gain, g)
 
 
 def passed_along(value, axis, steps):
@@ -685,18 +743,31 @@
     return [1 << k for k in range((lax.axis_size(axis) - 1).bit_length())]
 
 
-def all_states(packed):
+def all_states(packed, *beside):
     bits = bits_of("seq")
     half = E // 2
     sides = [(packed[:, :half], bits[1:] + bits[:1]), (packed[:, half:], bits[:0:-1] + bits[:1])]
     held = [value[None] for value, _ in sides]
     orders = [[0], [0]]
+    stages = []
     for k in range(len(bits)):
+        before = tuple(held)
         for side, (_, path) in enumerate(sides):
             came = swapped(held[side], "seq", path[k])
             held[side] = jnp.concatenate([held[side], came])
             orders[side] = orders[side] + [o ^ path[k] for o in orders[side]]
-    return held, orders
+        fill = [make(before) for make in beside[k : k + 1]]
+        held = list(together(*held, *fill))[:2]
+        stages.append(tuple(held))
+    return held, orders, stages
+
+
+def together(*values):
+    return lax.optimization_barrier(values)
+
+
+def tied(value, *others):
+    return lax.optimization_barrier((value,) + others)[0]
 
 
 def decay_table(held, order):
@@ -729,24 +800,73 @@
     return jnp.concatenate(sides, axis=1)
 
 
+def cut(value, width, side):
+    return lax.dynamic_slice_in_dim(value, side * width, width, 1)
+
+
 def gathered(piece):
-    seqs, parts = lax.axis_size("seq"), lax.axis_size("fsdp")
-    height, width = piece.shape
-    mine = height // seqs
-    own = lax.dynamic_slice_in_dim(piece, lax.axis_index("seq") * mine, mine, 0)
-    pieces = lax.all_gather(own, ("seq", "fsdp"))
-    pieces = pieces.reshape(seqs, parts, mine, width).transpose(1, 0, 2, 3)
-    return pieces.reshape(parts * height, width)
-
-
-def reduced(value):
-    seqs, parts = lax.axis_size("seq"), lax.axis_size("fsdp")
-    height, width = value.shape
-    value = value.astype(bf16).reshape(parts, height // parts, width)
-    value = lax.psum_scatter(value, "seq", scatter_dimension=1, tiled=True)
-    value = lax.psum_scatter(value, "fsdp", scatter_dimension=0, tiled=True)
-    value = lax.all_gather(value, "seq", axis=1, tiled=True)
-    return value[0].astype(f32)
+    return lax.all_gather(piece, "fsdp", axis=0, tiled=True)
+
+
+def both_cores(mine):
+    return mine, swapped(mine, "seq", 1)
+
+
+def far_product(left, right, width, core):
+    return tn(left, cut(right, width, 1 - core)).astype(bf16)
+
+
+def half_product(left, right, width, core, there):
+    came = swapped(there, "seq", 1)
+    return (tn(left, cut(right, width, core)) + came.astype(f32)).astype(bf16)
+
+
+def part_sum(value):
+    return lax.psum_scatter(value, "fsdp", scatter_dimension=0, tiled=True)
+
+
+def added(value, bit):
+    return (value.astype(f32) + swapped(value, "seq", bit).astype(f32)).astype(bf16)
+
+
+def plane_step(first, second, k):
+    bits = bits_of("seq")[1:]
+    return added(first, bits[k]), added(second, bits[-1 - k])
+
+
+def plane_sum(first, second):
+    for k in range(len(bits_of("seq")) - 1):
+        first, second = plane_step(first, second, k)
+    return first, second
+
+
+def swapped_pair(value):
+    return value, swapped(value, "seq", 1)
+
+
+def big_of(mine, other, core):
+    def both(low, high):
+        return ordered(mine[:, low:high], other[:, low:high], core)
+
+    at = HZ + 2 * HD
+    gate, conv = both(0, HZ), both(at, at + HX)
+    tops, bottoms = both(HZ, HZ + HD), both(HZ + HD, at)
+    steps = mine[:, at + HX : at + HX + H]
+    return (
+        jnp.concatenate([gate, conv, steps], axis=1).astype(f32),
+        jnp.concatenate([tops, bottoms]).astype(f32),
+    )
+
+
+def plane_sum_rows(value):
+    half = value.shape[0] // 2
+    return jnp.concatenate(plane_sum(value[:half], value[half:]))
+
+
+def ordered(mine, other, core):
+    return jnp.concatenate(
+        [jnp.where(core == 0, mine, other), jnp.where(core == 0, other, mine)], axis=1
+    )
 
 
 def reduced_small(value):
@@ -840,17 +960,26 @@
         taps = found[0].reshape(parts, K, CV // parts).transpose(1, 0, 2).reshape(K, CV)
         return [taps] + [v.reshape(-1) for v in found[1:]]
 
-    weights = [
-        (
-            gathered(jnp.pad(entering_projection[i][:, E:], ((0, 0), (0, 128 - H)))),
-            gathered(entering_projection[i][:, :E]),
-            gathered(exit_projection[i]),
-        )
-        for i in range(layers)
-    ]
+    core = lax.axis_index("seq") & 1
+    cores = jnp.reshape(core, (1,)).astype(jnp.int32)
+    bits = bits_of("seq")
+    found = []
+    for i in range(layers):
+        w = entering_projection[i]
+        steps = jnp.pad(w[:, E + CV :], ((0, 0), (0, 128 - H)))
+        piece = jnp.concatenate([cut(w[:, E : E + CV], HX, core), steps], axis=1)
+        gate, out = cut(w[:, :E], HZ, core), cut(exit_projection[i], HD, core)
+        if i == 0:
+            found.append((gathered(piece), gathered(gate), gathered(out)))
+        else:
+            rest = out.shape[0] // 2
+            both = gathered(jnp.concatenate([gate, out[:rest], out[rest:]], axis=1))
+            found.append((gathered(piece), both, None))
+    weights = []
     kept = []
     for i in range(layers):
-        wx, wz, w_out = weights[i]
+        wx = found[i][0]
+        wx = both_cores(wx if i == 0 else tied(wx, current))
         taps, shifts, strides, rates, bypass, gain_in, gain_out = small_of(i)
         cw = jnp.concatenate([taps, shifts[None], jnp.zeros((3, CV), f32)])
         pv = jnp.concatenate(
@@ -858,18 +987,26 @@
         )
         skip = jnp.repeat(bypass, P_SIZE)[None]
         gain_in, gain_out = gain_in[None], gain_out[None]
-        normed, xc, dtr = project(current, gain_in, wx)
+        normed, xc, dtr = project(cores, current, gain_in, *wx)
         edge = passed_along(xc[t - (K - 1) :], "seq", 1).astype(f32)
         edge = jnp.concatenate([jnp.zeros((8 - (K - 1), CV), f32), edge])
         pre, x, bc, dt, cum, cumt, dtt, packed = prepare(xc, edge, cw, dtr, spike, tok, pv, e2)
-        held, orders = all_states(packed)
         yi = within(x, bc, cum, cumt, dtt, tok, doct)
-        z = project_gate(normed, wz)
+        held, orders, stages = all_states(packed, lambda before: yi)
+        if i == 0:
+            wz, wo = tied(found[i][1], x), tied(found[i][2], *stages[1])
+        else:
+            both = tied(found[i][1], *stages[1])
+            wz, wo = both[:, :HZ], both[:, HZ:].reshape(parts, -1, 2, HD)
+            wo = wo.transpose(0, 2, 1, 3).reshape(E, HD)
+        wz, wo = both_cores(wz), both_cores(wo)
+        weights.append((wx, wz, wo))
+        z = project_gate(cores, tied(normed, *stages[0]), *wz)
         logs = decay_table(held[0], orders[0])
         incoming = joined_states(held, orders, logs, True)
         out_type = bf16 if i == layers - 1 else f32
         y, low, new, prior = across(
-            yi, x, bc, dt, cum, tok, z, incoming, skip, gain_out, w_out, current, e2, out_type
+            cores, yi, x, bc, dt, cum, tok, z, incoming, skip, gain_out, *wo, current, e2, out_type
         )
         kept.append(
             (current, normed, z, xc, dtr, edge, pre, x, bc, dt, cum, cumt, logs, y, low, prior,
@@ -878,50 +1015,89 @@
         current = new
     grad = upstream_gradient[0]
     results = [None] * layers
+    waiting = {}
     for i in reversed(range(layers)):
-        wx, wz, w_out = weights[i]
+        wx, wz, wo = weights[i]
         (source, normed, z, xc, dtr, edge, pre, x, bc, dt, cum, cumt, logs, y, low, prior,
          cw, pv, skip, gain_in, gain_out) = kept[i]
         dy, dz, gb, acc, state = open_back(
-            grad, w_out, y, z, x, bc, cum, tok, gain_out, e2
+            cores, grad, *wo, y, z, x, bc, cum, tok, gain_out, e2
         )
-        held, orders = all_states(state)
-        grad_out = reduced(tn(low, gb))
-        grad_gate = reduced(tn(normed, dz))
-        dxdt, dbc, cross = within_back(x, dy, bc, dt, cum, cumt, tok, doct, hot, sel)
+        far_gate = far_product(normed, dz, HZ, core)
+        far_out = far_product(low, gb, HD, core)
+        shared = (bc, dt, cum, cumt, tok, doct, hot, sel)
+        near0 = within_back(tied(x, far_gate, far_out), dy, *shared, 0)
+        top = waiting.get(i + 1)
+        near1 = []
+
+        def second_half(before):
+            near1.extend(within_back(tied(x, near0[2], *before), dy, *shared, 1))
+            return near1[2]
+
+        held, orders, stages = all_states(state, lambda before: near0[2], second_half)
+        half_gate = half_product(normed, tied(dz, near1[2]), HZ, core, far_gate)
+        half_out = half_product(low, tied(gb, near1[2]), HD, core, far_out)
+        grad_out, grad_gate = part_sum(half_out), part_sum(half_gate)
         later = joined_states(held, orders, logs, False)
+        later = tied(later, half_out, half_gate)
+        if top is not None:
+            sums = plane_step(*tied(top, *stages[0]), 0)
         dxc, cacc, hacc, first = across_back(
-            x, pre, xc, edge, bc, dy, dxdt, dbc, cross, dt, cum, dtr, tok, prior, later, skip, cw,
-            pv, e2, et,
+            x, pre, xc, edge, bc, dy, near0, near1, dt, cum, dtr, tok, prior, later, skip, cw, pv, e2, et
         )
+        if top is not None:
+            first, sums = together(first, sums)
+        first, grad_out = together(first, grad_out)
         masked = [first[: K - 1] * tok[: K - 1, k : k + 1] for k in range(K - 1)]
         borrowed = jnp.stack(
             [sum(cw[k] * masked[k][e - k] for k in range(e + 1)) for e in range(K - 1)]
         )
         back = passed_along(borrowed, "seq", -1)
-        mended = (dxc[t - (K - 1) :, :CV].astype(f32) + back).astype(bf16)
-        dxc = dxc.at[t - (K - 1) :, :CV].set(mended)
-        grad_conv = reduced(tn(normed, dxc))
-        grad, nacc = close_back(dz, dxc, wz, wx, source, gain_in, grad)
-        big = (jnp.concatenate([grad_gate, grad_conv[:, : CV + H]], axis=1), grad_out)
+        gap = jnp.zeros((K - 1, 128), f32)
+        back = jnp.concatenate([back[:, :HX], gap, back[:, HX:], gap], axis=1)
+        mended = (dxc[t - (K - 1) :].astype(f32) + back).astype(bf16)
+        dxc = dxc.at[t - (K - 1) :].set(mended)
+        dxc, grad_gate = together(dxc, grad_gate)
+        far_conv = far_product(normed, dxc, CX, core)
+        conv_half = half_product(normed, dxc, CX, core, far_conv)
+        rest = grad_out.shape[0] // 2
+        grad_out = jnp.concatenate([grad_out[:rest], grad_out[rest:]], axis=1)
+        if i == 0:
+            early = plane_sum(*tied((grad_gate, grad_out), far_conv))
+            grad = tied(grad, conv_half, *early)
+            early = swapped_pair(jnp.concatenate(early, axis=1))
+            if top is not None:
+                for k in range(1, len(bits) - 1):
+                    sums = plane_step(*sums, k)
+                results[i + 1] = results[i + 1] + (swapped_pair(jnp.concatenate(sums)),)
+        grad, nacc = close_back(cores, dz, dxc, wz, wx, source, gain_in, grad)
+        grad_conv = part_sum(conv_half)
+        if i > 0:
+            grad = tied(grad, conv_half)
+            value = jnp.concatenate([grad_gate, grad_out, grad_conv], axis=1)
+            half = value.shape[0] // 2
+            waiting[i] = (value[:half], value[half:])
         tiny = [
             cacc[:K], cacc[K], hacc[0, :H], hacc[1, :H],
             jnp.sum(acc[1].reshape(H, P_SIZE), axis=1), nacc[0], acc[0],
         ]
-        results[i] = (big, tiny)
+        results[i] = (tiny,)
     packed = []
     for i in range(layers):
-        tiny = results[i][1]
+        tiny = results[i][0]
         taps = tiny[0].reshape(K, parts, CV // parts).transpose(1, 0, 2).reshape(parts, -1)
         packed.append(jnp.concatenate([taps] + [v.reshape(parts, -1) for v in tiny[1:]], axis=1))
     mine = reduced_small(jnp.stack(packed, axis=1))
+    late = swapped_pair(plane_sum_rows(grad_conv))
+    results[0] += (tuple(jnp.concatenate(v, axis=1) for v in zip(early, late)),)
+    bigs = [big_of(*results[i][1], core) for i in range(layers)]
     smalls, at = [], 0
     for size in SMALL:
         width = size // parts
         smalls.append(mine[:, at : at + width])
         at += width
     smalls[0] = smalls[0].reshape(layers, K, CV // parts)
-    bigs = [jnp.stack([results[i][0][j] for i in range(layers)]) for j in range(2)]
+    bigs = [jnp.stack([v[j] for v in bigs]) for j in range(2)]
     return (current[None], grad[None], *bigs, *smalls)
 
 

time: 935 us -> 669 us (0.72)
  waiting for transfers between devices: 337 us -> 117 us
  blocking collectives: 86.3 us -> 11.2 us
  local copies, waits for them, and re-layouts: 88.9 us -> 63.1 us
  Pallas kernels: 280 us -> 295 us
  starting transfers between devices: 53.1 us -> 68 us
  matrix products: 30.1 us -> 44.2 us
  other arithmetic: 34.7 us -> 45.5 us
    all_gather x6 -> x5, waiting for transfers between devices: 171 us -> 19.6 us  [gathered(): return lax.all_gather(piece, 'fsdp', axis=0, tiled=True)]
    all_gather x6 -> x0, blocking collectives: 75.5 us -> none  [reduced(): value = lax.all_gather(value, 'seq', axis=1, tiled=True)]
    unnamed x24 -> x11, waiting for transfers between devices: 51.6 us -> 0.18 us
    unnamed x88 -> x124, local copies, waits for them, and re-layouts: 26 us -> 3.12 us
    reduce_scatter x6, waiting for transfers between devices: 33.1 us -> 11.5 us  [part_sum(): return lax.psum_scatter(value, 'fsdp', scatter_dimension=0, tiled=True)]
    reshape x6 -> x1, local copies, waits for them, and re-layouts: 20.4 us -> 0.29 us  [local(): wz, wo = (both[:, :HZ], both[:, HZ:].reshape(parts, -1, 2, HD))]
    pallas_call x12 -> x14, Pallas kernels: 172 us -> 186 us  [the longest x4 55.8 us: within_back(): pl.pallas_call(partial(within_back_kernel, range(part * size, (part + 1)...]
    dot_general x6 -> x12, matrix products: 30.1 us -> 44.2 us  [tn(): lax.dot_general(a, b, (((0,), (0,)), ((), ())), preferred_element_type=f32)]
  transfers between devices with their start and end apart: 52 -> 72, of which waited for: 29 -> 25; matrix products, arithmetic and copies ran while one was open for 15% -> 18% of each run, Pallas kernels for 26% -> 39%
where the time goes in v2:
time: 669 us; the launch traced here: 659 us
  Pallas kernels  295 us (44%)
  waiting for transfers between devices  117 us (17%)
  starting transfers between devices  68 us (10%)
  local copies, waits for them, and re-layouts  63.1 us (9%)
  other arithmetic  45.5 us (7%)
  matrix products  44.2 us (7%)
  between operations  15.8 us (2%)
  blocking collectives  11.2 us (2%)
    ppermute x56, waiting for transfers between devices, swapped(): lax.ppermute(value, axis, [(source, source ^ bit) for source in range(cou...  81 us
    pallas_call x2, Pallas kernels, across_back(): pl.pallas_call(across_back_kernel, grid=(n,), in_specs=[turned(E), turned...  63.2 us
    pallas_call x4, Pallas kernels, within_back(): pl.pallas_call(partial(within_back_kernel, range(part * size, (part + 1)...  55.8 us
    ppermute x56, starting transfers between devices, swapped(): lax.ppermute(value, axis, [(source, source ^ bit) for source in range(cou...  49.9 us
    dot_general x12, matrix products, tn(): lax.dot_general(a, b, (((0,), (0,)), ((), ())), preferred_element_type=f32)  44.2 us
    pallas_call x2, Pallas kernels, open_back(): pl.pallas_call(open_back_kernel, grid=(n,), in_specs=[SMEM, turned(D), fu...  41.8 us
    pallas_call x2, Pallas kernels, across(): pl.pallas_call(across_kernel, grid=(t // TT,), in_specs=[SMEM, rows(E), r...  34.1 us
    pallas_call x2, Pallas kernels, prepare(): pl.pallas_call(prepare_kernel, grid=(t // TT,), in_specs=[rows(CV), full(...  30 us
  transfers between devices with their start and end apart: 72, of which 25 were waited for; matrix products, arithmetic and copies ran while one was open for 18% of the time, Pallas kernels for 39%

profile of v2, /device:TPU:1, one launch (start us, length us, event | category | flops | bytes accessed | tf_op | source)
XLA Modules:
  0.0 659.2 jit_solution(4918476355715545832)
XLA Ops:
  11.3 4.5 collective-permute-start.2
  19.1 11.2 %all-gather.2 = bf16[4,2,2834]{2,1,0:T(2,128)(2,1)S(1)} all-gather(bf16[1,2,2834]{2,1,0:T(2,128)(2,1)S(1)} %bitcast.317), channel_id=2, replica_groups=mesh['seq'=8,'fsdp'=4] {'fsdp'}, dimensions={0}, use_global_device_ids=true | all-gather | bytes 56680 | tf_op jit(solution)/shard_map/all_gather | solution.py:952
  31.9 18.4 %all-gather.9.cloned.1.call-done.mine_ref.xm_ref = bf16[768,1024]{1,0:T(8,128)(2,1)} async-done(((bf16[192,1024]{1,0:T(8,128)(2,1)}), bf16[768,1024]{1,0:T(8,128)(2,1)}) %all-gather.9.cloned.1.call-update) | async-done | bytes 1572880 | tf_op jit(solution)/shard_map/all_gather | solution.py:808
  54.8 8.0 %project.2 = (bf16[1024,768]{1,0:T(8,128)(2,1)}, bf16[1024,1792]{1,0:T(8,128)(2,1)}, f32[1024,128]{1,0:T(8,128)}) custom-call(s32[1]{0:T(128)} %bitcast.core_ref, bf16[1024,768]{1,0:T(8,128)(2,1)} %bitcast.338, f32[1,768]{1,0:T(1,128)} %broadcast_in_dim_reshape_squeeze.18.gain_ref, bf16[768,1024]{1,0:T(8,128)(2,1)} %all-gather.9.cloned.1.call-done.mine_ref.xm_ref, ...), custom_call_target="tpu_custom_call" | custom-call | flops 8000000000 | bytes 24000000 | tf_op jit(solution)/shard_map/project/pallas_call | solution.py:130
  68.5 15.0 %prepare.2 = (bf16[1024,1792]{1,0:T(8,128)(2,1)}, bf16[1024,1536]{1,0:T(8,128)(2,1)}, bf16[1024,256]{1,0:T(8,128)(2,1)}, f32[1024,128]{1,0:T(8,128)}, f32[1024,1...) custom-call(bf16[1024,1792]{1,0:T(8,128)(2,1)} %get-tuple-element.156.xc_ref.halo_ref, ...), custom_call_target="tpu_custom_call" | custom-call | flops 15000000512 | bytes 45000000 | tf_op jit(solution)/shard_map/prepare/pallas_call | solution.py:230
  88.8 7.8 %within.2.yi_ref = bf16[1024,1536]{1,0:T(8,128)(2,1)} custom-call(bf16[1024,1536]{1,0:T(8,128)(2,1)} %get-tuple-element.239.x_ref, bf16[1024,256]{1,0:T(8,128)(2,1)} %get-tuple-element.159.bc_ref, f32[1024,128]{1,0:T(8,128)} %get-tuple-element.160.cum_ref, f32[32,1024]{1,0:T(8,128)} %get-tuple-element.161.cumt_ref, f32[32,1024]{1,0:T(8,128)} %get-tuple-element.162.dtt_ref, ...), custom_call_target="tpu_custom_call" | custom-call | flops 8000000000 | bytes 24000000 | tf_op jit(solution)/shard_map/within/pallas_call | solution.py:284
  101.1 7.6 %collective-permute-done.7 = bf16[2,144,768]{2,1,0:T(8,128)(2,1)S(1)} collective-permute-done((bf16[2,144,768]{2,1,0:T(8,128)(2,1)S(1)}, bf16[2,144,768]{2,1,0:T(8,128)(2,1)S(1)}, u32[]{:S(2)}, u32[]{:S(2)}) %collective-permute-start.7) | collective-permute-done | bytes 442400 | tf_op jit(solution)/shard_map/ppermute | solution.py:739
  108.8 3.2 collective-permute-done.6
  114.2 6.3 project_gate.2.z_ref
  131.5 17.1 %across.2 = (bf16[1024,1536]{1,0:T(8,128)(2,1)}, bf16[1024,1536]{1,0:T(8,128)(2,1)}, f32[1024,768]{1,0:T(8,128)}, bf16[8,128,1536]{2,1,0:T(8,128)(2,1)}) custom-call(s32[1]{0:T(128)} %bitcast.core_ref, bf16[1024,1536]{1,0:T(8,128)(2,1)} %within.2.yi_ref, bf16[1024,1536]{1,0:T(8,128)(2,1)} %get-tuple-element.239.x_ref, ...), custom_call_target="tpu_custom_call" | custom-call | flops 16000000000 | bytes 48000000 | tf_op jit(solution)/shard_map/across/pallas_call | solution.py:350
  155.1 8.4 %project.3 = (bf16[1024,768]{1,0:T(8,128)(2,1)}, bf16[1024,1792]{1,0:T(8,128)(2,1)}, f32[1024,128]{1,0:T(8,128)}) custom-call(s32[1]{0:T(128)} %bitcast.core_ref, f32[1024,768]{1,0:T(8,128)} %get-tuple-element.175.x_ref.res_ref, f32[1,768]{1,0:T(1,128)} %broadcast_in_dim_reshape_squeeze.21.gain_ref, ...), custom_call_target="tpu_custom_call" | custom-call | flops 8000000000 | bytes 24000000 | tf_op jit(solution)/shard_map/project/pallas_call | solution.py:130
  164.2 3.5 collective-permute-start.12
  169.0 15.0 %prepare.3 = (bf16[1024,1792]{1,0:T(8,128)(2,1)}, bf16[1024,1536]{1,0:T(8,128)(2,1)}, bf16[1024,256]{1,0:T(8,128)(2,1)}, f32[1024,128]{1,0:T(8,128)}, f32[1024,1...) custom-call(bf16[1024,1792]{1,0:T(8,128)(2,1)} %get-tuple-element.177.xc_ref.halo_ref, ...), custom_call_target="tpu_custom_call" | custom-call | flops 15000000512 | bytes 45000000 | tf_op jit(solution)/shard_map/prepare/pallas_call | solution.py:230
  186.5 7.8 %within.3.yi_ref = bf16[1024,1536]{1,0:T(8,128)(2,1)} custom-call(bf16[1024,1536]{1,0:T(8,128)(2,1)} %get-tuple-element.208.x_ref, bf16[1024,256]{1,0:T(8,128)(2,1)} %get-tuple-element.180.bc_ref, f32[1024,128]{1,0:T(8,128)} %get-tuple-element.181.cum_ref, f32[32,1024]{1,0:T(8,128)} %get-tuple-element.182.cumt_ref, f32[32,1024]{1,0:T(8,128)} %get-tuple-element.183.dtt_ref, ...), custom_call_target="tpu_custom_call" | custom-call | flops 8000000000 | bytes 24000000 | tf_op jit(solution)/shard_map/within/pallas_call | solution.py:284
  196.1 7.1 %collective-permute-done.16 = bf16[2,144,768]{2,1,0:T(8,128)(2,1)S(1)} collective-permute-done((bf16[2,144,768]{2,1,0:T(8,128)(2,1)S(1)}, bf16[2,144,768]{2,1,0:T(8,128)(2,1)S(1)}, u32[]{:S(2)}, u32[]{:S(2)}) %collective-permute-start.16) | collective-permute-done | bytes 442400 | tf_op jit(solution)/shard_map/ppermute | solution.py:739
  205.5 3.9 collective-permute-start.19
  226.2 6.4 project_gate.3.z_ref
  232.6 17.0 %across.3 = (bf16[1024,1536]{1,0:T(8,128)(2,1)}, bf16[1024,1536]{1,0:T(8,128)(2,1)}, bf16[1024,768]{1,0:T(8,128)(2,1)}, bf16[8,128,1536]{2,1,0:T(8,128)(2,1)}) custom-call(s32[1]{0:T(128)} %bitcast.core_ref, bf16[1024,1536]{1,0:T(8,128)(2,1)} %within.3.yi_ref, bf16[1024,1536]{1,0:T(8,128)(2,1)} %get-tuple-element.208.x_ref, ...), custom_call_target="tpu_custom_call" | custom-call | flops 16000000000 | bytes 48000000 | tf_op jit(solution)/shard_map/across/pallas_call | solution.py:350
  249.6 21.0 %open_back.2 = (bf16[1024,1536]{1,0:T(8,128)(2,1)}, bf16[1024,1536]{1,0:T(8,128)(2,1)}, bf16[1024,768]{1,0:T(8,128)(2,1)}, f32[8,1536]{1,0:T(8,128)}, bf16[128,1536]{1,0:T(8,128)(2,1)}) custom-call(s32[1]{0:T(128)} %bitcast.core_ref, bf16[1024,768]{1,0:T(8,128)(2,1)} %bitcast.336, bf16[1536,384]{1,0:T(8,128)(2,1)} %bitcast.67.mine_ref, ...), custom_call_target="tpu_custom_call" | custom-call | flops 20000000000 | bytes 60000000 | tf_op jit(solution)/shard_map/open_back/pallas_call | solution.py:436
  273.1 3.1 convolution_convert_fusion.1
  279.8 13.7 %within_back.4 = (bf16[1024,768]{1,0:T(8,128)(2,1)}, f32[1024,256]{1,0:T(8,128)}, f32[1024,128]{1,0:T(8,128)}) custom-call(bf16[1024,1536]{1,0:T(8,128)(2,1)} %get-tuple-element.208.x_ref, bf16[1024,1536]{1,0:T(8,128)(2,1)} %get-tuple-element.199.dy_ref, bf16[1024,256]{1,0:T(8,128)(2,1)} %get-tuple-element.180.bc_ref, ...), custom_call_target="tpu_custom_call" | custom-call | flops 12000000000 | bytes 36000000 | tf_op jit(solution)/shard_map/within_back/pallas_call | solution.py:513
  293.6 14.3 %within_back.5 = (bf16[1024,768]{1,0:T(8,128)(2,1)}, f32[1024,256]{1,0:T(8,128)}, f32[1024,128]{1,0:T(8,128)}) custom-call(bf16[1024,1536]{1,0:T(8,128)(2,1)} %get-tuple-element.208.x_ref, bf16[1024,1536]{1,0:T(8,128)(2,1)} %get-tuple-element.199.dy_ref, bf16[1024,256]{1,0:T(8,128)(2,1)} %get-tuple-element.180.bc_ref, ...), custom_call_target="tpu_custom_call" | custom-call | flops 12000000000 | bytes 36000000 | tf_op jit(solution)/shard_map/within_back/pallas_call | solution.py:513
  307.9 4.7 fusion
  314.6 9.1 %collective-permute-done.24 = bf16[2,128,768]{2,1,0:T(8,128)(2,1)S(1)} collective-permute-done((bf16[2,128,768]{2,1,0:T(8,128)(2,1)S(1)}, bf16[2,128,768]{2,1,0:T(8,128)(2,1)S(1)}, u32[]{:S(2)}, u32[]{:S(2)}) %collective-permute-start.24) | collective-permute-done | bytes 393248 | tf_op jit(solution)/shard_map/ppermute | solution.py:739
  329.0 4.3 add_convert_fusion.3
  337.6 31.6 %across_back.2 = (bf16[1024,2048]{1,0:T(8,128)(2,1)}, f32[8,1792]{1,0:T(8,128)}, f32[8,128]{1,0:T(8,128)}, f32[8,1792]{1,0:T(8,128)}) custom-call(bf16[1024,1536]{1,0:T(8,128)(2,1)} %get-tuple-element.208.x_ref, bf16[1024,1792]{1,0:T(8,128)(2,1)} %get-tuple-element.198.pre_ref, bf16[1024,1792]{1,0:T(8,128)(2,1)} %get-tuple-element.177.xc_ref.halo_ref, ...), custom_call_target="tpu_custom_call" | custom-call | flops 31000000512 | bytes 93000000 | tf_op jit(solution)/shard_map/across_back/pallas_call | solution.py:660
  378.4 4.6 fusion.10
  383.0 12.6 %close_back.2 = (f32[1024,768]{1,0:T(8,128)}, f32[8,768]{1,0:T(8,128)}) custom-call(s32[1]{0:T(128)} %bitcast.core_ref, bf16[1024,1536]{1,0:T(8,128)(2,1)} %get-tuple-element.219.dz_ref, bf16[1024,2048]{1,0:T(8,128)(2,1)} %scatter.6.dxc_ref, bf16[768,768]{1,0:T(8,128)(2,1)} %get-tuple-element.368.mine_ref.zm_ref, ...), custom_call_target="tpu_custom_call" | custom-call | flops 12000000000 | bytes 36000000 | tf_op jit(solution)/shard_map/close_back/pallas_call | solution.py:716
  398.6 20.9 %open_back.3 = (bf16[1024,1536]{1,0:T(8,128)(2,1)}, bf16[1024,1536]{1,0:T(8,128)(2,1)}, bf16[1024,768]{1,0:T(8,128)(2,1)}, f32[8,1536]{1,0:T(8,128)}, bf16[128,1536]{1,0:T(8,128)(2,1)}) custom-call(s32[1]{0:T(128)} %bitcast.core_ref, f32[1024,768]{1,0:T(8,128)} %get-tuple-element.265.g_ref, bf16[1536,384]{1,0:T(8,128)(2,1)} %bitcast.343, ...), custom_call_target="tpu_custom_call" | custom-call | flops 20000000000 | bytes 60000000 | tf_op jit(solution)/shard_map/open_back/pallas_call | solution.py:436
  422.8 3.1 convolution_convert_fusion
  429.3 13.7 %within_back.6 = (bf16[1024,768]{1,0:T(8,128)(2,1)}, f32[1024,256]{1,0:T(8,128)}, f32[1024,128]{1,0:T(8,128)}) custom-call(bf16[1024,1536]{1,0:T(8,128)(2,1)} %get-tuple-element.239.x_ref, bf16[1024,1536]{1,0:T(8,128)(2,1)} %get-tuple-element.230.dy_ref, bf16[1024,256]{1,0:T(8,128)(2,1)} %get-tuple-element.159.bc_ref, ...), custom_call_target="tpu_custom_call" | custom-call | flops 12000000000 | bytes 36000000 | tf_op jit(solution)/shard_map/within_back/pallas_call | solution.py:513
  443.1 14.1 %within_back.7 = (bf16[1024,768]{1,0:T(8,128)(2,1)}, f32[1024,256]{1,0:T(8,128)}, f32[1024,128]{1,0:T(8,128)}) custom-call(bf16[1024,1536]{1,0:T(8,128)(2,1)} %get-tuple-element.239.x_ref, bf16[1024,1536]{1,0:T(8,128)(2,1)} %get-tuple-element.230.dy_ref, bf16[1024,256]{1,0:T(8,128)(2,1)} %get-tuple-element.159.bc_ref, ...), custom_call_target="tpu_custom_call" | custom-call | flops 12000000000 | bytes 36000000 | tf_op jit(solution)/shard_map/within_back/pallas_call | solution.py:513
  457.3 4.0 fusion.1
  466.2 5.7 collective-permute-done.34
  477.3 4.7 add_convert_fusion.2
  486.9 31.6 %across_back.3 = (bf16[1024,2048]{1,0:T(8,128)(2,1)}, f32[8,1792]{1,0:T(8,128)}, f32[8,128]{1,0:T(8,128)}, f32[8,1792]{1,0:T(8,128)}) custom-call(bf16[1024,1536]{1,0:T(8,128)(2,1)} %get-tuple-element.239.x_ref, bf16[1024,1792]{1,0:T(8,128)(2,1)} %get-tuple-element.229.pre_ref, bf16[1024,1792]{1,0:T(8,128)(2,1)} %get-tuple-element.156.xc_ref.halo_ref, ...), custom_call_target="tpu_custom_call" | custom-call | flops 31000000512 | bytes 93000000 | tf_op jit(solution)/shard_map/across_back/pallas_call | solution.py:660
  520.1 10.4 %collective-permute-done.39 = bf16[96,2560]{1,0:T(8,128)(2,1)S(1)} collective-permute-done((bf16[96,2560]{1,0:T(8,128)(2,1)S(1)}, bf16[96,2560]{1,0:T(8,128)(2,1)S(1)}, u32[]{:S(2)}, u32[]{:S(2)}) %collective-permute-start.39) | collective-permute-done | bytes 491552 | tf_op jit(solution)/shard_map/ppermute | solution.py:739
  531.5 3.6 collective-permute-start.41
  540.3 4.6 fusion.13
  557.8 6.3 collective-permute-done.53
  564.2 8.3 %collective-permute-done.46 = bf16[192,768]{1,0:T(8,128)(2,1)S(1)} collective-permute-done((bf16[192,768]{1,0:T(8,128)(2,1)S(1)}, bf16[192,768]{1,0:T(8,128)(2,1)S(1)}, u32[]{:S(2)}, u32[]{:S(2)}) %collective-permute-start.46) | collective-permute-done | bytes 294944 | tf_op jit(solution)/shard_map/ppermute | solution.py:739
  582.7 3.0 add_convert_fusion
  585.8 12.4 %close_back.3 = (f32[1024,768]{1,0:T(8,128)}, f32[8,768]{1,0:T(8,128)}) custom-call(s32[1]{0:T(128)} %bitcast.core_ref, bf16[1024,1536]{1,0:T(8,128)(2,1)} %get-tuple-element.250.dz_ref, bf16[1024,2048]{1,0:T(8,128)(2,1)} %scatter.9.dxc_ref, bf16[768,768]{1,0:T(8,128)(2,1)} %all-gather.11.cloned.1.call-done.mine_ref.zm_ref, ...), custom_call_target="tpu_custom_call" | custom-call | flops 12000000000 | bytes 36000000 | tf_op jit(solution)/shard_map/close_back/pallas_call | solution.py:716
  600.3 8.6 %collective-permute-done.56 = f32[2,2,2834]{2,1,0:T(2,128)S(1)} collective-permute-done((f32[2,2,2834]{2,1,0:T(2,128)S(1)}, f32[2,2,2834]{2,1,0:T(2,128)S(1)}, u32[]{:S(2)}, u32[]{:S(2)}) %collective-permute-start.56) | collective-permute-done | bytes 45376 | tf_op jit(solution)/shard_map/ppermute | solution.py:739
  609.2 11.4 %reduce-scatter.17.cloned.1.call-done = bf16[192,1024]{1,0:T(8,128)(2,1)} async-done(((bf16[768,1024]{1,0:T(8,128)(2,1)}), bf16[192,1024]{1,0:T(8,128)(2,1)}) %reduce-scatter.17.cloned.1.call-update) | async-done | bytes 393232 | tf_op jit(solution)/shard_map/reduce_scatter | solution.py:825
  635.8 4.2 collective-permute-done.51
  640.0 4.9 collective-permute-start.52
  648.5 4.0 maximum_convert_fusion
  (516 shorter events, 176.7 us)
Async XLA Ops:
  7.2 43.1 %all-gather.9.cloned.1.call-start = ((), (), s32[]{:S(2)}) async-start(), calls=%async_computation.6 | async-start | bytes 1966080 | tf_op jit(solution)/shard_map/all_gather | solution.py:808
  10.3 75.7 %all-gather.11.cloned.1.call-start = ((), (), s32[]{:S(2)}) async-start(), calls=%async_computation.7 | async-start | bytes 1474560 | tf_op jit(solution)/shard_map/all_gather | solution.py:808
  11.1 102.7 %all-gather.17.cloned.1.call-start = ((), (), s32[]{:S(2)}) async-start(), calls=%async_computation.16 | async-start | bytes 1474560 | tf_op jit(solution)/shard_map/all_gather | solution.py:808
  11.3 43.3 %collective-permute-start.2 = (s32[3]{0:T(128)S(1)}, s32[3]{0:T(128)S(1)}, u32[]{:S(2)}, u32[]{:S(2)}) collective-permute-start(s32[3]{0:T(128)S(1)} %slice_bitcast_fusion.10), channel_id=1, source_target_pairs={{0,4},{4,8},{8,12},{12,16},{16,20},{20,24},{24,28},{1,5},{5,9},{9,... | collective-permute-start | bytes 44 | tf_op jit(solution)/shard_map/ppermute | solution.py:734
  18.8 131.2 %all-gather.13.cloned.1.call-start = ((), (), s32[]{:S(2)}) async-start(), calls=%async_computation.8 | async-start | bytes 1966080 | tf_op jit(solution)/shard_map/all_gather | solution.py:808
  84.6 12.0 %collective-permute-start.4 = (bf16[1,144,768]{2,1,0:T(8,128)(2,1)S(1)}, bf16[1,144,768]{2,1,0:T(8,128)(2,1)S(1)}, u32[]{:S(2)}, u32[]{:S(2)}) collective-permute-start(bf16[1,144,768]{2,1,0:T(8,128)(2,1)S(1)} %get-tuple-element.385), channel_id=1, source_target_pairs={{0,16},{4,20},{8,24},{12,28},{16,0},{20,4},{24,8},{28,12},{1,17},{... | collective-permute-start | bytes 663560 | tf_op jit(solution)/shard_map/ppermute | solution.py:739
  85.7 10.9 %collective-permute-start.3 = (bf16[1,144,768]{2,1,0:T(8,128)(2,1)S(1)}, bf16[1,144,768]{2,1,0:T(8,128)(2,1)S(1)}, u32[]{:S(2)}, u32[]{:S(2)}) collective-permute-start(bf16[1,144,768]{2,1,0:T(8,128)(2,1)S(1)} %get-tuple-element.386), channel_id=1, source_target_pairs={{0,8},{4,12},{8,0},{12,4},{16,24},{20,28},{24,16},{28,20},{1,9},{5... | collective-permute-start | bytes 663560 | tf_op jit(solution)/shard_map/ppermute | solution.py:739
  86.0 28.3 %collective-permute-start.5 = (bf16[768,768]{1,0:T(8,128)(2,1)}, bf16[768,768]{1,0:T(8,128)(2,1)}, u32[]{:S(2)}, u32[]{:S(2)}) collective-permute-start(bf16[768,768]{1,0:T(8,128)(2,1)} %all-gather.11.cloned.1.call-done.mine_ref.zm_ref), channel_id=1, source_target_pairs={{0,4},{4,0},{8,12},{12,8},{16,20},{20,16},{24,28},{28,24},{1,5},{5... | collective-permute-start | bytes 3538952 | tf_op jit(solution)/shard_map/ppermute | solution.py:739
  96.7 12.0 %collective-permute-start.7 = (bf16[2,144,768]{2,1,0:T(8,128)(2,1)S(1)}, bf16[2,144,768]{2,1,0:T(8,128)(2,1)S(1)}, u32[]{:S(2)}, u32[]{:S(2)}) collective-permute-start(bf16[2,144,768]{2,1,0:T(8,128)(2,1)S(1)} %pad_maximum_fusion.26), channel_id=1, source_target_pairs={{0,8},{4,12},{8,0},{12,4},{16,24},{20,28},{24,16},{28,20},{1,9},{5... | collective-permute-start | bytes 1327112 | tf_op jit(solution)/shard_map/ppermute | solution.py:739
  99.0 111.2 %all-gather.15.cloned.1.call-start = ((), (), s32[]{:S(2)}) async-start(), calls=%async_computation.9 | async-start | bytes 2949120 | tf_op jit(solution)/shard_map/all_gather | solution.py:808
  100.3 11.6 %collective-permute-start.6 = (bf16[2,144,768]{2,1,0:T(8,128)(2,1)S(1)}, bf16[2,144,768]{2,1,0:T(8,128)(2,1)S(1)}, u32[]{:S(2)}, u32[]{:S(2)}) collective-permute-start(bf16[2,144,768]{2,1,0:T(8,128)(2,1)S(1)} %pad_maximum_fusion.25), channel_id=1, source_target_pairs={{0,16},{4,20},{8,24},{12,28},{16,0},{20,4},{24,8},{28,12},{1,17},{... | collective-permute-start | bytes 1327112 | tf_op jit(solution)/shard_map/ppermute | solution.py:739
  113.1 8.9 %collective-permute-start.8 = (bf16[4,144,768]{2,1,0:T(8,128)(2,1)S(1)}, bf16[4,144,768]{2,1,0:T(8,128)(2,1)}, u32[]{:S(2)}, u32[]{:S(2)}) collective-permute-start(bf16[4,144,768]{2,1,0:T(8,128)(2,1)S(1)} %pad_maximum_fusion.10), channel_id=1, source_target_pairs={{0,4},{4,0},{8,12},{12,8},{16,20},{20,16},{24,28},{28,24},{1,5},{5... | collective-permute-start | bytes 2654216 | tf_op jit(solution)/shard_map/ppermute | solution.py:739
  113.8 17.7 %collective-permute-start.10 = (bf16[1536,384]{1,0:T(8,128)(2,1)}, bf16[1536,384]{1,0:T(8,128)(2,1)}, u32[]{:S(2)}, u32[]{:S(2)}) collective-permute-start(bf16[1536,384]{1,0:T(8,128)(2,1)} %bitcast.341), channel_id=1, source_target_pairs={{0,4},{4,0},{8,12},{12,8},{16,20},{20,16},{24,28},{28,24},{1,5},{5... | collective-permute-start | bytes 3538952 | tf_op jit(solution)/shard_map/ppermute | solution.py:739
  152.9 216.4 %reduce-scatter.7.cloned.1.call-start = ((), (), s32[]{:S(2)}) async-start(), calls=%async_computation.10 | async-start | bytes 1474560 | tf_op jit(solution)/shard_map/reduce_scatter | solution.py:825
  185.1 9.1 %collective-permute-start.14 = (bf16[1,144,768]{2,1,0:T(8,128)(2,1)S(1)}, bf16[1,144,768]{2,1,0:T(8,128)(2,1)S(1)}, u32[]{:S(2)}, u32[]{:S(2)}) collective-permute-start(bf16[1,144,768]{2,1,0:T(8,128)(2,1)S(1)} %get-tuple-element.383), channel_id=1, source_target_pairs={{0,16},{4,20},{8,24},{12,28},{16,0},{20,4},{24,8},{28,12},{1,17},{... | collective-permute-start | bytes 663560 | tf_op jit(solution)/shard_map/ppermute | solution.py:739
  194.4 8.9 %collective-permute-start.16 = (bf16[2,144,768]{2,1,0:T(8,128)(2,1)S(1)}, bf16[2,144,768]{2,1,0:T(8,128)(2,1)S(1)}, u32[]{:S(2)}, u32[]{:S(2)}) collective-permute-start(bf16[2,144,768]{2,1,0:T(8,128)(2,1)S(1)} %pad_maximum_fusion.28), channel_id=1, source_target_pairs={{0,8},{4,12},{8,0},{12,4},{16,24},{20,28},{24,16},{28,20},{1,9},{5... | collective-permute-start | bytes 1327112 | tf_op jit(solution)/shard_map/ppermute | solution.py:739
  205.5 9.6 %collective-permute-start.19 = (bf16[4,144,768]{2,1,0:T(8,128)(2,1)S(1)}, bf16[4,144,768]{2,1,0:T(8,128)(2,1)}, u32[]{:S(2)}, u32[]{:S(2)}) collective-permute-start(bf16[4,144,768]{2,1,0:T(8,128)(2,1)S(1)} %pad_maximum_fusion.13), channel_id=1, source_target_pairs={{0,4},{4,0},{8,12},{12,8},{16,20},{20,16},{24,28},{28,24},{1,5},{5... | collective-permute-start | bytes 2654216 | tf_op jit(solution)/shard_map/ppermute | solution.py:739
  213.0 13.2 %collective-permute-start.17 = (bf16[768,768]{1,0:T(8,128)(2,1)}, bf16[768,768]{1,0:T(8,128)(2,1)}, u32[]{:S(2)}, u32[]{:S(2)}) collective-permute-start(bf16[768,768]{1,0:T(8,128)(2,1)} %get-tuple-element.368.mine_ref.zm_ref), channel_id=1, source_target_pairs={{0,4},{4,0},{8,12},{12,8},{16,20},{20,16},{24,28},{28,24},{1,5},{5... | collective-permute-start | bytes 3538952 | tf_op jit(solution)/shard_map/ppermute | solution.py:739
  215.0 17.5 %collective-permute-start.20 = (bf16[1536,384]{1,0:T(8,128)(2,1)}, bf16[1536,384]{1,0:T(8,128)(2,1)}, u32[]{:S(2)}, u32[]{:S(2)}) collective-permute-start(bf16[1536,384]{1,0:T(8,128)(2,1)} %bitcast.67.mine_ref), channel_id=1, source_target_pairs={{0,4},{4,0},{8,12},{12,8},{16,20},{20,16},{24,28},{28,24},{1,5},{5... | collective-permute-start | bytes 3538952 | tf_op jit(solution)/shard_map/ppermute | solution.py:739
  271.6 21.9 %collective-permute-start.22 = (bf16[1,128,768]{2,1,0:T(8,128)(2,1)S(1)}, bf16[1,128,768]{2,1,0:T(8,128)(2,1)S(1)}, u32[]{:S(2)}, u32[]{:S(2)}) collective-permute-start(bf16[1,128,768]{2,1,0:T(8,128)(2,1)S(1)} %get-tuple-element.393), channel_id=1, source_target_pairs={{0,16},{4,20},{8,24},{12,28},{16,0},{20,4},{24,8},{28,12},{1,17},{... | collective-permute-start | bytes 589832 | tf_op jit(solution)/shard_map/ppermute | solution.py:739
  272.0 21.6 %collective-permute-start.21 = (bf16[1,128,768]{2,1,0:T(8,128)(2,1)S(1)}, bf16[1,128,768]{2,1,0:T(8,128)(2,1)S(1)}, u32[]{:S(2)}, u32[]{:S(2)}) collective-permute-start(bf16[1,128,768]{2,1,0:T(8,128)(2,1)S(1)} %get-tuple-element.394), channel_id=1, source_target_pairs={{0,8},{4,12},{8,0},{12,4},{16,24},{20,28},{24,16},{28,20},{1,9},{5... | collective-permute-start | bytes 589832 | tf_op jit(solution)/shard_map/ppermute | solution.py:739
  276.3 31.6 %collective-permute-start.27 = (bf16[1536,384]{1,0:T(8,128)(2,1)S(1)}, bf16[1536,384]{1,0:T(8,128)(2,1)S(1)}, u32[]{:S(2)}, u32[]{:S(2)}) collective-permute-start(bf16[1536,384]{1,0:T(8,128)(2,1)S(1)} %convolution_convert_fusion.1), channel_id=1, source_target_pairs={{0,4},{4,0},{8,12},{12,8},{16,20},{20,16},{24,28},{28,24},{1,5},{5... | collective-permute-start | bytes 3538952 | tf_op jit(solution)/shard_map/ppermute | solution.py:739
  312.7 65.7 %reduce-scatter.9.cloned.1.call-start = ((), (), s32[]{:S(2)}) async-start(), calls=%async_computation.11 | async-start | bytes 1474560 | tf_op jit(solution)/shard_map/reduce_scatter | solution.py:825
  312.7 10.9 %collective-permute-start.24 = (bf16[2,128,768]{2,1,0:T(8,128)(2,1)S(1)}, bf16[2,128,768]{2,1,0:T(8,128)(2,1)S(1)}, u32[]{:S(2)}, u32[]{:S(2)}) collective-permute-start(bf16[2,128,768]{2,1,0:T(8,128)(2,1)S(1)} %pad_maximum_fusion.30), channel_id=1, source_target_pairs={{0,8},{4,12},{8,0},{12,4},{16,24},{20,28},{24,16},{28,20},{1,9},{5... | collective-permute-start | bytes 1179656 | tf_op jit(solution)/shard_map/ppermute | solution.py:739
  313.1 15.9 %collective-permute-start.28 = (bf16[768,768]{1,0:T(8,128)(2,1)}, bf16[768,768]{1,0:T(8,128)(2,1)}, u32[]{:S(2)}, u32[]{:S(2)}) collective-permute-start(bf16[768,768]{1,0:T(8,128)(2,1)} %fusion.24), channel_id=1, source_target_pairs={{0,4},{4,0},{8,12},{12,8},{16,20},{20,16},{24,28},{28,24},{1,5},{5... | collective-permute-start | bytes 3538952 | tf_op jit(solution)/shard_map/ppermute | solution.py:739
  313.4 10.6 %collective-permute-start.23 = (bf16[2,128,768]{2,1,0:T(8,128)(2,1)S(1)}, bf16[2,128,768]{2,1,0:T(8,128)(2,1)S(1)}, u32[]{:S(2)}, u32[]{:S(2)}) collective-permute-start(bf16[2,128,768]{2,1,0:T(8,128)(2,1)S(1)} %pad_maximum_fusion.29), channel_id=1, source_target_pairs={{0,16},{4,20},{8,24},{12,28},{16,0},{20,4},{24,8},{28,12},{1,17},{... | collective-permute-start | bytes 1179656 | tf_op jit(solution)/shard_map/ppermute | solution.py:739
  324.1 9.3 %collective-permute-start.26 = (bf16[4,128,768]{2,1,0:T(8,128)(2,1)S(1)}, bf16[4,128,768]{2,1,0:T(8,128)(2,1)}, u32[]{:S(2)}, u32[]{:S(2)}) collective-permute-start(bf16[4,128,768]{2,1,0:T(8,128)(2,1)S(1)} %pad_maximum_fusion.17), channel_id=1, source_target_pairs={{0,4},{4,0},{8,12},{12,8},{16,20},{20,16},{24,28},{28,24},{1,5},{5... | collective-permute-start | bytes 2359304 | tf_op jit(solution)/shard_map/ppermute | solution.py:739
  333.4 151.3 %reduce-scatter.11.cloned.1.call-start = ((), (), s32[]{:S(2)}) async-start(), calls=%async_computation.12 | async-start | bytes 1966080 | tf_op jit(solution)/shard_map/reduce_scatter | solution.py:825
  383.0 12.6 %collective-permute-start.30 = (bf16[768,1024]{1,0:T(8,128)(2,1)}, bf16[768,1024]{1,0:T(8,128)(2,1)S(1)}, u32[]{:S(2)}, u32[]{:S(2)}) collective-permute-start(bf16[768,1024]{1,0:T(8,128)(2,1)} %fusion.10), channel_id=1, source_target_pairs={{0,4},{4,0},{8,12},{12,8},{16,20},{20,16},{24,28},{28,24},{1,5},{5... | collective-permute-start | bytes 4718600 | tf_op jit(solution)/shard_map/ppermute | solution.py:739
  398.6 132.1 %reduce-scatter.13.cloned.1.call-start = ((), (), s32[]{:S(2)}) async-start(), calls=%async_computation.13 | async-start | bytes 1474560 | tf_op jit(solution)/shard_map/reduce_scatter | solution.py:825
  420.6 22.4 %collective-permute-start.32 = (bf16[1,128,768]{2,1,0:T(8,128)(2,1)S(1)}, bf16[1,128,768]{2,1,0:T(8,128)(2,1)S(1)}, u32[]{:S(2)}, u32[]{:S(2)}) collective-permute-start(bf16[1,128,768]{2,1,0:T(8,128)(2,1)S(1)} %get-tuple-element.391), channel_id=1, source_target_pairs={{0,16},{4,20},{8,24},{12,28},{16,0},{20,4},{24,8},{28,12},{1,17},{... | collective-permute-start | bytes 589832 | tf_op jit(solution)/shard_map/ppermute | solution.py:739
  421.8 21.3 %collective-permute-start.31 = (bf16[1,128,768]{2,1,0:T(8,128)(2,1)S(1)}, bf16[1,128,768]{2,1,0:T(8,128)(2,1)S(1)}, u32[]{:S(2)}, u32[]{:S(2)}) collective-permute-start(bf16[1,128,768]{2,1,0:T(8,128)(2,1)S(1)} %get-tuple-element.392), channel_id=1, source_target_pairs={{0,8},{4,12},{8,0},{12,4},{16,24},{20,28},{24,16},{28,20},{1,9},{5... | collective-permute-start | bytes 589832 | tf_op jit(solution)/shard_map/ppermute | solution.py:739
  425.9 31.3 %collective-permute-start.37 = (bf16[1536,384]{1,0:T(8,128)(2,1)S(1)}, bf16[1536,384]{1,0:T(8,128)(2,1)S(1)}, u32[]{:S(2)}, u32[]{:S(2)}) collective-permute-start(bf16[1536,384]{1,0:T(8,128)(2,1)S(1)} %convolution_convert_fusion), channel_id=1, source_target_pairs={{0,4},{4,0},{8,12},{12,8},{16,20},{20,16},{24,28},{28,24},{1,5},{5... | collective-permute-start | bytes 3538952 | tf_op jit(solution)/shard_map/ppermute | solution.py:739
  461.3 79.1 %reduce-scatter.15.cloned.1.call-start = ((), (), s32[]{:S(2)}) async-start(), calls=%async_computation.14 | async-start | bytes 1474560 | tf_op jit(solution)/shard_map/reduce_scatter | solution.py:825
  461.3 16.0 %collective-permute-start.38 = (bf16[768,768]{1,0:T(8,128)(2,1)}, bf16[768,768]{1,0:T(8,128)(2,1)}, u32[]{:S(2)}, u32[]{:S(2)}) collective-permute-start(bf16[768,768]{1,0:T(8,128)(2,1)} %fusion.27), channel_id=1, source_target_pairs={{0,4},{4,0},{8,12},{12,8},{16,20},{20,16},{24,28},{28,24},{1,5},{5... | collective-permute-start | bytes 3538952 | tf_op jit(solution)/shard_map/ppermute | solution.py:739
  461.4 10.4 %collective-permute-start.34 = (bf16[2,128,768]{2,1,0:T(8,128)(2,1)S(1)}, bf16[2,128,768]{2,1,0:T(8,128)(2,1)S(1)}, u32[]{:S(2)}, u32[]{:S(2)}) collective-permute-start(bf16[2,128,768]{2,1,0:T(8,128)(2,1)S(1)} %pad_maximum_fusion.32), channel_id=1, source_target_pairs={{0,8},{4,12},{8,0},{12,4},{16,24},{20,28},{24,16},{28,20},{1,9},{5... | collective-permute-start | bytes 1179656 | tf_op jit(solution)/shard_map/ppermute | solution.py:739
  462.2 10.0 %collective-permute-start.33 = (bf16[2,128,768]{2,1,0:T(8,128)(2,1)S(1)}, bf16[2,128,768]{2,1,0:T(8,128)(2,1)S(1)}, u32[]{:S(2)}, u32[]{:S(2)}) collective-permute-start(bf16[2,128,768]{2,1,0:T(8,128)(2,1)S(1)} %pad_maximum_fusion.31), channel_id=1, source_target_pairs={{0,16},{4,20},{8,24},{12,28},{16,0},{20,4},{24,8},{28,12},{1,17},{... | collective-permute-start | bytes 1179656 | tf_op jit(solution)/shard_map/ppermute | solution.py:739
  472.3 9.8 %collective-permute-start.36 = (bf16[4,128,768]{2,1,0:T(8,128)(2,1)S(1)}, bf16[4,128,768]{2,1,0:T(8,128)(2,1)S(1)}, u32[]{:S(2)}, u32[]{:S(2)}) collective-permute-start(bf16[4,128,768]{2,1,0:T(8,128)(2,1)S(1)} %pad_maximum_fusion.20), channel_id=1, source_target_pairs={{0,4},{4,0},{8,12},{12,8},{16,20},{20,16},{24,28},{28,24},{1,5},{5... | collective-permute-start | bytes 2359304 | tf_op jit(solution)/shard_map/ppermute | solution.py:739
  482.1 138.5 %reduce-scatter.17.cloned.1.call-start = ((), (), s32[]{:S(2)}) async-start(), calls=%async_computation.15 | async-start | bytes 1966080 | tf_op jit(solution)/shard_map/reduce_scatter | solution.py:825
  485.8 34.2 %collective-permute-start.40 = (bf16[96,2560]{1,0:T(8,128)(2,1)S(1)}, bf16[96,2560]{1,0:T(8,128)(2,1)S(1)}, u32[]{:S(2)}, u32[]{:S(2)}) collective-permute-start(bf16[96,2560]{1,0:T(8,128)(2,1)S(1)} %get-tuple-element.257), channel_id=1, source_target_pairs={{0,16},{4,20},{8,24},{12,28},{16,0},{20,4},{24,8},{28,12},{1,17},{... | collective-permute-start | bytes 1474568 | tf_op jit(solution)/shard_map/ppermute | solution.py:739
  518.5 12.0 %collective-permute-start.39 = (bf16[96,2560]{1,0:T(8,128)(2,1)S(1)}, bf16[96,2560]{1,0:T(8,128)(2,1)S(1)}, u32[]{:S(2)}, u32[]{:S(2)}) collective-permute-start(bf16[96,2560]{1,0:T(8,128)(2,1)S(1)} %get-tuple-element.256), channel_id=1, source_target_pairs={{0,8},{4,12},{8,0},{12,4},{16,24},{20,28},{24,16},{28,20},{1,9},{5... | collective-permute-start | bytes 1474568 | tf_op jit(solution)/shard_map/ppermute | solution.py:739
  549.1 15.0 %collective-permute-start.53 = (bf16[96,2560]{1,0:T(8,128)(2,1)S(1)}, bf16[96,2560]{1,0:T(8,128)(2,1)S(1)}, u32[]{:S(2)}, u32[]{:S(2)}) collective-permute-start(bf16[96,2560]{1,0:T(8,128)(2,1)S(1)} %add_convert_fusion.7), channel_id=1, source_target_pairs={{0,16},{4,20},{8,24},{12,28},{16,0},{20,4},{24,8},{28,12},{1,17},{... | collective-permute-start | bytes 1474568 | tf_op jit(solution)/shard_map/ppermute | solution.py:739
  550.6 24.0 %collective-permute-start.54 = (bf16[96,2560]{1,0:T(8,128)(2,1)S(1)}, bf16[96,2560]{1,0:T(8,128)(2,1)S(1)}, u32[]{:S(2)}, u32[]{:S(2)}) collective-permute-start(bf16[96,2560]{1,0:T(8,128)(2,1)S(1)} %add_convert_fusion.6), channel_id=1, source_target_pairs={{0,8},{4,12},{8,0},{12,4},{16,24},{20,28},{24,16},{28,20},{1,9},{5... | collective-permute-start | bytes 1474568 | tf_op jit(solution)/shard_map/ppermute | solution.py:739
  553.6 18.9 %collective-permute-start.46 = (bf16[192,768]{1,0:T(8,128)(2,1)S(1)}, bf16[192,768]{1,0:T(8,128)(2,1)S(1)}, u32[]{:S(2)}, u32[]{:S(2)}) collective-permute-start(bf16[192,768]{1,0:T(8,128)(2,1)S(1)} %add_convert_fusion.9), channel_id=1, source_target_pairs={{0,8},{4,12},{8,0},{12,4},{16,24},{20,28},{24,16},{28,20},{1,9},{5... | collective-permute-start | bytes 884744 | tf_op jit(solution)/shard_map/ppermute | solution.py:739
  555.8 16.9 %collective-permute-start.44 = (bf16[192,768]{1,0:T(8,128)(2,1)S(1)}, bf16[192,768]{1,0:T(8,128)(2,1)S(1)}, u32[]{:S(2)}, u32[]{:S(2)}) collective-permute-start(bf16[192,768]{1,0:T(8,128)(2,1)S(1)} %add_convert_fusion.11), channel_id=1, source_target_pairs={{0,16},{4,20},{8,24},{12,28},{16,0},{20,4},{24,8},{28,12},{1,17},{... | collective-permute-start | bytes 884744 | tf_op jit(solution)/shard_map/ppermute | solution.py:739
  599.3 9.7 %collective-permute-start.56 = (f32[2,2,2834]{2,1,0:T(2,128)S(1)}, f32[2,2,2834]{2,1,0:T(2,128)S(1)}, u32[]{:S(2)}, u32[]{:S(2)}) collective-permute-start(f32[2,2,2834]{2,1,0:T(2,128)S(1)} %broadcast_select_fusion.8), channel_id=1, source_target_pairs={{0,2},{1,3},{2,0},{3,1},{4,6},{5,7},{6,4},{7,5},{8,10},{9,11},{10,... | collective-permute-start | bytes 136040 | tf_op jit(solution)/shard_map/ppermute | solution.py:739
  609.1 15.0 %collective-permute-start.57 = (f32[1,2,2834]{2,1,0:T(2,128)S(1)}, f32[1,2,2834]{2,1,0:T(2,128)S(1)}, u32[]{:S(2)}, u32[]{:S(2)}) collective-permute-start(f32[1,2,2834]{2,1,0:T(2,128)S(1)} %broadcast_select_fusion.9), channel_id=1, source_target_pairs={{0,1},{1,0},{2,3},{3,2},{4,5},{5,4},{6,7},{7,6},{8,9},{9,8},{10,11... | collective-permute-start | bytes 68024 | tf_op jit(solution)/shard_map/ppermute | solution.py:739
  635.3 9.6 %collective-permute-start.60 = (f32[1,2,2834]{2,1,0:T(2,128)S(1)}, f32[1,2,2834]{2,1,0:T(2,128)S(1)}, u32[]{:S(2)}, u32[]{:S(2)}) collective-permute-start(f32[1,2,2834]{2,1,0:T(2,128)S(1)} %add.429), channel_id=1, source_target_pairs={{0,16},{4,20},{8,24},{12,28},{16,0},{20,4},{24,8},{28,12},{1,17},{... | collective-permute-start | bytes 68024 | tf_op jit(solution)/shard_map/ppermute | solution.py:739
  (85 other events, 696.9 us)
Sparse Core Ops, SparseCore 0:
  10.4 39.8 all-gather.8
  51.9 28.6 all-gather.10
  82.1 29.5 all-gather.16
  113.2 36.7 all-gather.12
  153.0 48.7 all-gather.14
  312.8 26.3 reduce-scatter.6
  341.6 27.8 reduce-scatter.8
  398.7 33.7 reduce-scatter.10
  461.4 26.9 reduce-scatter.12
  490.5 27.9 reduce-scatter.14
  585.9 34.6 reduce-scatter.16

commit v3 on v2

--- a/solution.py
+++ b/solution.py
@@ -757,7 +757,7 @@
             held[side] = jnp.concatenate([held[side], came])
             orders[side] = orders[side] + [o ^ path[k] for o in orders[side]]
         fill = [make(before) for make in beside[k : k + 1]]
-        held = list(together(*held, *fill))[:2]
+        held = list(together(*held, *fill)[:2])
         stages.append(tuple(held))
     return held, orders, stages
 
@@ -816,8 +816,7 @@
     return tn(left, cut(right, width, 1 - core)).astype(bf16)
 
 
-def half_product(left, right, width, core, there):
-    came = swapped(there, "seq", 1)
+def half_product(left, right, width, core, came):
     return (tn(left, cut(right, width, core)) + came.astype(f32)).astype(bf16)
 
 
@@ -992,16 +991,24 @@
         edge = jnp.concatenate([jnp.zeros((8 - (K - 1), CV), f32), edge])
         pre, x, bc, dt, cum, cumt, dtt, packed = prepare(xc, edge, cw, dtr, spike, tok, pv, e2)
         yi = within(x, bc, cum, cumt, dtt, tok, doct)
-        held, orders, stages = all_states(packed, lambda before: yi)
         if i == 0:
-            wz, wo = tied(found[i][1], x), tied(found[i][2], *stages[1])
+            wz = both_cores(tied(found[i][1], x))
+            made = []
+
+            def gate_beside(before):
+                made.append(project_gate(cores, tied(normed, *before), *wz))
+                return made[0]
+
+            held, orders, stages = all_states(packed, lambda before: yi, gate_beside)
+            wo, z = both_cores(tied(found[i][2], *stages[1])), made[0]
         else:
+            held, orders, stages = all_states(packed, lambda before: yi)
             both = tied(found[i][1], *stages[1])
             wz, wo = both[:, :HZ], both[:, HZ:].reshape(parts, -1, 2, HD)
             wo = wo.transpose(0, 2, 1, 3).reshape(E, HD)
-        wz, wo = both_cores(wz), both_cores(wo)
+            wz, wo = both_cores(wz), both_cores(wo)
+            z = project_gate(cores, tied(normed, *stages[0]), *wz)
         weights.append((wx, wz, wo))
-        z = project_gate(cores, tied(normed, *stages[0]), *wz)
         logs = decay_table(held[0], orders[0])
         incoming = joined_states(held, orders, logs, True)
         out_type = bf16 if i == layers - 1 else f32
@@ -1034,14 +1041,15 @@
             near1.extend(within_back(tied(x, near0[2], *before), dy, *shared, 1))
             return near1[2]
 
-        held, orders, stages = all_states(state, lambda before: near0[2], second_half)
-        half_gate = half_product(normed, tied(dz, near1[2]), HZ, core, far_gate)
-        half_out = half_product(low, tied(gb, near1[2]), HD, core, far_out)
+        came = (swapped(far_gate, "seq", 1), swapped(far_out, "seq", 1))
+        held, orders, stages = all_states(state, lambda before: (near0[2], came), second_half)
+        half_gate = half_product(normed, tied(dz, near1[2]), HZ, core, came[0])
+        half_out = half_product(low, tied(gb, near1[2]), HD, core, came[1])
         grad_out, grad_gate = part_sum(half_out), part_sum(half_gate)
         later = joined_states(held, orders, logs, False)
         later = tied(later, half_out, half_gate)
         if top is not None:
-            sums = plane_step(*tied(top, *stages[0]), 0)
+            sums = added(tied(top, later), bits[1])
         dxc, cacc, hacc, first = across_back(
             x, pre, xc, edge, bc, dy, near0, near1, dt, cum, dtr, tok, prior, later, skip, cw, pv, e2, et
         )
@@ -1059,24 +1067,23 @@
         dxc = dxc.at[t - (K - 1) :].set(mended)
         dxc, grad_gate = together(dxc, grad_gate)
         far_conv = far_product(normed, dxc, CX, core)
-        conv_half = half_product(normed, dxc, CX, core, far_conv)
+        conv_half = half_product(normed, dxc, CX, core, swapped(far_conv, "seq", 1))
         rest = grad_out.shape[0] // 2
         grad_out = jnp.concatenate([grad_out[:rest], grad_out[rest:]], axis=1)
         if i == 0:
             early = plane_sum(*tied((grad_gate, grad_out), far_conv))
+            if top is not None:
+                for bit in bits[2:]:
+                    sums = added(sums, bit)
+                grad = tied(grad, sums)
+                results[i + 1] += (swapped_pair(sums),)
             grad = tied(grad, conv_half, *early)
             early = swapped_pair(jnp.concatenate(early, axis=1))
-            if top is not None:
-                for k in range(1, len(bits) - 1):
-                    sums = plane_step(*sums, k)
-                results[i + 1] = results[i + 1] + (swapped_pair(jnp.concatenate(sums)),)
         grad, nacc = close_back(cores, dz, dxc, wz, wx, source, gain_in, grad)
         grad_conv = part_sum(conv_half)
         if i > 0:
             grad = tied(grad, conv_half)
-            value = jnp.concatenate([grad_gate, grad_out, grad_conv], axis=1)
-            half = value.shape[0] // 2
-            waiting[i] = (value[:half], value[half:])
+            waiting[i] = jnp.concatenate([grad_gate, grad_out, grad_conv], axis=1)
         tiny = [
             cacc[:K], cacc[K], hacc[0, :H], hacc[1, :H],
             jnp.sum(acc[1].reshape(H, P_SIZE), axis=1), nacc[0], acc[0],
@@ -1087,10 +1094,13 @@
         tiny = results[i][0]
         taps = tiny[0].reshape(K, parts, CV // parts).transpose(1, 0, 2).reshape(parts, -1)
         packed.append(jnp.concatenate([taps] + [v.reshape(parts, -1) for v in tiny[1:]], axis=1))
-    mine = reduced_small(jnp.stack(packed, axis=1))
+    mine = reduced_small(tied(jnp.stack(packed, axis=1), grad_conv))
     late = swapped_pair(plane_sum_rows(grad_conv))
     results[0] += (tuple(jnp.concatenate(v, axis=1) for v in zip(early, late)),)
-    bigs = [big_of(*results[i][1], core) for i in range(layers)]
+    bigs = [
+        big_of(*(tied(results[i][1], grad_conv) if i else results[i][1]), core)
+        for i in range(layers)
+    ]
     smalls, at = [], 0
     for size in SMALL:
         width = size // parts

time: 669 us -> 651 us (0.973)
  waiting for transfers between devices: 117 us -> 84.4 us
    ppermute x56 -> x54, waiting for transfers between devices: 81 us -> 56.3 us  [swapped(): lax.ppermute(value, axis, [(source, source ^ bit) for source in range(cou...]
    reduce_scatter x6, waiting for transfers between devices: 11.5 us -> 3.18 us  [part_sum(): return lax.psum_scatter(value, 'fsdp', scatter_dimension=0, tiled=True)]
    ppermute x56 -> x54, starting transfers between devices: 49.9 us -> 55.6 us  [swapped(): lax.ppermute(value, axis, [(source, source ^ bit) for source in range(cou...]
  transfers between devices with their start and end apart: 72 -> 70, of which waited for: 25 -> 20; matrix products, arithmetic and copies ran while one was open for 18% -> 20% of each run, Pallas kernels for 39% -> 38%
where the time goes in v3:
time: 651 us; the launch traced here: 641 us
  Pallas kernels  295 us (45%)
  waiting for transfers between devices  84.4 us (13%)
  starting transfers between devices  72.8 us (11%)
  local copies, waits for them, and re-layouts  63.9 us (10%)
  other arithmetic  51.2 us (8%)
  matrix products  46.2 us (7%)
  between operations  16 us (2%)
  blocking collectives  11.2 us (2%)
    pallas_call x2, Pallas kernels, across_back(): pl.pallas_call(across_back_kernel, grid=(n,), in_specs=[turned(E), turned...  63.2 us
    pallas_call x4, Pallas kernels, within_back(): pl.pallas_call(partial(within_back_kernel, range(part * size, (part + 1)...  56.6 us
    ppermute x54, waiting for transfers between devices, swapped(): lax.ppermute(value, axis, [(source, source ^ bit) for source in range(cou...  56.3 us
    ppermute x54, starting transfers between devices, swapped(): lax.ppermute(value, axis, [(source, source ^ bit) for source in range(cou...  55.6 us
    dot_general x12, matrix products, tn(): lax.dot_general(a, b, (((0,), (0,)), ((), ())), preferred_element_type=f32)  46.2 us
    pallas_call x2, Pallas kernels, open_back(): pl.pallas_call(open_back_kernel, grid=(n,), in_specs=[SMEM, turned(D), fu...  41.7 us
    pallas_call x2, Pallas kernels, across(): pl.pallas_call(across_kernel, grid=(t // TT,), in_specs=[SMEM, rows(E), r...  34.1 us
    pallas_call x2, Pallas kernels, prepare(): pl.pallas_call(prepare_kernel, grid=(t // TT,), in_specs=[rows(CV), full(...  30 us
  transfers between devices with their start and end apart: 70, of which 20 were waited for; matrix products, arithmetic and copies ran while one was open for 20% of the time, Pallas kernels for 38%

profile of v3, /device:TPU:1, one launch (start us, length us, event | category | flops | bytes accessed | tf_op | source)
XLA Modules:
  0.0 640.8 jit_solution(12048454789749917309)
XLA Ops:
  11.3 4.5 collective-permute-start.2
  19.1 11.2 %all-gather.2 = bf16[4,2,2834]{2,1,0:T(2,128)(2,1)S(1)} all-gather(bf16[1,2,2834]{2,1,0:T(2,128)(2,1)S(1)} %bitcast.317), channel_id=2, replica_groups=mesh['seq'=8,'fsdp'=4] {'fsdp'}, dimensions={0}, use_global_device_ids=true | all-gather | bytes 56680 | tf_op jit(solution)/shard_map/all_gather | solution.py:951
  31.9 18.4 %all-gather.9.cloned.1.call-done.mine_ref.xm_ref = bf16[768,1024]{1,0:T(8,128)(2,1)} async-done(((bf16[192,1024]{1,0:T(8,128)(2,1)}), bf16[768,1024]{1,0:T(8,128)(2,1)}) %all-gather.9.cloned.1.call-update) | async-done | bytes 1572880 | tf_op jit(solution)/shard_map/all_gather | solution.py:808
  55.4 8.0 %project.2 = (bf16[1024,768]{1,0:T(8,128)(2,1)}, bf16[1024,1792]{1,0:T(8,128)(2,1)}, f32[1024,128]{1,0:T(8,128)}) custom-call(s32[1]{0:T(128)} %bitcast.core_ref, bf16[1024,768]{1,0:T(8,128)(2,1)} %bitcast.338, f32[1,768]{1,0:T(1,128)} %broadcast_in_dim_reshape_squeeze.18.gain_ref, bf16[768,1024]{1,0:T(8,128)(2,1)} %all-gather.9.cloned.1.call-done.mine_ref.xm_ref, ...), custom_call_target="tpu_custom_call" | custom-call | flops 8000000000 | bytes 24000000 | tf_op jit(solution)/shard_map/project/pallas_call | solution.py:130
  64.2 3.0 collective-permute-start.1
  69.1 15.0 %prepare.2 = (bf16[1024,1792]{1,0:T(8,128)(2,1)}, bf16[1024,1536]{1,0:T(8,128)(2,1)}, bf16[1024,256]{1,0:T(8,128)(2,1)}, f32[1024,128]{1,0:T(8,128)}, f32[1024,1...) custom-call(bf16[1024,1792]{1,0:T(8,128)(2,1)} %get-tuple-element.158.xc_ref.halo_ref, ...), custom_call_target="tpu_custom_call" | custom-call | flops 15000000512 | bytes 45000000 | tf_op jit(solution)/shard_map/prepare/pallas_call | solution.py:230
  89.4 7.8 %within.2.yi_ref = bf16[1024,1536]{1,0:T(8,128)(2,1)} custom-call(bf16[1024,1536]{1,0:T(8,128)(2,1)} %get-tuple-element.241.x_ref, bf16[1024,256]{1,0:T(8,128)(2,1)} %get-tuple-element.161.bc_ref, f32[1024,128]{1,0:T(8,128)} %get-tuple-element.162.cum_ref, f32[32,1024]{1,0:T(8,128)} %get-tuple-element.163.cumt_ref, f32[32,1024]{1,0:T(8,128)} %get-tuple-element.164.dtt_ref, ...), custom_call_target="tpu_custom_call" | custom-call | flops 8000000000 | bytes 24000000 | tf_op jit(solution)/shard_map/within/pallas_call | solution.py:284
  98.8 10.4 %collective-permute-done.7 = bf16[2,144,768]{2,1,0:T(8,128)(2,1)S(1)} collective-permute-done((bf16[2,144,768]{2,1,0:T(8,128)(2,1)S(1)}, bf16[2,144,768]{2,1,0:T(8,128)(2,1)S(1)}, u32[]{:S(2)}, u32[]{:S(2)}) %collective-permute-start.7) | collective-permute-done | bytes 442400 | tf_op jit(solution)/shard_map/ppermute | solution.py:739
  111.4 6.3 project_gate.2.z_ref
  134.6 17.1 %across.2 = (bf16[1024,1536]{1,0:T(8,128)(2,1)}, bf16[1024,1536]{1,0:T(8,128)(2,1)}, f32[1024,768]{1,0:T(8,128)}, bf16[8,128,1536]{2,1,0:T(8,128)(2,1)}) custom-call(s32[1]{0:T(128)} %bitcast.core_ref, bf16[1024,1536]{1,0:T(8,128)(2,1)} %within.2.yi_ref, bf16[1024,1536]{1,0:T(8,128)(2,1)} %get-tuple-element.241.x_ref, ...), custom_call_target="tpu_custom_call" | custom-call | flops 16000000000 | bytes 48000000 | tf_op jit(solution)/shard_map/across/pallas_call | solution.py:350
  159.1 8.4 %project.3 = (bf16[1024,768]{1,0:T(8,128)(2,1)}, bf16[1024,1792]{1,0:T(8,128)(2,1)}, f32[1024,128]{1,0:T(8,128)}) custom-call(s32[1]{0:T(128)} %bitcast.core_ref, f32[1024,768]{1,0:T(8,128)} %get-tuple-element.177.x_ref.res_ref, f32[1,768]{1,0:T(1,128)} %broadcast_in_dim_reshape_squeeze.21.gain_ref, ...), custom_call_target="tpu_custom_call" | custom-call | flops 8000000000 | bytes 24000000 | tf_op jit(solution)/shard_map/project/pallas_call | solution.py:130
  168.3 3.5 collective-permute-start.12
  173.1 15.0 %prepare.3 = (bf16[1024,1792]{1,0:T(8,128)(2,1)}, bf16[1024,1536]{1,0:T(8,128)(2,1)}, bf16[1024,256]{1,0:T(8,128)(2,1)}, f32[1024,128]{1,0:T(8,128)}, f32[1024,1...) custom-call(bf16[1024,1792]{1,0:T(8,128)(2,1)} %get-tuple-element.179.xc_ref.halo_ref, ...), custom_call_target="tpu_custom_call" | custom-call | flops 15000000512 | bytes 45000000 | tf_op jit(solution)/shard_map/prepare/pallas_call | solution.py:230
  190.5 7.8 %within.3.yi_ref = bf16[1024,1536]{1,0:T(8,128)(2,1)} custom-call(bf16[1024,1536]{1,0:T(8,128)(2,1)} %get-tuple-element.210.x_ref, bf16[1024,256]{1,0:T(8,128)(2,1)} %get-tuple-element.182.bc_ref, f32[1024,128]{1,0:T(8,128)} %get-tuple-element.183.cum_ref, f32[32,1024]{1,0:T(8,128)} %get-tuple-element.184.cumt_ref, f32[32,1024]{1,0:T(8,128)} %get-tuple-element.185.dtt_ref, ...), custom_call_target="tpu_custom_call" | custom-call | flops 8000000000 | bytes 24000000 | tf_op jit(solution)/shard_map/within/pallas_call | solution.py:284
  200.1 7.1 %collective-permute-done.16 = bf16[2,144,768]{2,1,0:T(8,128)(2,1)S(1)} collective-permute-done((bf16[2,144,768]{2,1,0:T(8,128)(2,1)S(1)}, bf16[2,144,768]{2,1,0:T(8,128)(2,1)S(1)}, u32[]{:S(2)}, u32[]{:S(2)}) %collective-permute-start.16) | collective-permute-done | bytes 442400 | tf_op jit(solution)/shard_map/ppermute | solution.py:739
  209.5 3.9 collective-permute-start.19
  230.3 6.4 project_gate.3.z_ref
  236.6 17.0 %across.3 = (bf16[1024,1536]{1,0:T(8,128)(2,1)}, bf16[1024,1536]{1,0:T(8,128)(2,1)}, bf16[1024,768]{1,0:T(8,128)(2,1)}, bf16[8,128,1536]{2,1,0:T(8,128)(2,1)}) custom-call(s32[1]{0:T(128)} %bitcast.core_ref, bf16[1024,1536]{1,0:T(8,128)(2,1)} %within.3.yi_ref, bf16[1024,1536]{1,0:T(8,128)(2,1)} %get-tuple-element.210.x_ref, ...), custom_call_target="tpu_custom_call" | custom-call | flops 16000000000 | bytes 48000000 | tf_op jit(solution)/shard_map/across/pallas_call | solution.py:350
  253.6 20.8 %open_back.2 = (bf16[1024,1536]{1,0:T(8,128)(2,1)}, bf16[1024,1536]{1,0:T(8,128)(2,1)}, bf16[1024,768]{1,0:T(8,128)(2,1)}, f32[8,1536]{1,0:T(8,128)}, bf16[128,1536]{1,0:T(8,128)(2,1)}) custom-call(s32[1]{0:T(128)} %bitcast.core_ref, bf16[1024,768]{1,0:T(8,128)(2,1)} %bitcast.336, bf16[1536,384]{1,0:T(8,128)(2,1)} %bitcast.67.mine_ref, ...), custom_call_target="tpu_custom_call" | custom-call | flops 20000000000 | bytes 60000000 | tf_op jit(solution)/shard_map/open_back/pallas_call | solution.py:436
  274.5 4.1 convolution_convert_fusion.1
  282.2 13.7 %within_back.4 = (bf16[1024,768]{1,0:T(8,128)(2,1)}, f32[1024,256]{1,0:T(8,128)}, f32[1024,128]{1,0:T(8,128)}) custom-call(bf16[1024,1536]{1,0:T(8,128)(2,1)} %get-tuple-element.210.x_ref, bf16[1024,1536]{1,0:T(8,128)(2,1)} %get-tuple-element.201.dy_ref, bf16[1024,256]{1,0:T(8,128)(2,1)} %get-tuple-element.182.bc_ref, ...), custom_call_target="tpu_custom_call" | custom-call | flops 12000000000 | bytes 36000000 | tf_op jit(solution)/shard_map/within_back/pallas_call | solution.py:513
  296.1 14.6 %within_back.5 = (bf16[1024,768]{1,0:T(8,128)(2,1)}, f32[1024,256]{1,0:T(8,128)}, f32[1024,128]{1,0:T(8,128)}) custom-call(bf16[1024,1536]{1,0:T(8,128)(2,1)} %get-tuple-element.210.x_ref, bf16[1024,1536]{1,0:T(8,128)(2,1)} %get-tuple-element.201.dy_ref, bf16[1024,256]{1,0:T(8,128)(2,1)} %get-tuple-element.182.bc_ref, ...), custom_call_target="tpu_custom_call" | custom-call | flops 12000000000 | bytes 36000000 | tf_op jit(solution)/shard_map/within_back/pallas_call | solution.py:513
  310.7 4.7 fusion
  317.1 8.3 %collective-permute-done.26 = bf16[2,128,768]{2,1,0:T(8,128)(2,1)S(1)} collective-permute-done((bf16[2,128,768]{2,1,0:T(8,128)(2,1)S(1)}, bf16[2,128,768]{2,1,0:T(8,128)(2,1)S(1)}, u32[]{:S(2)}, u32[]{:S(2)}) %collective-permute-start.26) | collective-permute-done | bytes 393248 | tf_op jit(solution)/shard_map/ppermute | solution.py:739
  330.9 4.3 add_convert_fusion.3
  339.4 31.6 %across_back.2 = (bf16[1024,2048]{1,0:T(8,128)(2,1)}, f32[8,1792]{1,0:T(8,128)}, f32[8,128]{1,0:T(8,128)}, f32[8,1792]{1,0:T(8,128)}) custom-call(bf16[1024,1536]{1,0:T(8,128)(2,1)} %get-tuple-element.210.x_ref, bf16[1024,1792]{1,0:T(8,128)(2,1)} %get-tuple-element.200.pre_ref, bf16[1024,1792]{1,0:T(8,128)(2,1)} %get-tuple-element.179.xc_ref.halo_ref, ...), custom_call_target="tpu_custom_call" | custom-call | flops 31000000512 | bytes 93000000 | tf_op jit(solution)/shard_map/across_back/pallas_call | solution.py:660
  380.1 4.6 fusion.10
  384.7 12.6 %close_back.2 = (f32[1024,768]{1,0:T(8,128)}, f32[8,768]{1,0:T(8,128)}) custom-call(s32[1]{0:T(128)} %bitcast.core_ref, bf16[1024,1536]{1,0:T(8,128)(2,1)} %get-tuple-element.221.dz_ref, bf16[1024,2048]{1,0:T(8,128)(2,1)} %scatter.6.dxc_ref, bf16[768,768]{1,0:T(8,128)(2,1)} %get-tuple-element.372.mine_ref.zm_ref, ...), custom_call_target="tpu_custom_call" | custom-call | flops 12000000000 | bytes 36000000 | tf_op jit(solution)/shard_map/close_back/pallas_call | solution.py:716
  397.2 3.0 add_convert_fusion.1
  400.3 20.8 %open_back.3 = (bf16[1024,1536]{1,0:T(8,128)(2,1)}, bf16[1024,1536]{1,0:T(8,128)(2,1)}, bf16[1024,768]{1,0:T(8,128)(2,1)}, f32[8,1536]{1,0:T(8,128)}, bf16[128,1536]{1,0:T(8,128)(2,1)}) custom-call(s32[1]{0:T(128)} %bitcast.core_ref, f32[1024,768]{1,0:T(8,128)} %get-tuple-element.268.g_ref, bf16[1536,384]{1,0:T(8,128)(2,1)} %bitcast.343, ...), custom_call_target="tpu_custom_call" | custom-call | flops 20000000000 | bytes 60000000 | tf_op jit(solution)/shard_map/open_back/pallas_call | solution.py:436
  421.2 3.0 fusion.27
  429.0 13.7 %within_back.6 = (bf16[1024,768]{1,0:T(8,128)(2,1)}, f32[1024,256]{1,0:T(8,128)}, f32[1024,128]{1,0:T(8,128)}) custom-call(bf16[1024,1536]{1,0:T(8,128)(2,1)} %get-tuple-element.241.x_ref, bf16[1024,1536]{1,0:T(8,128)(2,1)} %get-tuple-element.232.dy_ref, bf16[1024,256]{1,0:T(8,128)(2,1)} %get-tuple-element.161.bc_ref, ...), custom_call_target="tpu_custom_call" | custom-call | flops 12000000000 | bytes 36000000 | tf_op jit(solution)/shard_map/within_back/pallas_call | solution.py:513
  442.9 14.5 %within_back.7 = (bf16[1024,768]{1,0:T(8,128)(2,1)}, f32[1024,256]{1,0:T(8,128)}, f32[1024,128]{1,0:T(8,128)}) custom-call(bf16[1024,1536]{1,0:T(8,128)(2,1)} %get-tuple-element.241.x_ref, bf16[1024,1536]{1,0:T(8,128)(2,1)} %get-tuple-element.232.dy_ref, bf16[1024,256]{1,0:T(8,128)(2,1)} %get-tuple-element.161.bc_ref, ...), custom_call_target="tpu_custom_call" | custom-call | flops 12000000000 | bytes 36000000 | tf_op jit(solution)/shard_map/within_back/pallas_call | solution.py:513
  457.4 4.8 fusion.1
  468.6 3.9 collective-permute-done.36
  480.3 4.3 add_convert_fusion.2
  491.0 31.6 %across_back.3 = (bf16[1024,2048]{1,0:T(8,128)(2,1)}, f32[8,1792]{1,0:T(8,128)}, f32[8,128]{1,0:T(8,128)}, f32[8,1792]{1,0:T(8,128)}) custom-call(bf16[1024,1536]{1,0:T(8,128)(2,1)} %get-tuple-element.241.x_ref, bf16[1024,1792]{1,0:T(8,128)(2,1)} %get-tuple-element.231.pre_ref, bf16[1024,1792]{1,0:T(8,128)(2,1)} %get-tuple-element.158.xc_ref.halo_ref, ...), custom_call_target="tpu_custom_call" | custom-call | flops 31000000512 | bytes 93000000 | tf_op jit(solution)/shard_map/across_back/pallas_call | solution.py:660
  532.9 4.6 fusion.13
  542.6 3.5 collective-permute-done.45
  552.1 3.4 collective-permute-done.46
  556.6 6.0 collective-permute-start.47
  562.6 5.5 add_convert_fusion
  568.1 8.7 %collective-permute-done.41 = bf16[192,2560]{1,0:T(8,128)(2,1)} collective-permute-done((bf16[192,2560]{1,0:T(8,128)(2,1)S(1)}, bf16[192,2560]{1,0:T(8,128)(2,1)}, u32[]{:S(2)}, u32[]{:S(2)}) %collective-permute-start.41) | collective-permute-done | bytes 983072 | tf_op jit(solution)/shard_map/ppermute | solution.py:739
  578.2 3.3 collective-permute-start.53
  584.7 12.4 %close_back.3 = (f32[1024,768]{1,0:T(8,128)}, f32[8,768]{1,0:T(8,128)}) custom-call(s32[1]{0:T(128)} %bitcast.core_ref, bf16[1024,1536]{1,0:T(8,128)(2,1)} %get-tuple-element.252.dz_ref, bf16[1024,2048]{1,0:T(8,128)(2,1)} %scatter.9.dxc_ref, bf16[768,768]{1,0:T(8,128)(2,1)} %all-gather.11.cloned.1.call-done.mine_ref.zm_ref, bf16[768,768]{1,0:T(8,128)(2,1)} %copy-done.66, ...), custom_call_target="tpu_custom_call" | custom-call | flops 12000000000 | bytes 36000000 | tf_op jit(solution)/shard_map/close_back/pallas_call | solution.py:716
  598.2 3.1 reduce-scatter.17.cloned.1.call-done
  618.5 3.3 collective-permute-done.51
  630.0 4.0 maximum_convert_fusion
  (535 shorter events, 177.2 us)
Async XLA Ops:
  7.2 43.1 %all-gather.9.cloned.1.call-start = ((), (), s32[]{:S(2)}) async-start(), calls=%async_computation.6 | async-start | bytes 1966080 | tf_op jit(solution)/shard_map/all_gather | solution.py:808
  10.3 76.3 %all-gather.11.cloned.1.call-start = ((), (), s32[]{:S(2)}) async-start(), calls=%async_computation.7 | async-start | bytes 1474560 | tf_op jit(solution)/shard_map/all_gather | solution.py:808
  11.1 112.1 %all-gather.17.cloned.1.call-start = ((), (), s32[]{:S(2)}) async-start(), calls=%async_computation.16 | async-start | bytes 1474560 | tf_op jit(solution)/shard_map/all_gather | solution.py:808
  11.3 43.9 %collective-permute-start.2 = (s32[3]{0:T(128)S(1)}, s32[3]{0:T(128)S(1)}, u32[]{:S(2)}, u32[]{:S(2)}) collective-permute-start(s32[3]{0:T(128)S(1)} %slice_bitcast_fusion.10), channel_id=1, source_target_pairs={{0,4},{4,8},{8,12},{12,16},{16,20},{20,24},{24,28},{1,5},{5,9},{9,... | collective-permute-start | bytes 44 | tf_op jit(solution)/shard_map/ppermute | solution.py:734
  18.8 135.2 %all-gather.13.cloned.1.call-start = ((), (), s32[]{:S(2)}) async-start(), calls=%async_computation.8 | async-start | bytes 1966080 | tf_op jit(solution)/shard_map/all_gather | solution.py:808
  85.2 11.9 %collective-permute-start.4 = (bf16[1,144,768]{2,1,0:T(8,128)(2,1)S(1)}, bf16[1,144,768]{2,1,0:T(8,128)(2,1)S(1)}, u32[]{:S(2)}, u32[]{:S(2)}) collective-permute-start(bf16[1,144,768]{2,1,0:T(8,128)(2,1)S(1)} %get-tuple-element.387), channel_id=1, source_target_pairs={{0,16},{4,20},{8,24},{12,28},{16,0},{20,4},{24,8},{28,12},{1,17},{... | collective-permute-start | bytes 663560 | tf_op jit(solution)/shard_map/ppermute | solution.py:739
  86.3 10.9 %collective-permute-start.3 = (bf16[1,144,768]{2,1,0:T(8,128)(2,1)S(1)}, bf16[1,144,768]{2,1,0:T(8,128)(2,1)S(1)}, u32[]{:S(2)}, u32[]{:S(2)}) collective-permute-start(bf16[1,144,768]{2,1,0:T(8,128)(2,1)S(1)} %get-tuple-element.388), channel_id=1, source_target_pairs={{0,8},{4,12},{8,0},{12,4},{16,24},{20,28},{24,16},{28,20},{1,9},{5... | collective-permute-start | bytes 663560 | tf_op jit(solution)/shard_map/ppermute | solution.py:739
  86.6 23.8 %collective-permute-start.5 = (bf16[768,768]{1,0:T(8,128)(2,1)}, bf16[768,768]{1,0:T(8,128)(2,1)S(1)}, u32[]{:S(2)}, u32[]{:S(2)}) collective-permute-start(bf16[768,768]{1,0:T(8,128)(2,1)} %all-gather.11.cloned.1.call-done.mine_ref.zm_ref), channel_id=1, source_target_pairs={{0,4},{4,0},{8,12},{12,8},{16,20},{20,16},{24,28},{28,24},{1,5},{5... | collective-permute-start | bytes 3538952 | tf_op jit(solution)/shard_map/ppermute | solution.py:739
  97.3 12.0 %collective-permute-start.7 = (bf16[2,144,768]{2,1,0:T(8,128)(2,1)S(1)}, bf16[2,144,768]{2,1,0:T(8,128)(2,1)S(1)}, u32[]{:S(2)}, u32[]{:S(2)}) collective-permute-start(bf16[2,144,768]{2,1,0:T(8,128)(2,1)S(1)} %pad_maximum_fusion.25), channel_id=1, source_target_pairs={{0,8},{4,12},{8,0},{12,4},{16,24},{20,28},{24,16},{28,20},{1,9},{5... | collective-permute-start | bytes 1327112 | tf_op jit(solution)/shard_map/ppermute | solution.py:739
  98.7 11.5 %collective-permute-start.6 = (bf16[2,144,768]{2,1,0:T(8,128)(2,1)S(1)}, bf16[2,144,768]{2,1,0:T(8,128)(2,1)S(1)}, u32[]{:S(2)}, u32[]{:S(2)}) collective-permute-start(bf16[2,144,768]{2,1,0:T(8,128)(2,1)S(1)} %pad_maximum_fusion.24), channel_id=1, source_target_pairs={{0,16},{4,20},{8,24},{12,28},{16,0},{20,4},{24,8},{28,12},{1,17},{... | collective-permute-start | bytes 1327112 | tf_op jit(solution)/shard_map/ppermute | solution.py:739
  119.7 94.5 %all-gather.15.cloned.1.call-start = ((), (), s32[]{:S(2)}) async-start(), calls=%async_computation.9 | async-start | bytes 2949120 | tf_op jit(solution)/shard_map/all_gather | solution.py:808
  123.2 11.4 %collective-permute-start.10 = (bf16[1536,384]{1,0:T(8,128)(2,1)}, bf16[1536,384]{1,0:T(8,128)(2,1)}, u32[]{:S(2)}, u32[]{:S(2)}) collective-permute-start(bf16[1536,384]{1,0:T(8,128)(2,1)} %bitcast.341), channel_id=1, source_target_pairs={{0,4},{4,0},{8,12},{12,8},{16,20},{20,16},{24,28},{28,24},{1,5},{5... | collective-permute-start | bytes 3538952 | tf_op jit(solution)/shard_map/ppermute | solution.py:739
  156.9 214.1 %reduce-scatter.7.cloned.1.call-start = ((), (), s32[]{:S(2)}) async-start(), calls=%async_computation.10 | async-start | bytes 1474560 | tf_op jit(solution)/shard_map/reduce_scatter | solution.py:824
  189.2 9.1 %collective-permute-start.14 = (bf16[1,144,768]{2,1,0:T(8,128)(2,1)S(1)}, bf16[1,144,768]{2,1,0:T(8,128)(2,1)S(1)}, u32[]{:S(2)}, u32[]{:S(2)}) collective-permute-start(bf16[1,144,768]{2,1,0:T(8,128)(2,1)S(1)} %get-tuple-element.385), channel_id=1, source_target_pairs={{0,16},{4,20},{8,24},{12,28},{16,0},{20,4},{24,8},{28,12},{1,17},{... | collective-permute-start | bytes 663560 | tf_op jit(solution)/shard_map/ppermute | solution.py:739
  198.4 8.9 %collective-permute-start.16 = (bf16[2,144,768]{2,1,0:T(8,128)(2,1)S(1)}, bf16[2,144,768]{2,1,0:T(8,128)(2,1)S(1)}, u32[]{:S(2)}, u32[]{:S(2)}) collective-permute-start(bf16[2,144,768]{2,1,0:T(8,128)(2,1)S(1)} %pad_maximum_fusion.27), channel_id=1, source_target_pairs={{0,8},{4,12},{8,0},{12,4},{16,24},{20,28},{24,16},{28,20},{1,9},{5... | collective-permute-start | bytes 1327112 | tf_op jit(solution)/shard_map/ppermute | solution.py:739
  199.8 8.7 %collective-permute-start.15 = (bf16[2,144,768]{2,1,0:T(8,128)(2,1)S(1)}, bf16[2,144,768]{2,1,0:T(8,128)(2,1)S(1)}, u32[]{:S(2)}, u32[]{:S(2)}) collective-permute-start(bf16[2,144,768]{2,1,0:T(8,128)(2,1)S(1)} %pad_maximum_fusion.26), channel_id=1, source_target_pairs={{0,16},{4,20},{8,24},{12,28},{16,0},{20,4},{24,8},{28,12},{1,17},{... | collective-permute-start | bytes 1327112 | tf_op jit(solution)/shard_map/ppermute | solution.py:739
  209.5 9.6 %collective-permute-start.19 = (bf16[4,144,768]{2,1,0:T(8,128)(2,1)S(1)}, bf16[4,144,768]{2,1,0:T(8,128)(2,1)}, u32[]{:S(2)}, u32[]{:S(2)}) collective-permute-start(bf16[4,144,768]{2,1,0:T(8,128)(2,1)S(1)} %pad_maximum_fusion.12), channel_id=1, source_target_pairs={{0,4},{4,0},{8,12},{12,8},{16,20},{20,16},{24,28},{28,24},{1,5},{5... | collective-permute-start | bytes 2654216 | tf_op jit(solution)/shard_map/ppermute | solution.py:739
  217.1 13.2 %collective-permute-start.17 = (bf16[768,768]{1,0:T(8,128)(2,1)}, bf16[768,768]{1,0:T(8,128)(2,1)}, u32[]{:S(2)}, u32[]{:S(2)}) collective-permute-start(bf16[768,768]{1,0:T(8,128)(2,1)} %get-tuple-element.372.mine_ref.zm_ref), channel_id=1, source_target_pairs={{0,4},{4,0},{8,12},{12,8},{16,20},{20,16},{24,28},{28,24},{1,5},{5... | collective-permute-start | bytes 3538952 | tf_op jit(solution)/shard_map/ppermute | solution.py:739
  219.1 17.5 %collective-permute-start.20 = (bf16[1536,384]{1,0:T(8,128)(2,1)}, bf16[1536,384]{1,0:T(8,128)(2,1)}, u32[]{:S(2)}, u32[]{:S(2)}) collective-permute-start(bf16[1536,384]{1,0:T(8,128)(2,1)} %bitcast.67.mine_ref), channel_id=1, source_target_pairs={{0,4},{4,0},{8,12},{12,8},{16,20},{20,16},{24,28},{28,24},{1,5},{5... | collective-permute-start | bytes 3538952 | tf_op jit(solution)/shard_map/ppermute | solution.py:739
  278.5 17.5 %collective-permute-start.24 = (bf16[1536,384]{1,0:T(8,128)(2,1)S(1)}, bf16[1536,384]{1,0:T(8,128)(2,1)S(1)}, u32[]{:S(2)}, u32[]{:S(2)}) collective-permute-start(bf16[1536,384]{1,0:T(8,128)(2,1)S(1)} %convolution_convert_fusion.1), channel_id=1, source_target_pairs={{0,4},{4,0},{8,12},{12,8},{16,20},{20,16},{24,28},{28,24},{1,5},{5... | collective-permute-start | bytes 3538952 | tf_op jit(solution)/shard_map/ppermute | solution.py:739
  280.5 15.6 %collective-permute-start.23 = (bf16[768,768]{1,0:T(8,128)(2,1)S(1)}, bf16[768,768]{1,0:T(8,128)(2,1)S(1)}, u32[]{:S(2)}, u32[]{:S(2)}) collective-permute-start(bf16[768,768]{1,0:T(8,128)(2,1)S(1)} %fusion.24), channel_id=1, source_target_pairs={{0,4},{4,0},{8,12},{12,8},{16,20},{20,16},{24,28},{28,24},{1,5},{5... | collective-permute-start | bytes 3538952 | tf_op jit(solution)/shard_map/ppermute | solution.py:739
  280.7 15.3 %collective-permute-start.22 = (bf16[1,128,768]{2,1,0:T(8,128)(2,1)S(1)}, bf16[1,128,768]{2,1,0:T(8,128)(2,1)S(1)}, u32[]{:S(2)}, u32[]{:S(2)}) collective-permute-start(bf16[1,128,768]{2,1,0:T(8,128)(2,1)S(1)} %get-tuple-element.395), channel_id=1, source_target_pairs={{0,16},{4,20},{8,24},{12,28},{16,0},{20,4},{24,8},{28,12},{1,17},{... | collective-permute-start | bytes 589832 | tf_op jit(solution)/shard_map/ppermute | solution.py:739
  281.0 15.0 %collective-permute-start.21 = (bf16[1,128,768]{2,1,0:T(8,128)(2,1)S(1)}, bf16[1,128,768]{2,1,0:T(8,128)(2,1)S(1)}, u32[]{:S(2)}, u32[]{:S(2)}) collective-permute-start(bf16[1,128,768]{2,1,0:T(8,128)(2,1)S(1)} %get-tuple-element.396), channel_id=1, source_target_pairs={{0,8},{4,12},{8,0},{12,4},{16,24},{20,28},{24,16},{28,20},{1,9},{5... | collective-permute-start | bytes 589832 | tf_op jit(solution)/shard_map/ppermute | solution.py:739
  315.5 64.6 %reduce-scatter.9.cloned.1.call-start = ((), (), s32[]{:S(2)}) async-start(), calls=%async_computation.11 | async-start | bytes 1474560 | tf_op jit(solution)/shard_map/reduce_scatter | solution.py:824
  315.6 9.8 %collective-permute-start.26 = (bf16[2,128,768]{2,1,0:T(8,128)(2,1)S(1)}, bf16[2,128,768]{2,1,0:T(8,128)(2,1)S(1)}, u32[]{:S(2)}, u32[]{:S(2)}) collective-permute-start(bf16[2,128,768]{2,1,0:T(8,128)(2,1)S(1)} %pad_maximum_fusion.29), channel_id=1, source_target_pairs={{0,8},{4,12},{8,0},{12,4},{16,24},{20,28},{24,16},{28,20},{1,9},{5... | collective-permute-start | bytes 1179656 | tf_op jit(solution)/shard_map/ppermute | solution.py:739
  315.9 9.6 %collective-permute-start.25 = (bf16[2,128,768]{2,1,0:T(8,128)(2,1)S(1)}, bf16[2,128,768]{2,1,0:T(8,128)(2,1)S(1)}, u32[]{:S(2)}, u32[]{:S(2)}) collective-permute-start(bf16[2,128,768]{2,1,0:T(8,128)(2,1)S(1)} %pad_maximum_fusion.28), channel_id=1, source_target_pairs={{0,16},{4,20},{8,24},{12,28},{16,0},{20,4},{24,8},{28,12},{1,17},{... | collective-permute-start | bytes 1179656 | tf_op jit(solution)/shard_map/ppermute | solution.py:739
  325.6 9.7 %collective-permute-start.28 = (bf16[4,128,768]{2,1,0:T(8,128)(2,1)S(1)}, bf16[4,128,768]{2,1,0:T(8,128)(2,1)}, u32[]{:S(2)}, u32[]{:S(2)}) collective-permute-start(bf16[4,128,768]{2,1,0:T(8,128)(2,1)S(1)} %pad_maximum_fusion.16), channel_id=1, source_target_pairs={{0,4},{4,0},{8,12},{12,8},{16,20},{20,16},{24,28},{28,24},{1,5},{5... | collective-permute-start | bytes 2359304 | tf_op jit(solution)/shard_map/ppermute | solution.py:739
  335.2 154.2 %reduce-scatter.11.cloned.1.call-start = ((), (), s32[]{:S(2)}) async-start(), calls=%async_computation.12 | async-start | bytes 1966080 | tf_op jit(solution)/shard_map/reduce_scatter | solution.py:824
  384.7 12.6 %collective-permute-start.30 = (bf16[768,1024]{1,0:T(8,128)(2,1)}, bf16[768,1024]{1,0:T(8,128)(2,1)S(1)}, u32[]{:S(2)}, u32[]{:S(2)}) collective-permute-start(bf16[768,1024]{1,0:T(8,128)(2,1)} %fusion.10), channel_id=1, source_target_pairs={{0,4},{4,0},{8,12},{12,8},{16,20},{20,16},{24,28},{28,24},{1,5},{5... | collective-permute-start | bytes 4718600 | tf_op jit(solution)/shard_map/ppermute | solution.py:739
  400.2 122.6 %reduce-scatter.13.cloned.1.call-start = ((), (), s32[]{:S(2)}) async-start(), calls=%async_computation.13 | async-start | bytes 1474560 | tf_op jit(solution)/shard_map/reduce_scatter | solution.py:824
  426.1 16.7 %collective-permute-start.34 = (bf16[1536,384]{1,0:T(8,128)(2,1)S(1)}, bf16[1536,384]{1,0:T(8,128)(2,1)S(1)}, u32[]{:S(2)}, u32[]{:S(2)}) collective-permute-start(bf16[1536,384]{1,0:T(8,128)(2,1)S(1)} %convolution_convert_fusion), channel_id=1, source_target_pairs={{0,4},{4,0},{8,12},{12,8},{16,20},{20,16},{24,28},{28,24},{1,5},{5... | collective-permute-start | bytes 3538952 | tf_op jit(solution)/shard_map/ppermute | solution.py:739
  426.7 16.2 %collective-permute-start.33 = (bf16[768,768]{1,0:T(8,128)(2,1)S(1)}, bf16[768,768]{1,0:T(8,128)(2,1)S(1)}, u32[]{:S(2)}, u32[]{:S(2)}) collective-permute-start(bf16[768,768]{1,0:T(8,128)(2,1)S(1)} %fusion.27), channel_id=1, source_target_pairs={{0,4},{4,0},{8,12},{12,8},{16,20},{20,16},{24,28},{28,24},{1,5},{5... | collective-permute-start | bytes 3538952 | tf_op jit(solution)/shard_map/ppermute | solution.py:739
  426.8 15.9 %collective-permute-start.32 = (bf16[1,128,768]{2,1,0:T(8,128)(2,1)S(1)}, bf16[1,128,768]{2,1,0:T(8,128)(2,1)S(1)}, u32[]{:S(2)}, u32[]{:S(2)}) collective-permute-start(bf16[1,128,768]{2,1,0:T(8,128)(2,1)S(1)} %get-tuple-element.393), channel_id=1, source_target_pairs={{0,16},{4,20},{8,24},{12,28},{16,0},{20,4},{24,8},{28,12},{1,17},{... | collective-permute-start | bytes 589832 | tf_op jit(solution)/shard_map/ppermute | solution.py:739
  428.0 14.7 %collective-permute-start.31 = (bf16[1,128,768]{2,1,0:T(8,128)(2,1)S(1)}, bf16[1,128,768]{2,1,0:T(8,128)(2,1)S(1)}, u32[]{:S(2)}, u32[]{:S(2)}) collective-permute-start(bf16[1,128,768]{2,1,0:T(8,128)(2,1)S(1)} %get-tuple-element.394), channel_id=1, source_target_pairs={{0,8},{4,12},{8,0},{12,4},{16,24},{20,28},{24,16},{28,20},{1,9},{5... | collective-permute-start | bytes 589832 | tf_op jit(solution)/shard_map/ppermute | solution.py:739
  462.3 70.6 %reduce-scatter.15.cloned.1.call-start = ((), (), s32[]{:S(2)}) async-start(), calls=%async_computation.14 | async-start | bytes 1474560 | tf_op jit(solution)/shard_map/reduce_scatter | solution.py:824
  462.3 10.1 %collective-permute-start.36 = (bf16[2,128,768]{2,1,0:T(8,128)(2,1)S(1)}, bf16[2,128,768]{2,1,0:T(8,128)(2,1)}, u32[]{:S(2)}, u32[]{:S(2)}) collective-permute-start(bf16[2,128,768]{2,1,0:T(8,128)(2,1)S(1)} %pad_maximum_fusion.31), channel_id=1, source_target_pairs={{0,8},{4,12},{8,0},{12,4},{16,24},{20,28},{24,16},{28,20},{1,9},{5... | collective-permute-start | bytes 1179656 | tf_op jit(solution)/shard_map/ppermute | solution.py:739
  462.9 10.7 %collective-permute-start.35 = (bf16[2,128,768]{2,1,0:T(8,128)(2,1)S(1)}, bf16[2,128,768]{2,1,0:T(8,128)(2,1)}, u32[]{:S(2)}, u32[]{:S(2)}) collective-permute-start(bf16[2,128,768]{2,1,0:T(8,128)(2,1)S(1)} %pad_maximum_fusion.30), channel_id=1, source_target_pairs={{0,16},{4,20},{8,24},{12,28},{16,0},{20,4},{24,8},{28,12},{1,17},{... | collective-permute-start | bytes 1179656 | tf_op jit(solution)/shard_map/ppermute | solution.py:739
  474.6 10.1 %collective-permute-start.38 = (bf16[4,128,768]{2,1,0:T(8,128)(2,1)S(1)}, bf16[4,128,768]{2,1,0:T(8,128)(2,1)}, u32[]{:S(2)}, u32[]{:S(2)}) collective-permute-start(bf16[4,128,768]{2,1,0:T(8,128)(2,1)S(1)} %pad_maximum_fusion.19), channel_id=1, source_target_pairs={{0,4},{4,0},{8,12},{12,8},{16,20},{20,16},{24,28},{28,24},{1,5},{5... | collective-permute-start | bytes 2359304 | tf_op jit(solution)/shard_map/ppermute | solution.py:739
  484.6 116.6 %reduce-scatter.17.cloned.1.call-start = ((), (), s32[]{:S(2)}) async-start(), calls=%async_computation.15 | async-start | bytes 1966080 | tf_op jit(solution)/shard_map/reduce_scatter | solution.py:824
  490.5 32.1 %collective-permute-start.39 = (bf16[192,2560]{1,0:T(8,128)(2,1)S(1)}, bf16[192,2560]{1,0:T(8,128)(2,1)S(1)}, u32[]{:S(2)}, u32[]{:S(2)}) collective-permute-start(bf16[192,2560]{1,0:T(8,128)(2,1)S(1)} %pad_maximum_fusion.8), channel_id=1, source_target_pairs={{0,8},{4,12},{8,0},{12,4},{16,24},{20,28},{24,16},{28,20},{1,9},{5... | collective-permute-start | bytes 2949128 | tf_op jit(solution)/shard_map/ppermute | solution.py:739
  537.5 8.6 %collective-permute-start.45 = (bf16[192,768]{1,0:T(8,128)(2,1)S(1)}, bf16[192,768]{1,0:T(8,128)(2,1)S(1)}, u32[]{:S(2)}, u32[]{:S(2)}) collective-permute-start(bf16[192,768]{1,0:T(8,128)(2,1)S(1)} %pad_maximum_fusion.32), channel_id=1, source_target_pairs={{0,16},{4,20},{8,24},{12,28},{16,0},{20,4},{24,8},{28,12},{1,17},{... | collective-permute-start | bytes 884744 | tf_op jit(solution)/shard_map/ppermute | solution.py:739
  539.8 22.7 %collective-permute-start.42 = (bf16[768,1024]{1,0:T(8,128)(2,1)}, bf16[768,1024]{1,0:T(8,128)(2,1)}, u32[]{:S(2)}, u32[]{:S(2)}) collective-permute-start(bf16[768,1024]{1,0:T(8,128)(2,1)} %fusion.13), channel_id=1, source_target_pairs={{0,4},{4,0},{8,12},{12,8},{16,20},{20,16},{24,28},{28,24},{1,5},{5... | collective-permute-start | bytes 4718600 | tf_op jit(solution)/shard_map/ppermute | solution.py:739
  541.1 8.1 %collective-permute-start.43 = (bf16[192,768]{1,0:T(8,128)(2,1)S(1)}, bf16[192,768]{1,0:T(8,128)(2,1)S(1)}, u32[]{:S(2)}, u32[]{:S(2)}) collective-permute-start(bf16[192,768]{1,0:T(8,128)(2,1)S(1)} %copy-done.14), channel_id=1, source_target_pairs={{0,8},{4,12},{8,0},{12,4},{16,24},{20,28},{24,16},{28,20},{1,9},{5... | collective-permute-start | bytes 884744 | tf_op jit(solution)/shard_map/ppermute | solution.py:739
  546.1 9.4 %collective-permute-start.46 = (bf16[192,768]{1,0:T(8,128)(2,1)S(1)}, bf16[192,768]{1,0:T(8,128)(2,1)S(1)}, u32[]{:S(2)}, u32[]{:S(2)}) collective-permute-start(bf16[192,768]{1,0:T(8,128)(2,1)S(1)} %add_convert_fusion.7), channel_id=1, source_target_pairs={{0,8},{4,12},{8,0},{12,4},{16,24},{20,28},{24,16},{28,20},{1,9},{5... | collective-permute-start | bytes 884744 | tf_op jit(solution)/shard_map/ppermute | solution.py:739
  551.5 25.2 %collective-permute-start.41 = (bf16[192,2560]{1,0:T(8,128)(2,1)S(1)}, bf16[192,2560]{1,0:T(8,128)(2,1)}, u32[]{:S(2)}, u32[]{:S(2)}) collective-permute-start(bf16[192,2560]{1,0:T(8,128)(2,1)S(1)} %add_convert_fusion.5), channel_id=1, source_target_pairs={{0,16},{4,20},{8,24},{12,28},{16,0},{20,4},{24,8},{28,12},{1,17},{... | collective-permute-start | bytes 2949128 | tf_op jit(solution)/shard_map/ppermute | solution.py:739
  556.6 24.9 %collective-permute-start.47 = (bf16[192,1536]{1,0:T(8,128)(2,1)}, bf16[192,1536]{1,0:T(8,128)(2,1)S(1)}, u32[]{:S(2)}, u32[]{:S(2)}) collective-permute-start(bf16[192,1536]{1,0:T(8,128)(2,1)} %pad_maximum_fusion.22), channel_id=1, source_target_pairs={{0,4},{4,0},{8,12},{12,8},{16,20},{20,16},{24,28},{28,24},{1,5},{5... | collective-permute-start | bytes 1769480 | tf_op jit(solution)/shard_map/ppermute | solution.py:739
  578.2 20.0 %collective-permute-start.53 = (bf16[192,2560]{1,0:T(8,128)(2,1)S(1)}, bf16[192,2560]{1,0:T(8,128)(2,1)S(1)}, u32[]{:S(2)}, u32[]{:S(2)}) collective-permute-start(bf16[192,2560]{1,0:T(8,128)(2,1)S(1)} %add_convert_fusion.4), channel_id=1, source_target_pairs={{0,4},{4,0},{8,12},{12,8},{16,20},{20,16},{24,28},{28,24},{1,5},{5... | collective-permute-start | bytes 2949128 | tf_op jit(solution)/shard_map/ppermute | solution.py:739
  602.9 8.8 %collective-permute-start.48 = (bf16[96,1024]{1,0:T(8,128)(2,1)S(1)}, bf16[96,1024]{1,0:T(8,128)(2,1)S(1)}, u32[]{:S(2)}, u32[]{:S(2)}) collective-permute-start(bf16[96,1024]{1,0:T(8,128)(2,1)S(1)} %get-tuple-element.391), channel_id=1, source_target_pairs={{0,8},{4,12},{8,0},{12,4},{16,24},{20,28},{24,16},{28,20},{1,9},{5... | collective-permute-start | bytes 589832 | tf_op jit(solution)/shard_map/ppermute | solution.py:739
  (96 other events, 697.9 us)
Sparse Core Ops, SparseCore 0:
  10.4 39.8 all-gather.8
  51.8 28.6 all-gather.10
  82.1 29.5 all-gather.16
  119.8 34.0 all-gather.12
  157.0 48.7 all-gather.14
  315.6 27.1 reduce-scatter.6
  345.2 27.8 reduce-scatter.8
  400.4 33.7 reduce-scatter.10
  462.4 27.4 reduce-scatter.12
  492.0 27.8 reduce-scatter.14
  568.2 33.0 reduce-scatter.16

commit v4 on v3

--- a/solution.py
+++ b/solution.py
@@ -1043,8 +1043,8 @@
 
         came = (swapped(far_gate, "seq", 1), swapped(far_out, "seq", 1))
         held, orders, stages = all_states(state, lambda before: (near0[2], came), second_half)
-        half_gate = half_product(normed, tied(dz, near1[2]), HZ, core, came[0])
-        half_out = half_product(low, tied(gb, near1[2]), HD, core, came[1])
+        half_gate = half_product(normed, tied(dz, *stages[1]), HZ, core, came[0])
+        half_out = half_product(low, tied(gb, *stages[1]), HD, core, came[1])
         grad_out, grad_gate = part_sum(half_out), part_sum(half_gate)
         later = joined_states(held, orders, logs, False)
         later = tied(later, half_out, half_gate)

time: 651 us -> 637 us (0.978)
  waiting for transfers between devices: 84.4 us -> 73.6 us
    ppermute x54, waiting for transfers between devices: 56.3 us -> 42.7 us  [swapped(): lax.ppermute(value, axis, [(source, source ^ bit) for source in range(cou...]
  transfers between devices with their start and end apart: 70 -> 70, of which waited for: 20 -> 19; matrix products, arithmetic and copies ran while one was open for 20% -> 20% of each run, Pallas kernels for 38% -> 41%
where the time goes in v4:
time: 637 us; the launch traced here: 627 us
  Pallas kernels  295 us (46%)
  waiting for transfers between devices  73.6 us (12%)
  starting transfers between devices  72.5 us (11%)
  local copies, waits for them, and re-layouts  67.5 us (11%)
  other arithmetic  47.6 us (7%)
  matrix products  44.3 us (7%)
  between operations  15.9 us (2%)
  blocking collectives  11.2 us (2%)
    pallas_call x2, Pallas kernels, across_back(): pl.pallas_call(across_back_kernel, grid=(n,), in_specs=[turned(E), turned...  63.2 us
    pallas_call x4, Pallas kernels, within_back(): pl.pallas_call(partial(within_back_kernel, range(part * size, (part + 1)...  55.9 us
    ppermute x54, starting transfers between devices, swapped(): lax.ppermute(value, axis, [(source, source ^ bit) for source in range(cou...  55.5 us
    dot_general x12, matrix products, tn(): lax.dot_general(a, b, (((0,), (0,)), ((), ())), preferred_element_type=f32)  44.3 us
    ppermute x54, waiting for transfers between devices, swapped(): lax.ppermute(value, axis, [(source, source ^ bit) for source in range(cou...  42.7 us
    pallas_call x2, Pallas kernels, open_back(): pl.pallas_call(open_back_kernel, grid=(n,), in_specs=[SMEM, turned(D), fu...  41.7 us
    pallas_call x2, Pallas kernels, across(): pl.pallas_call(across_kernel, grid=(t // TT,), in_specs=[SMEM, rows(E), r...  34.1 us
    pallas_call x2, Pallas kernels, prepare(): pl.pallas_call(prepare_kernel, grid=(t // TT,), in_specs=[rows(CV), full(...  30 us
  transfers between devices with their start and end apart: 70, of which 19 were waited for; matrix products, arithmetic and copies ran while one was open for 20% of the time, Pallas kernels for 41%

profile of v4, /device:TPU:1, one launch (start us, length us, event | category | flops | bytes accessed | tf_op | source)
XLA Modules:
  0.0 627.3 jit_solution(6352433453549557791)
XLA Ops:
  11.3 4.5 collective-permute-start.2
  19.1 11.2 %all-gather.2 = bf16[4,2,2834]{2,1,0:T(2,128)(2,1)S(1)} all-gather(bf16[1,2,2834]{2,1,0:T(2,128)(2,1)S(1)} %bitcast.317), channel_id=2, replica_groups=mesh['seq'=8,'fsdp'=4] {'fsdp'}, dimensions={0}, use_global_device_ids=true | all-gather | bytes 56680 | tf_op jit(solution)/shard_map/all_gather | solution.py:951
  31.9 18.4 %all-gather.9.cloned.1.call-done.mine_ref.xm_ref = bf16[768,1024]{1,0:T(8,128)(2,1)} async-done(((bf16[192,1024]{1,0:T(8,128)(2,1)}), bf16[768,1024]{1,0:T(8,128)(2,1)}) %all-gather.9.cloned.1.call-update) | async-done | bytes 1572880 | tf_op jit(solution)/shard_map/all_gather | solution.py:808
  55.4 8.0 %project.2 = (bf16[1024,768]{1,0:T(8,128)(2,1)}, bf16[1024,1792]{1,0:T(8,128)(2,1)}, f32[1024,128]{1,0:T(8,128)}) custom-call(s32[1]{0:T(128)} %bitcast.core_ref, bf16[1024,768]{1,0:T(8,128)(2,1)} %bitcast.338, f32[1,768]{1,0:T(1,128)} %broadcast_in_dim_reshape_squeeze.18.gain_ref, bf16[768,1024]{1,0:T(8,128)(2,1)} %all-gather.9.cloned.1.call-done.mine_ref.xm_ref, ...), custom_call_target="tpu_custom_call" | custom-call | flops 8000000000 | bytes 24000000 | tf_op jit(solution)/shard_map/project/pallas_call | solution.py:130
  64.2 3.0 collective-permute-start.1
  69.1 15.0 %prepare.2 = (bf16[1024,1792]{1,0:T(8,128)(2,1)}, bf16[1024,1536]{1,0:T(8,128)(2,1)}, bf16[1024,256]{1,0:T(8,128)(2,1)}, f32[1024,128]{1,0:T(8,128)}, f32[1024,1...) custom-call(bf16[1024,1792]{1,0:T(8,128)(2,1)} %get-tuple-element.158.xc_ref.halo_ref, ...), custom_call_target="tpu_custom_call" | custom-call | flops 15000000512 | bytes 45000000 | tf_op jit(solution)/shard_map/prepare/pallas_call | solution.py:230
  89.4 7.8 %within.2.yi_ref = bf16[1024,1536]{1,0:T(8,128)(2,1)} custom-call(bf16[1024,1536]{1,0:T(8,128)(2,1)} %get-tuple-element.241.x_ref, bf16[1024,256]{1,0:T(8,128)(2,1)} %get-tuple-element.161.bc_ref, f32[1024,128]{1,0:T(8,128)} %get-tuple-element.162.cum_ref, f32[32,1024]{1,0:T(8,128)} %get-tuple-element.163.cumt_ref, f32[32,1024]{1,0:T(8,128)} %get-tuple-element.164.dtt_ref, ...), custom_call_target="tpu_custom_call" | custom-call | flops 8000000000 | bytes 24000000 | tf_op jit(solution)/shard_map/within/pallas_call | solution.py:284
  98.8 10.4 %collective-permute-done.7 = bf16[2,144,768]{2,1,0:T(8,128)(2,1)S(1)} collective-permute-done((bf16[2,144,768]{2,1,0:T(8,128)(2,1)S(1)}, bf16[2,144,768]{2,1,0:T(8,128)(2,1)S(1)}, u32[]{:S(2)}, u32[]{:S(2)}) %collective-permute-start.7) | collective-permute-done | bytes 442400 | tf_op jit(solution)/shard_map/ppermute | solution.py:739
  111.4 6.3 %project_gate.2.z_ref = bf16[1024,1536]{1,0:T(8,128)(2,1)} custom-call(s32[1]{0:T(128)} %bitcast.core_ref, bf16[1024,768]{1,0:T(8,128)(2,1)} %get-tuple-element.170.normed_ref, bf16[768,768]{1,0:T(8,128)(2,1)} %all-gather.11.cloned.1.call-done.mine_ref.zm_ref, bf16[768,768]{1,0:T(8,128)(2,1)} %copy-done.61), custom_call_target="tpu_custom_call" | custom-call | flops 6000000000 | bytes 18000000 | tf_op jit(solution)/shard_map/project_gate/pallas_call | solution.py:150
  134.6 17.1 %across.2 = (bf16[1024,1536]{1,0:T(8,128)(2,1)}, bf16[1024,1536]{1,0:T(8,128)(2,1)}, f32[1024,768]{1,0:T(8,128)}, bf16[8,128,1536]{2,1,0:T(8,128)(2,1)}) custom-call(s32[1]{0:T(128)} %bitcast.core_ref, bf16[1024,1536]{1,0:T(8,128)(2,1)} %within.2.yi_ref, bf16[1024,1536]{1,0:T(8,128)(2,1)} %get-tuple-element.241.x_ref, ...), custom_call_target="tpu_custom_call" | custom-call | flops 16000000000 | bytes 48000000 | tf_op jit(solution)/shard_map/across/pallas_call | solution.py:350
  159.1 8.4 %project.3 = (bf16[1024,768]{1,0:T(8,128)(2,1)}, bf16[1024,1792]{1,0:T(8,128)(2,1)}, f32[1024,128]{1,0:T(8,128)}) custom-call(s32[1]{0:T(128)} %bitcast.core_ref, f32[1024,768]{1,0:T(8,128)} %get-tuple-element.177.x_ref.res_ref, f32[1,768]{1,0:T(1,128)} %broadcast_in_dim_reshape_squeeze.21.gain_ref, ...), custom_call_target="tpu_custom_call" | custom-call | flops 8000000000 | bytes 24000000 | tf_op jit(solution)/shard_map/project/pallas_call | solution.py:130
  168.3 3.5 collective-permute-start.12
  173.1 15.0 %prepare.3 = (bf16[1024,1792]{1,0:T(8,128)(2,1)}, bf16[1024,1536]{1,0:T(8,128)(2,1)}, bf16[1024,256]{1,0:T(8,128)(2,1)}, f32[1024,128]{1,0:T(8,128)}, f32[1024,1...) custom-call(bf16[1024,1792]{1,0:T(8,128)(2,1)} %get-tuple-element.179.xc_ref.halo_ref, ...), custom_call_target="tpu_custom_call" | custom-call | flops 15000000512 | bytes 45000000 | tf_op jit(solution)/shard_map/prepare/pallas_call | solution.py:230
  190.5 7.8 %within.3.yi_ref = bf16[1024,1536]{1,0:T(8,128)(2,1)} custom-call(bf16[1024,1536]{1,0:T(8,128)(2,1)} %get-tuple-element.210.x_ref, bf16[1024,256]{1,0:T(8,128)(2,1)} %get-tuple-element.182.bc_ref, f32[1024,128]{1,0:T(8,128)} %get-tuple-element.183.cum_ref, f32[32,1024]{1,0:T(8,128)} %get-tuple-element.184.cumt_ref, f32[32,1024]{1,0:T(8,128)} %get-tuple-element.185.dtt_ref, ...), custom_call_target="tpu_custom_call" | custom-call | flops 8000000000 | bytes 24000000 | tf_op jit(solution)/shard_map/within/pallas_call | solution.py:284
  200.1 7.1 %collective-permute-done.16 = bf16[2,144,768]{2,1,0:T(8,128)(2,1)S(1)} collective-permute-done((bf16[2,144,768]{2,1,0:T(8,128)(2,1)S(1)}, bf16[2,144,768]{2,1,0:T(8,128)(2,1)S(1)}, u32[]{:S(2)}, u32[]{:S(2)}) %collective-permute-start.16) | collective-permute-done | bytes 442400 | tf_op jit(solution)/shard_map/ppermute | solution.py:739
  209.5 3.9 collective-permute-start.19
  230.3 6.4 %project_gate.3.z_ref = bf16[1024,1536]{1,0:T(8,128)(2,1)} custom-call(s32[1]{0:T(128)} %bitcast.core_ref, bf16[1024,768]{1,0:T(8,128)(2,1)} %get-tuple-element.191.normed_ref, bf16[768,768]{1,0:T(8,128)(2,1)} %get-tuple-element.372.mine_ref.zm_ref, bf16[768,768]{1,0:T(8,128)(2,1)} %collective-permute-done.17.other_ref.zo_ref), custom_call_target="tpu_custom_call" | custom-call | flops 6000000000 | bytes 18000000 | tf_op jit(solution)/shard_map/project_gate/pallas_call | solution.py:150
  236.6 17.0 %across.3 = (bf16[1024,1536]{1,0:T(8,128)(2,1)}, bf16[1024,1536]{1,0:T(8,128)(2,1)}, bf16[1024,768]{1,0:T(8,128)(2,1)}, bf16[8,128,1536]{2,1,0:T(8,128)(2,1)}) custom-call(s32[1]{0:T(128)} %bitcast.core_ref, bf16[1024,1536]{1,0:T(8,128)(2,1)} %within.3.yi_ref, bf16[1024,1536]{1,0:T(8,128)(2,1)} %get-tuple-element.210.x_ref, ...), custom_call_target="tpu_custom_call" | custom-call | flops 16000000000 | bytes 48000000 | tf_op jit(solution)/shard_map/across/pallas_call | solution.py:350
  253.6 20.8 %open_back.2 = (bf16[1024,1536]{1,0:T(8,128)(2,1)}, bf16[1024,1536]{1,0:T(8,128)(2,1)}, bf16[1024,768]{1,0:T(8,128)(2,1)}, f32[8,1536]{1,0:T(8,128)}, bf16[128,1536]{1,0:T(8,128)(2,1)}) custom-call(s32[1]{0:T(128)} %bitcast.core_ref, bf16[1024,768]{1,0:T(8,128)(2,1)} %bitcast.336, bf16[1536,384]{1,0:T(8,128)(2,1)} %bitcast.67.mine_ref, ...), custom_call_target="tpu_custom_call" | custom-call | flops 20000000000 | bytes 60000000 | tf_op jit(solution)/shard_map/open_back/pallas_call | solution.py:436
  274.5 4.1 convolution_convert_fusion.1
  283.2 13.7 %within_back.4 = (bf16[1024,768]{1,0:T(8,128)(2,1)}, f32[1024,256]{1,0:T(8,128)}, f32[1024,128]{1,0:T(8,128)}) custom-call(bf16[1024,1536]{1,0:T(8,128)(2,1)} %get-tuple-element.210.x_ref, bf16[1024,1536]{1,0:T(8,128)(2,1)} %get-tuple-element.201.dy_ref, bf16[1024,256]{1,0:T(8,128)(2,1)} %get-tuple-element.182.bc_ref, ...), custom_call_target="tpu_custom_call" | custom-call | flops 12000000000 | bytes 36000000 | tf_op jit(solution)/shard_map/within_back/pallas_call | solution.py:513
  298.6 14.3 %within_back.5 = (bf16[1024,768]{1,0:T(8,128)(2,1)}, f32[1024,256]{1,0:T(8,128)}, f32[1024,128]{1,0:T(8,128)}) custom-call(bf16[1024,1536]{1,0:T(8,128)(2,1)} %get-tuple-element.210.x_ref, bf16[1024,1536]{1,0:T(8,128)(2,1)} %get-tuple-element.201.dy_ref, bf16[1024,256]{1,0:T(8,128)(2,1)} %get-tuple-element.182.bc_ref, ...), custom_call_target="tpu_custom_call" | custom-call | flops 12000000000 | bytes 36000000 | tf_op jit(solution)/shard_map/within_back/pallas_call | solution.py:513
  314.7 2.8 fusion
  322.5 4.3 add_convert_fusion.3
  331.0 31.6 %across_back.2 = (bf16[1024,2048]{1,0:T(8,128)(2,1)}, f32[8,1792]{1,0:T(8,128)}, f32[8,128]{1,0:T(8,128)}, f32[8,1792]{1,0:T(8,128)}) custom-call(bf16[1024,1536]{1,0:T(8,128)(2,1)} %get-tuple-element.210.x_ref, bf16[1024,1792]{1,0:T(8,128)(2,1)} %get-tuple-element.200.pre_ref, bf16[1024,1792]{1,0:T(8,128)(2,1)} %get-tuple-element.179.xc_ref.halo_ref, ...), custom_call_target="tpu_custom_call" | custom-call | flops 31000000512 | bytes 93000000 | tf_op jit(solution)/shard_map/across_back/pallas_call | solution.py:660
  366.7 3.2 collective-permute-done.29
  372.3 3.5 reduce-scatter.9.cloned.1.call-done
  375.7 4.6 fusion.10
  381.1 12.5 %close_back.2 = (f32[1024,768]{1,0:T(8,128)}, f32[8,768]{1,0:T(8,128)}) custom-call(s32[1]{0:T(128)} %bitcast.core_ref, bf16[1024,1536]{1,0:T(8,128)(2,1)} %get-tuple-element.221.dz_ref, bf16[1024,2048]{1,0:T(8,128)(2,1)} %scatter.6.dxc_ref, bf16[768,768]{1,0:T(8,128)(2,1)} %get-tuple-element.372.mine_ref.zm_ref, ...), custom_call_target="tpu_custom_call" | custom-call | flops 12000000000 | bytes 36000000 | tf_op jit(solution)/shard_map/close_back/pallas_call | solution.py:716
  393.7 3.0 add_convert_fusion.1
  396.8 20.8 %open_back.3 = (bf16[1024,1536]{1,0:T(8,128)(2,1)}, bf16[1024,1536]{1,0:T(8,128)(2,1)}, bf16[1024,768]{1,0:T(8,128)(2,1)}, f32[8,1536]{1,0:T(8,128)}, bf16[128,1536]{1,0:T(8,128)(2,1)}) custom-call(s32[1]{0:T(128)} %bitcast.core_ref, f32[1024,768]{1,0:T(8,128)} %get-tuple-element.268.g_ref, bf16[1536,384]{1,0:T(8,128)(2,1)} %bitcast.343, ...), custom_call_target="tpu_custom_call" | custom-call | flops 20000000000 | bytes 60000000 | tf_op jit(solution)/shard_map/open_back/pallas_call | solution.py:436
  417.7 3.0 fusion.27
  420.7 2.9 convolution_convert_fusion
  426.6 13.7 %within_back.6 = (bf16[1024,768]{1,0:T(8,128)(2,1)}, f32[1024,256]{1,0:T(8,128)}, f32[1024,128]{1,0:T(8,128)}) custom-call(bf16[1024,1536]{1,0:T(8,128)(2,1)} %get-tuple-element.241.x_ref, bf16[1024,1536]{1,0:T(8,128)(2,1)} %get-tuple-element.232.dy_ref, bf16[1024,256]{1,0:T(8,128)(2,1)} %get-tuple-element.161.bc_ref, ...), custom_call_target="tpu_custom_call" | custom-call | flops 12000000000 | bytes 36000000 | tf_op jit(solution)/shard_map/within_back/pallas_call | solution.py:513
  441.1 14.2 %within_back.7 = (bf16[1024,768]{1,0:T(8,128)(2,1)}, f32[1024,256]{1,0:T(8,128)}, f32[1024,128]{1,0:T(8,128)}) custom-call(bf16[1024,1536]{1,0:T(8,128)(2,1)} %get-tuple-element.241.x_ref, bf16[1024,1536]{1,0:T(8,128)(2,1)} %get-tuple-element.232.dy_ref, bf16[1024,256]{1,0:T(8,128)(2,1)} %get-tuple-element.161.bc_ref, ...), custom_call_target="tpu_custom_call" | custom-call | flops 12000000000 | bytes 36000000 | tf_op jit(solution)/shard_map/within_back/pallas_call | solution.py:513
  457.2 2.8 fusion.1
  467.7 4.2 add_convert_fusion.2
  478.7 31.6 %across_back.3 = (bf16[1024,2048]{1,0:T(8,128)(2,1)}, f32[8,1792]{1,0:T(8,128)}, f32[8,128]{1,0:T(8,128)}, f32[8,1792]{1,0:T(8,128)}) custom-call(bf16[1024,1536]{1,0:T(8,128)(2,1)} %get-tuple-element.241.x_ref, bf16[1024,1792]{1,0:T(8,128)(2,1)} %get-tuple-element.231.pre_ref, bf16[1024,1792]{1,0:T(8,128)(2,1)} %get-tuple-element.158.xc_ref.halo_ref, ...), custom_call_target="tpu_custom_call" | custom-call | flops 31000000512 | bytes 93000000 | tf_op jit(solution)/shard_map/across_back/pallas_call | solution.py:660
  519.9 4.6 fusion.13
  530.0 3.4 collective-permute-done.45
  544.5 6.0 collective-permute-start.47
  550.5 5.5 add_convert_fusion
  556.0 8.6 %collective-permute-done.41 = bf16[192,2560]{1,0:T(8,128)(2,1)} collective-permute-done((bf16[192,2560]{1,0:T(8,128)(2,1)S(1)}, bf16[192,2560]{1,0:T(8,128)(2,1)}, u32[]{:S(2)}, u32[]{:S(2)}) %collective-permute-start.41) | collective-permute-done | bytes 983072 | tf_op jit(solution)/shard_map/ppermute | solution.py:739
  566.1 3.3 collective-permute-start.53
  572.6 12.5 %close_back.3 = (f32[1024,768]{1,0:T(8,128)}, f32[8,768]{1,0:T(8,128)}) custom-call(s32[1]{0:T(128)} %bitcast.core_ref, bf16[1024,1536]{1,0:T(8,128)(2,1)} %get-tuple-element.252.dz_ref, bf16[1024,2048]{1,0:T(8,128)(2,1)} %scatter.9.dxc_ref, bf16[768,768]{1,0:T(8,128)(2,1)} %all-gather.11.cloned.1.call-done.mine_ref.zm_ref, bf16[768,768]{1,0:T(8,128)(2,1)} %copy-done.61, ...), custom_call_target="tpu_custom_call" | custom-call | flops 12000000000 | bytes 36000000 | tf_op jit(solution)/shard_map/close_back/pallas_call | solution.py:716
  595.4 2.9 collective-permute-start.56
  605.0 3.3 collective-permute-done.51
  616.5 4.0 maximum_convert_fusion
  (529 shorter events, 174.7 us)
Async XLA Ops:
  7.2 43.1 %all-gather.9.cloned.1.call-start = ((), (), s32[]{:S(2)}) async-start(), calls=%async_computation.6 | async-start | bytes 1966080 | tf_op jit(solution)/shard_map/all_gather | solution.py:808
  10.3 76.3 %all-gather.11.cloned.1.call-start = ((), (), s32[]{:S(2)}) async-start(), calls=%async_computation.7 | async-start | bytes 1474560 | tf_op jit(solution)/shard_map/all_gather | solution.py:808
  11.1 112.1 %all-gather.17.cloned.1.call-start = ((), (), s32[]{:S(2)}) async-start(), calls=%async_computation.16 | async-start | bytes 1474560 | tf_op jit(solution)/shard_map/all_gather | solution.py:808
  11.3 43.9 %collective-permute-start.2 = (s32[3]{0:T(128)S(1)}, s32[3]{0:T(128)S(1)}, u32[]{:S(2)}, u32[]{:S(2)}) collective-permute-start(s32[3]{0:T(128)S(1)} %slice_bitcast_fusion.10), channel_id=1, source_target_pairs={{0,4},{4,8},{8,12},{12,16},{16,20},{20,24},{24,28},{1,5},{5,9},{9,... | collective-permute-start | bytes 44 | tf_op jit(solution)/shard_map/ppermute | solution.py:734
  18.8 135.2 %all-gather.13.cloned.1.call-start = ((), (), s32[]{:S(2)}) async-start(), calls=%async_computation.8 | async-start | bytes 1966080 | tf_op jit(solution)/shard_map/all_gather | solution.py:808
  85.2 11.9 %collective-permute-start.4 = (bf16[1,144,768]{2,1,0:T(8,128)(2,1)S(1)}, bf16[1,144,768]{2,1,0:T(8,128)(2,1)S(1)}, u32[]{:S(2)}, u32[]{:S(2)}) collective-permute-start(bf16[1,144,768]{2,1,0:T(8,128)(2,1)S(1)} %get-tuple-element.387), channel_id=1, source_target_pairs={{0,16},{4,20},{8,24},{12,28},{16,0},{20,4},{24,8},{28,12},{1,17},{... | collective-permute-start | bytes 663560 | tf_op jit(solution)/shard_map/ppermute | solution.py:739
  86.3 10.9 %collective-permute-start.3 = (bf16[1,144,768]{2,1,0:T(8,128)(2,1)S(1)}, bf16[1,144,768]{2,1,0:T(8,128)(2,1)S(1)}, u32[]{:S(2)}, u32[]{:S(2)}) collective-permute-start(bf16[1,144,768]{2,1,0:T(8,128)(2,1)S(1)} %get-tuple-element.388), channel_id=1, source_target_pairs={{0,8},{4,12},{8,0},{12,4},{16,24},{20,28},{24,16},{28,20},{1,9},{5... | collective-permute-start | bytes 663560 | tf_op jit(solution)/shard_map/ppermute | solution.py:739
  86.6 23.8 %collective-permute-start.5 = (bf16[768,768]{1,0:T(8,128)(2,1)}, bf16[768,768]{1,0:T(8,128)(2,1)S(1)}, u32[]{:S(2)}, u32[]{:S(2)}) collective-permute-start(bf16[768,768]{1,0:T(8,128)(2,1)} %all-gather.11.cloned.1.call-done.mine_ref.zm_ref), channel_id=1, source_target_pairs={{0,4},{4,0},{8,12},{12,8},{16,20},{20,16},{24,28},{28,24},{1,5},{5... | collective-permute-start | bytes 3538952 | tf_op jit(solution)/shard_map/ppermute | solution.py:739
  97.3 12.0 %collective-permute-start.7 = (bf16[2,144,768]{2,1,0:T(8,128)(2,1)S(1)}, bf16[2,144,768]{2,1,0:T(8,128)(2,1)S(1)}, u32[]{:S(2)}, u32[]{:S(2)}) collective-permute-start(bf16[2,144,768]{2,1,0:T(8,128)(2,1)S(1)} %pad_maximum_fusion.25), channel_id=1, source_target_pairs={{0,8},{4,12},{8,0},{12,4},{16,24},{20,28},{24,16},{28,20},{1,9},{5... | collective-permute-start | bytes 1327112 | tf_op jit(solution)/shard_map/ppermute | solution.py:739
  98.7 11.5 %collective-permute-start.6 = (bf16[2,144,768]{2,1,0:T(8,128)(2,1)S(1)}, bf16[2,144,768]{2,1,0:T(8,128)(2,1)S(1)}, u32[]{:S(2)}, u32[]{:S(2)}) collective-permute-start(bf16[2,144,768]{2,1,0:T(8,128)(2,1)S(1)} %pad_maximum_fusion.24), channel_id=1, source_target_pairs={{0,16},{4,20},{8,24},{12,28},{16,0},{20,4},{24,8},{28,12},{1,17},{... | collective-permute-start | bytes 1327112 | tf_op jit(solution)/shard_map/ppermute | solution.py:739
  119.7 94.5 %all-gather.15.cloned.1.call-start = ((), (), s32[]{:S(2)}) async-start(), calls=%async_computation.9 | async-start | bytes 2949120 | tf_op jit(solution)/shard_map/all_gather | solution.py:808
  123.2 11.4 %collective-permute-start.10 = (bf16[1536,384]{1,0:T(8,128)(2,1)}, bf16[1536,384]{1,0:T(8,128)(2,1)}, u32[]{:S(2)}, u32[]{:S(2)}) collective-permute-start(bf16[1536,384]{1,0:T(8,128)(2,1)} %bitcast.341), channel_id=1, source_target_pairs={{0,4},{4,0},{8,12},{12,8},{16,20},{20,16},{24,28},{28,24},{1,5},{5... | collective-permute-start | bytes 3538952 | tf_op jit(solution)/shard_map/ppermute | solution.py:739
  156.9 205.7 %reduce-scatter.7.cloned.1.call-start = ((), (), s32[]{:S(2)}) async-start(), calls=%async_computation.10 | async-start | bytes 1474560 | tf_op jit(solution)/shard_map/reduce_scatter | solution.py:824
  189.2 9.1 %collective-permute-start.14 = (bf16[1,144,768]{2,1,0:T(8,128)(2,1)S(1)}, bf16[1,144,768]{2,1,0:T(8,128)(2,1)S(1)}, u32[]{:S(2)}, u32[]{:S(2)}) collective-permute-start(bf16[1,144,768]{2,1,0:T(8,128)(2,1)S(1)} %get-tuple-element.385), channel_id=1, source_target_pairs={{0,16},{4,20},{8,24},{12,28},{16,0},{20,4},{24,8},{28,12},{1,17},{... | collective-permute-start | bytes 663560 | tf_op jit(solution)/shard_map/ppermute | solution.py:739
  198.4 8.9 %collective-permute-start.16 = (bf16[2,144,768]{2,1,0:T(8,128)(2,1)S(1)}, bf16[2,144,768]{2,1,0:T(8,128)(2,1)S(1)}, u32[]{:S(2)}, u32[]{:S(2)}) collective-permute-start(bf16[2,144,768]{2,1,0:T(8,128)(2,1)S(1)} %pad_maximum_fusion.27), channel_id=1, source_target_pairs={{0,8},{4,12},{8,0},{12,4},{16,24},{20,28},{24,16},{28,20},{1,9},{5... | collective-permute-start | bytes 1327112 | tf_op jit(solution)/shard_map/ppermute | solution.py:739
  199.8 8.7 %collective-permute-start.15 = (bf16[2,144,768]{2,1,0:T(8,128)(2,1)S(1)}, bf16[2,144,768]{2,1,0:T(8,128)(2,1)S(1)}, u32[]{:S(2)}, u32[]{:S(2)}) collective-permute-start(bf16[2,144,768]{2,1,0:T(8,128)(2,1)S(1)} %pad_maximum_fusion.26), channel_id=1, source_target_pairs={{0,16},{4,20},{8,24},{12,28},{16,0},{20,4},{24,8},{28,12},{1,17},{... | collective-permute-start | bytes 1327112 | tf_op jit(solution)/shard_map/ppermute | solution.py:739
  209.5 9.6 %collective-permute-start.19 = (bf16[4,144,768]{2,1,0:T(8,128)(2,1)S(1)}, bf16[4,144,768]{2,1,0:T(8,128)(2,1)}, u32[]{:S(2)}, u32[]{:S(2)}) collective-permute-start(bf16[4,144,768]{2,1,0:T(8,128)(2,1)S(1)} %pad_maximum_fusion.12), channel_id=1, source_target_pairs={{0,4},{4,0},{8,12},{12,8},{16,20},{20,16},{24,28},{28,24},{1,5},{5... | collective-permute-start | bytes 2654216 | tf_op jit(solution)/shard_map/ppermute | solution.py:739
  217.1 13.2 %collective-permute-start.17 = (bf16[768,768]{1,0:T(8,128)(2,1)}, bf16[768,768]{1,0:T(8,128)(2,1)}, u32[]{:S(2)}, u32[]{:S(2)}) collective-permute-start(bf16[768,768]{1,0:T(8,128)(2,1)} %get-tuple-element.372.mine_ref.zm_ref), channel_id=1, source_target_pairs={{0,4},{4,0},{8,12},{12,8},{16,20},{20,16},{24,28},{28,24},{1,5},{5... | collective-permute-start | bytes 3538952 | tf_op jit(solution)/shard_map/ppermute | solution.py:739
  219.1 17.5 %collective-permute-start.20 = (bf16[1536,384]{1,0:T(8,128)(2,1)}, bf16[1536,384]{1,0:T(8,128)(2,1)}, u32[]{:S(2)}, u32[]{:S(2)}) collective-permute-start(bf16[1536,384]{1,0:T(8,128)(2,1)} %bitcast.67.mine_ref), channel_id=1, source_target_pairs={{0,4},{4,0},{8,12},{12,8},{16,20},{20,16},{24,28},{28,24},{1,5},{5... | collective-permute-start | bytes 3538952 | tf_op jit(solution)/shard_map/ppermute | solution.py:739
  278.6 18.5 %collective-permute-start.24 = (bf16[1536,384]{1,0:T(8,128)(2,1)S(1)}, bf16[1536,384]{1,0:T(8,128)(2,1)S(1)}, u32[]{:S(2)}, u32[]{:S(2)}) collective-permute-start(bf16[1536,384]{1,0:T(8,128)(2,1)S(1)} %convolution_convert_fusion.1), channel_id=1, source_target_pairs={{0,4},{4,0},{8,12},{12,8},{16,20},{20,16},{24,28},{28,24},{1,5},{5... | collective-permute-start | bytes 3538952 | tf_op jit(solution)/shard_map/ppermute | solution.py:739
  281.5 15.6 %collective-permute-start.23 = (bf16[768,768]{1,0:T(8,128)(2,1)}, bf16[768,768]{1,0:T(8,128)(2,1)S(1)}, u32[]{:S(2)}, u32[]{:S(2)}) collective-permute-start(bf16[768,768]{1,0:T(8,128)(2,1)} %fusion.24), channel_id=1, source_target_pairs={{0,4},{4,0},{8,12},{12,8},{16,20},{20,16},{24,28},{28,24},{1,5},{5... | collective-permute-start | bytes 3538952 | tf_op jit(solution)/shard_map/ppermute | solution.py:739
  281.6 15.3 %collective-permute-start.22 = (bf16[1,128,768]{2,1,0:T(8,128)(2,1)S(1)}, bf16[1,128,768]{2,1,0:T(8,128)(2,1)S(1)}, u32[]{:S(2)}, u32[]{:S(2)}) collective-permute-start(bf16[1,128,768]{2,1,0:T(8,128)(2,1)S(1)} %get-tuple-element.395), channel_id=1, source_target_pairs={{0,16},{4,20},{8,24},{12,28},{16,0},{20,4},{24,8},{28,12},{1,17},{... | collective-permute-start | bytes 589832 | tf_op jit(solution)/shard_map/ppermute | solution.py:739
  282.0 15.0 %collective-permute-start.21 = (bf16[1,128,768]{2,1,0:T(8,128)(2,1)S(1)}, bf16[1,128,768]{2,1,0:T(8,128)(2,1)S(1)}, u32[]{:S(2)}, u32[]{:S(2)}) collective-permute-start(bf16[1,128,768]{2,1,0:T(8,128)(2,1)S(1)} %get-tuple-element.396), channel_id=1, source_target_pairs={{0,8},{4,12},{8,0},{12,4},{16,24},{20,28},{24,16},{28,20},{1,9},{5... | collective-permute-start | bytes 589832 | tf_op jit(solution)/shard_map/ppermute | solution.py:739
  297.0 15.8 %collective-permute-start.26 = (bf16[2,128,768]{2,1,0:T(8,128)(2,1)S(1)}, bf16[2,128,768]{2,1,0:T(8,128)(2,1)S(1)}, u32[]{:S(2)}, u32[]{:S(2)}) collective-permute-start(bf16[2,128,768]{2,1,0:T(8,128)(2,1)S(1)} %pad_maximum_fusion.29), channel_id=1, source_target_pairs={{0,8},{4,12},{8,0},{12,4},{16,24},{20,28},{24,16},{28,20},{1,9},{5... | collective-permute-start | bytes 1179656 | tf_op jit(solution)/shard_map/ppermute | solution.py:739
  297.4 15.5 %collective-permute-start.25 = (bf16[2,128,768]{2,1,0:T(8,128)(2,1)S(1)}, bf16[2,128,768]{2,1,0:T(8,128)(2,1)S(1)}, u32[]{:S(2)}, u32[]{:S(2)}) collective-permute-start(bf16[2,128,768]{2,1,0:T(8,128)(2,1)S(1)} %pad_maximum_fusion.28), channel_id=1, source_target_pairs={{0,16},{4,20},{8,24},{12,28},{16,0},{20,4},{24,8},{28,12},{1,17},{... | collective-permute-start | bytes 1179656 | tf_op jit(solution)/shard_map/ppermute | solution.py:739
  317.6 58.1 %reduce-scatter.9.cloned.1.call-start = ((), (), s32[]{:S(2)}) async-start(), calls=%async_computation.11 | async-start | bytes 1474560 | tf_op jit(solution)/shard_map/reduce_scatter | solution.py:824
  317.7 9.2 %collective-permute-start.28 = (bf16[4,128,768]{2,1,0:T(8,128)(2,1)S(1)}, bf16[4,128,768]{2,1,0:T(8,128)(2,1)}, u32[]{:S(2)}, u32[]{:S(2)}) collective-permute-start(bf16[4,128,768]{2,1,0:T(8,128)(2,1)S(1)} %pad_maximum_fusion.16), channel_id=1, source_target_pairs={{0,4},{4,0},{8,12},{12,8},{16,20},{20,16},{24,28},{28,24},{1,5},{5... | collective-permute-start | bytes 2359304 | tf_op jit(solution)/shard_map/ppermute | solution.py:739
  326.8 149.5 %reduce-scatter.11.cloned.1.call-start = ((), (), s32[]{:S(2)}) async-start(), calls=%async_computation.12 | async-start | bytes 1966080 | tf_op jit(solution)/shard_map/reduce_scatter | solution.py:824
  380.3 13.4 %collective-permute-start.30 = (bf16[768,1024]{1,0:T(8,128)(2,1)}, bf16[768,1024]{1,0:T(8,128)(2,1)S(1)}, u32[]{:S(2)}, u32[]{:S(2)}) collective-permute-start(bf16[768,1024]{1,0:T(8,128)(2,1)} %fusion.10), channel_id=1, source_target_pairs={{0,4},{4,0},{8,12},{12,8},{16,20},{20,16},{24,28},{28,24},{1,5},{5... | collective-permute-start | bytes 4718600 | tf_op jit(solution)/shard_map/ppermute | solution.py:739
  396.7 113.8 %reduce-scatter.13.cloned.1.call-start = ((), (), s32[]{:S(2)}) async-start(), calls=%async_computation.13 | async-start | bytes 1474560 | tf_op jit(solution)/shard_map/reduce_scatter | solution.py:824
  423.6 16.8 %collective-permute-start.34 = (bf16[1536,384]{1,0:T(8,128)(2,1)}, bf16[1536,384]{1,0:T(8,128)(2,1)S(1)}, u32[]{:S(2)}, u32[]{:S(2)}) collective-permute-start(bf16[1536,384]{1,0:T(8,128)(2,1)} %convolution_convert_fusion), channel_id=1, source_target_pairs={{0,4},{4,0},{8,12},{12,8},{16,20},{20,16},{24,28},{28,24},{1,5},{5... | collective-permute-start | bytes 3538952 | tf_op jit(solution)/shard_map/ppermute | solution.py:739
  423.6 16.8 %collective-permute-start.33 = (bf16[768,768]{1,0:T(8,128)(2,1)S(1)}, bf16[768,768]{1,0:T(8,128)(2,1)S(1)}, u32[]{:S(2)}, u32[]{:S(2)}) collective-permute-start(bf16[768,768]{1,0:T(8,128)(2,1)S(1)} %fusion.27), channel_id=1, source_target_pairs={{0,4},{4,0},{8,12},{12,8},{16,20},{20,16},{24,28},{28,24},{1,5},{5... | collective-permute-start | bytes 3538952 | tf_op jit(solution)/shard_map/ppermute | solution.py:739
  424.1 16.2 %collective-permute-start.32 = (bf16[1,128,768]{2,1,0:T(8,128)(2,1)S(1)}, bf16[1,128,768]{2,1,0:T(8,128)(2,1)S(1)}, u32[]{:S(2)}, u32[]{:S(2)}) collective-permute-start(bf16[1,128,768]{2,1,0:T(8,128)(2,1)S(1)} %get-tuple-element.393), channel_id=1, source_target_pairs={{0,16},{4,20},{8,24},{12,28},{16,0},{20,4},{24,8},{28,12},{1,17},{... | collective-permute-start | bytes 589832 | tf_op jit(solution)/shard_map/ppermute | solution.py:739
  425.4 15.0 %collective-permute-start.31 = (bf16[1,128,768]{2,1,0:T(8,128)(2,1)S(1)}, bf16[1,128,768]{2,1,0:T(8,128)(2,1)S(1)}, u32[]{:S(2)}, u32[]{:S(2)}) collective-permute-start(bf16[1,128,768]{2,1,0:T(8,128)(2,1)S(1)} %get-tuple-element.394), channel_id=1, source_target_pairs={{0,8},{4,12},{8,0},{12,4},{16,24},{20,28},{24,16},{28,20},{1,9},{5... | collective-permute-start | bytes 589832 | tf_op jit(solution)/shard_map/ppermute | solution.py:739
  440.5 14.8 %collective-permute-start.36 = (bf16[2,128,768]{2,1,0:T(8,128)(2,1)S(1)}, bf16[2,128,768]{2,1,0:T(8,128)(2,1)S(1)}, u32[]{:S(2)}, u32[]{:S(2)}) collective-permute-start(bf16[2,128,768]{2,1,0:T(8,128)(2,1)S(1)} %pad_maximum_fusion.31), channel_id=1, source_target_pairs={{0,8},{4,12},{8,0},{12,4},{16,24},{20,28},{24,16},{28,20},{1,9},{5... | collective-permute-start | bytes 1179656 | tf_op jit(solution)/shard_map/ppermute | solution.py:739
  440.8 14.6 %collective-permute-start.35 = (bf16[2,128,768]{2,1,0:T(8,128)(2,1)S(1)}, bf16[2,128,768]{2,1,0:T(8,128)(2,1)S(1)}, u32[]{:S(2)}, u32[]{:S(2)}) collective-permute-start(bf16[2,128,768]{2,1,0:T(8,128)(2,1)S(1)} %pad_maximum_fusion.30), channel_id=1, source_target_pairs={{0,16},{4,20},{8,24},{12,28},{16,0},{20,4},{24,8},{28,12},{1,17},{... | collective-permute-start | bytes 1179656 | tf_op jit(solution)/shard_map/ppermute | solution.py:739
  460.0 59.9 %reduce-scatter.15.cloned.1.call-start = ((), (), s32[]{:S(2)}) async-start(), calls=%async_computation.14 | async-start | bytes 1474560 | tf_op jit(solution)/shard_map/reduce_scatter | solution.py:824
  463.1 8.9 %collective-permute-start.38 = (bf16[4,128,768]{2,1,0:T(8,128)(2,1)S(1)}, bf16[4,128,768]{2,1,0:T(8,128)(2,1)}, u32[]{:S(2)}, u32[]{:S(2)}) collective-permute-start(bf16[4,128,768]{2,1,0:T(8,128)(2,1)S(1)} %pad_maximum_fusion.19), channel_id=1, source_target_pairs={{0,4},{4,0},{8,12},{12,8},{16,20},{20,16},{24,28},{28,24},{1,5},{5... | collective-permute-start | bytes 2359304 | tf_op jit(solution)/shard_map/ppermute | solution.py:739
  471.9 115.9 %reduce-scatter.17.cloned.1.call-start = ((), (), s32[]{:S(2)}) async-start(), calls=%async_computation.15 | async-start | bytes 1966080 | tf_op jit(solution)/shard_map/reduce_scatter | solution.py:824
  477.4 32.9 %collective-permute-start.39 = (bf16[192,2560]{1,0:T(8,128)(2,1)S(1)}, bf16[192,2560]{1,0:T(8,128)(2,1)S(1)}, u32[]{:S(2)}, u32[]{:S(2)}) collective-permute-start(bf16[192,2560]{1,0:T(8,128)(2,1)S(1)} %pad_maximum_fusion.8), channel_id=1, source_target_pairs={{0,8},{4,12},{8,0},{12,4},{16,24},{20,28},{24,16},{28,20},{1,9},{5... | collective-permute-start | bytes 2949128 | tf_op jit(solution)/shard_map/ppermute | solution.py:739
  524.5 8.9 %collective-permute-start.45 = (bf16[192,768]{1,0:T(8,128)(2,1)S(1)}, bf16[192,768]{1,0:T(8,128)(2,1)S(1)}, u32[]{:S(2)}, u32[]{:S(2)}) collective-permute-start(bf16[192,768]{1,0:T(8,128)(2,1)S(1)} %pad_maximum_fusion.32), channel_id=1, source_target_pairs={{0,16},{4,20},{8,24},{12,28},{16,0},{20,4},{24,8},{28,12},{1,17},{... | collective-permute-start | bytes 884744 | tf_op jit(solution)/shard_map/ppermute | solution.py:739
  527.3 23.2 %collective-permute-start.42 = (bf16[768,1024]{1,0:T(8,128)(2,1)}, bf16[768,1024]{1,0:T(8,128)(2,1)}, u32[]{:S(2)}, u32[]{:S(2)}) collective-permute-start(bf16[768,1024]{1,0:T(8,128)(2,1)} %fusion.13), channel_id=1, source_target_pairs={{0,4},{4,0},{8,12},{12,8},{16,20},{20,16},{24,28},{28,24},{1,5},{5... | collective-permute-start | bytes 4718600 | tf_op jit(solution)/shard_map/ppermute | solution.py:739
  533.5 10.0 %collective-permute-start.46 = (bf16[192,768]{1,0:T(8,128)(2,1)S(1)}, bf16[192,768]{1,0:T(8,128)(2,1)S(1)}, u32[]{:S(2)}, u32[]{:S(2)}) collective-permute-start(bf16[192,768]{1,0:T(8,128)(2,1)S(1)} %add_convert_fusion.7), channel_id=1, source_target_pairs={{0,8},{4,12},{8,0},{12,4},{16,24},{20,28},{24,16},{28,20},{1,9},{5... | collective-permute-start | bytes 884744 | tf_op jit(solution)/shard_map/ppermute | solution.py:739
  540.6 24.0 %collective-permute-start.41 = (bf16[192,2560]{1,0:T(8,128)(2,1)S(1)}, bf16[192,2560]{1,0:T(8,128)(2,1)}, u32[]{:S(2)}, u32[]{:S(2)}) collective-permute-start(bf16[192,2560]{1,0:T(8,128)(2,1)S(1)} %add_convert_fusion.5), channel_id=1, source_target_pairs={{0,16},{4,20},{8,24},{12,28},{16,0},{20,4},{24,8},{28,12},{1,17},{... | collective-permute-start | bytes 2949128 | tf_op jit(solution)/shard_map/ppermute | solution.py:739
  544.5 24.9 %collective-permute-start.47 = (bf16[192,1536]{1,0:T(8,128)(2,1)}, bf16[192,1536]{1,0:T(8,128)(2,1)S(1)}, u32[]{:S(2)}, u32[]{:S(2)}) collective-permute-start(bf16[192,1536]{1,0:T(8,128)(2,1)} %pad_maximum_fusion.22), channel_id=1, source_target_pairs={{0,4},{4,0},{8,12},{12,8},{16,20},{20,16},{24,28},{28,24},{1,5},{5... | collective-permute-start | bytes 1769480 | tf_op jit(solution)/shard_map/ppermute | solution.py:739
  566.1 20.2 %collective-permute-start.53 = (bf16[192,2560]{1,0:T(8,128)(2,1)S(1)}, bf16[192,2560]{1,0:T(8,128)(2,1)S(1)}, u32[]{:S(2)}, u32[]{:S(2)}) collective-permute-start(bf16[192,2560]{1,0:T(8,128)(2,1)S(1)} %add_convert_fusion.4), channel_id=1, source_target_pairs={{0,4},{4,0},{8,12},{12,8},{16,20},{20,16},{24,28},{28,24},{1,5},{5... | collective-permute-start | bytes 2949128 | tf_op jit(solution)/shard_map/ppermute | solution.py:739
  589.4 8.8 %collective-permute-start.48 = (bf16[96,1024]{1,0:T(8,128)(2,1)S(1)}, bf16[96,1024]{1,0:T(8,128)(2,1)S(1)}, u32[]{:S(2)}, u32[]{:S(2)}) collective-permute-start(bf16[96,1024]{1,0:T(8,128)(2,1)S(1)} %get-tuple-element.391), channel_id=1, source_target_pairs={{0,8},{4,12},{8,0},{12,4},{16,24},{20,28},{24,16},{28,20},{1,9},{5... | collective-permute-start | bytes 589832 | tf_op jit(solution)/shard_map/ppermute | solution.py:739
  602.7 8.1 %collective-permute-start.58 = (f32[1,2,2834]{2,1,0:T(2,128)S(1)}, f32[1,2,2834]{2,1,0:T(2,128)S(1)}, u32[]{:S(2)}, u32[]{:S(2)}) collective-permute-start(f32[1,2,2834]{2,1,0:T(2,128)S(1)} %add.421), channel_id=1, source_target_pairs={{0,16},{4,20},{8,24},{12,28},{16,0},{20,4},{24,8},{28,12},{1,17},{... | collective-permute-start | bytes 68024 | tf_op jit(solution)/shard_map/ppermute | solution.py:739
  (93 other events, 724.9 us)
Sparse Core Ops, SparseCore 0:
  10.4 39.8 all-gather.8
  51.8 28.6 all-gather.10
  82.1 29.5 all-gather.16
  119.8 34.0 all-gather.12
  157.0 48.7 all-gather.14
  317.7 27.7 reduce-scatter.6
  347.8 27.8 reduce-scatter.8
  396.8 33.3 reduce-scatter.10
  460.2 28.1 reduce-scatter.12
  490.5 27.9 reduce-scatter.14
  556.1 31.6 reduce-scatter.16
